TPU v7x, 32 devices: a whole 2x2x4 slice. The times are simulated.
32 devices in a mesh: head: 4 (over x, core), blk: 8 (over z, y).
Axes of the slice: x: 2, y: 2, z: 4, core: 2. Of those that a mesh axis runs over, the one named last changes fastest.
Arguments:
- layer_input: bfloat16 [2, 4096, 512], P(None, ('head', 'blk')), may hold values from -9 to 9
- segments: int32 [2, 4096], P(None, ('head', 'blk')), may hold values from 0 to 7, never falling along the last dimension, each value on 1 to 1024 neighbouring positions
- input_weight: bfloat16 [512, 1536], P(('head', 'blk')), may hold values from -0.25 to 0.25
- output_weight: bfloat16 [512, 512], P(('head', 'blk')), may hold values from -1 to 1
- up_weight: bfloat16 [512, 2048], P(('head', 'blk')), may hold values from -0.25 to 0.25
- down_weight: bfloat16 [2048, 512], P(('head', 'blk')), may hold values from -0.375 to 0.375
- query_bias: bfloat16 [512], P(('head', 'blk')), may hold values from -3 to 3
- value_bias: bfloat16 [512], P(('head', 'blk')), may hold values from -3 to 3
- output_bias: bfloat16 [512], P(('head', 'blk')), may hold values from -3 to 3
- up_bias: bfloat16 [2048], P(('head', 'blk')), may hold values from -3 to 3
- down_bias: bfloat16 [512], P(('head', 'blk')), may hold values from -3 to 3
- alphas: float32 [2], replicated, may hold values from 0.2 to 0.45
- out_grad: bfloat16 [2, 4096, 512], P(None, ('head', 'blk')), may hold values from -6 to 6
Outputs:
- layer_output: bfloat16 [2, 4096, 512], P(None, ('head', 'blk'))
- input_grad: bfloat16 [2, 4096, 512], P(None, ('head', 'blk'))
- input_weight_grad: float32 [512, 1536], P(('head', 'blk'))
- output_weight_grad: float32 [512, 512], P(('head', 'blk'))
- up_weight_grad: float32 [512, 2048], P(('head', 'blk'))
- down_weight_grad: float32 [2048, 512], P(('head', 'blk'))
- query_bias_grad: float32 [512], P(('head', 'blk'))
- value_bias_grad: float32 [512], P(('head', 'blk'))
- output_bias_grad: float32 [512], P(('head', 'blk'))
- up_bias_grad: float32 [2048], P(('head', 'blk'))
- down_bias_grad: float32 [512], P(('head', 'blk'))
- alphas_grad: float32 [2], replicated
- rms_values: float32 [3], replicated
Inputs may be any that keep to these rules, and one draw needn't show every extreme that they name: `segments`: A sequence's segment numbers never fall; each document holds 1 to 1024 tokens and some document holds exactly 1024.
All inputs are finite; a program needn't handle non-finite values.
Results may differ from a plain program's by a relative error of at most 0.017.
The roundings to bfloat16 on the way count: a program that leaves them out, or rounds other values in their place, can miss the bound.
Values may be sent and summed in bfloat16 or wider, within the bound.
A program may use at most 64 MiB of HBM per device.

v0:
```python
import math

import jax
import jax.numpy as jnp
from jax import lax
from jax.sharding import PartitionSpec as P

HEADS = 8
HD = 64


def from_behind(block, axis, distance):
    devices = range(lax.axis_size(axis))
    route = [((i - distance) % len(devices), i) for i in devices]
    return lax.ppermute(block, axis, route)


def outer_product(left, right):
    return lax.dot_general(
        left, right, (((0,), (0,)), ((), ())), preferred_element_type=jnp.float32
    )


def back_product(left, right):
    return lax.dot_general(
        left, right, (((1,), (1,)), ((), ())), preferred_element_type=jnp.float32
    )


def normal_cdf(values):
    return 0.5 * (1.0 + lax.erf(values * (1.0 / math.sqrt(2.0))))


def gelu_value(values):
    return values * normal_cdf(values)


def gelu_slope(values):
    return normal_cdf(values) + values * jnp.exp(-0.5 * values * values) * (
        1.0 / math.sqrt(2.0 * math.pi)
    )


def local(
    layer_input,
    segments,
    input_weight,
    output_weight,
    up_weight,
    down_weight,
    query_bias,
    value_bias,
    output_bias,
    up_bias,
    down_bias,
    alphas,
    out_grad,
):
    head_count = lax.axis_size("head")
    block_count = lax.axis_size("blk")
    block_index = lax.axis_index("blk")
    seq_count, seq_rows, model_width = layer_input.shape
    local_heads = HEADS // head_count
    group_rows = head_count * seq_rows
    group_width = model_width // head_count
    forward_turns = block_count - 1
    gathered_weights = (
        lax.all_gather(input_weight, ("head", "blk"), axis=0, tiled=True),
        lax.all_gather(output_weight, ("head", "blk"), axis=0, tiled=True),
        lax.all_gather(up_weight, ("head", "blk"), axis=0, tiled=True),
        lax.all_gather(down_weight, ("head", "blk"), axis=0, tiled=True),
        lax.all_gather(query_bias, ("head", "blk"), axis=0, tiled=True),
        lax.all_gather(value_bias, ("head", "blk"), axis=0, tiled=True),
        lax.all_gather(output_bias, ("head", "blk"), axis=0, tiled=True),
        lax.all_gather(up_bias, ("head", "blk"), axis=0, tiled=True),
        lax.all_gather(down_bias, ("head", "blk"), axis=0, tiled=True),
    )
    (
        full_input,
        full_output,
        full_up,
        full_down,
        bias_query,
        bias_value,
        bias_output,
        bias_up,
        bias_down,
    ) = gathered_weights
    all_numbers = lax.all_gather(segments, ("head", "blk"), axis=1, tiled=True)
    number_grid = all_numbers.reshape(seq_count, head_count, block_count, seq_rows)

    def block_numbers(source):
        picked = lax.dynamic_index_in_dim(number_grid, source, 2, keepdims=False)
        return picked.reshape(seq_count, group_rows)

    def block_places(source):
        head_part = jnp.arange(head_count, dtype=jnp.int32)[:, None] * block_count + source
        return (head_part * seq_rows + jnp.arange(seq_rows, dtype=jnp.int32)[None, :]).reshape(
            group_rows
        )

    query_numbers = block_numbers(block_index)
    query_places = block_places(block_index)
    flat_tokens = layer_input.reshape(-1, model_width)
    joint_bias = jnp.concatenate(
        [
            bias_query.astype(jnp.float32),
            jnp.zeros((model_width,), jnp.float32),
            bias_value.astype(jnp.float32),
        ]
    )
    projected = (
        jnp.dot(flat_tokens, full_input, preferred_element_type=jnp.float32) + joint_bias
    ).astype(jnp.bfloat16)
    projected = projected.reshape(seq_count, seq_rows, 3, model_width)
    grouped = lax.all_to_all(projected, "head", split_axis=3, concat_axis=1, tiled=True)
    queries = grouped[:, :, 0].reshape(seq_count, group_rows, local_heads, HD)
    own_pairs = grouped[:, :, 1:]

    def masked_scores(key_values, source):
        keys_here = key_values[:, :, 0].reshape(seq_count, group_rows, local_heads, HD)
        raw_scores = (
            jnp.einsum("sqhd,skhd->shqk", queries, keys_here, preferred_element_type=jnp.float32)
            * 0.125
        )
        visible = (query_numbers[:, :, None] == block_numbers(source)[:, None, :]) & (
            block_places(source)[None, None, :] <= query_places[None, :, None]
        )
        return jnp.where(visible[:, None], raw_scores, -1e30)

    def forward_turn(softmax_state, key_values, source):
        running, row_total, exact_weighted = softmax_state
        scores = masked_scores(key_values, source)
        newest = jnp.maximum(running, jnp.max(scores, -1))
        weights = jnp.exp(scores - newest[..., None])
        factor = jnp.exp(running - newest)
        values_here = key_values[:, :, 1].reshape(seq_count, group_rows, local_heads, HD)
        exact_weighted = exact_weighted * factor[..., None] + jnp.einsum(
            "shqk,skhd->shqd",
            weights,
            values_here.astype(jnp.float32),
            preferred_element_type=jnp.float32,
        )
        row_total = row_total * factor + jnp.sum(weights, -1)
        return (newest, row_total, exact_weighted)

    start_state = (
        jnp.full((seq_count, local_heads, group_rows), -1e30, jnp.float32),
        jnp.zeros((seq_count, local_heads, group_rows), jnp.float32),
        jnp.zeros((seq_count, local_heads, group_rows, HD), jnp.float32),
    )
    softmax_state = forward_turn(start_state, own_pairs, block_index)
    kept_blocks = jnp.zeros((), jnp.bfloat16)

    def forward_hop(hop_index, loop_state):
        key_values, softmax_state, kept_blocks = loop_state
        key_values = from_behind(key_values, "blk", 1)
        source = (block_index - hop_index) % block_count
        softmax_state = forward_turn(softmax_state, key_values, source)
        return (key_values, softmax_state, kept_blocks)

    last_pairs, softmax_state, kept_blocks = lax.fori_loop(
        1, forward_turns + 1, forward_hop, (own_pairs, softmax_state, kept_blocks)
    )
    running, row_total, exact_weighted = softmax_state
    log_total = running + jnp.log(row_total)
    exact_attended = exact_weighted / row_total[..., None]
    out_rows = exact_attended.transpose(0, 2, 1, 3).reshape(seq_count, group_rows, group_width)
    mixed_rows = lax.all_to_all(
        out_rows.astype(jnp.bfloat16), "head", split_axis=1, concat_axis=2, tiled=True
    ).reshape(-1, model_width)
    branch_attn = jnp.dot(
        mixed_rows, full_output, preferred_element_type=jnp.float32
    ) + bias_output.astype(jnp.float32)
    residual = flat_tokens.astype(jnp.float32) + alphas[0] * branch_attn
    hidden_in = residual.astype(jnp.bfloat16)
    pre_act = jnp.dot(hidden_in, full_up, preferred_element_type=jnp.float32) + bias_up.astype(
        jnp.float32
    )
    activation = gelu_value(pre_act).astype(jnp.bfloat16)
    branch_ffn = jnp.dot(
        activation, full_down, preferred_element_type=jnp.float32
    ) + bias_down.astype(jnp.float32)
    stream = residual + alphas[1] * branch_ffn
    attn_term = alphas[0] * branch_attn
    ffn_term = alphas[1] * branch_ffn
    squares = jnp.stack(
        [jnp.sum(stream * stream), jnp.sum(attn_term * attn_term), jnp.sum(ffn_term * ffn_term)]
    )
    squares = lax.psum(squares, ("head", "blk"))
    out_grads = out_grad.reshape(-1, model_width).astype(jnp.float32)
    grad_ffn = (alphas[1] * out_grads).astype(jnp.bfloat16)
    down_grad = outer_product(activation, grad_ffn)
    down_bias_term = jnp.sum(grad_ffn.astype(jnp.float32), 0)
    grad_act = back_product(grad_ffn, full_down)
    grad_pre = (grad_act * gelu_slope(pre_act)).astype(jnp.bfloat16)
    up_grad = outer_product(hidden_in, grad_pre)
    up_bias_term = jnp.sum(grad_pre.astype(jnp.float32), 0)
    grad_residual = out_grads + back_product(grad_pre, full_up)
    alpha_terms = jnp.stack([jnp.sum(grad_residual * branch_attn), jnp.sum(out_grads * branch_ffn)])
    grad_branch = (alphas[0] * grad_residual).astype(jnp.bfloat16)
    output_grad = outer_product(mixed_rows, grad_branch)
    output_bias_term = jnp.sum(grad_branch.astype(jnp.float32), 0)
    grad_mixed = (
        back_product(grad_branch, full_output)
        .astype(jnp.bfloat16)
        .reshape(seq_count, seq_rows, model_width)
    )
    grad_rows = lax.all_to_all(grad_mixed, "head", split_axis=2, concat_axis=1, tiled=True)
    grad_attended = grad_rows.reshape(seq_count, group_rows, local_heads, HD)
    grad_attended_wide = grad_attended.astype(jnp.float32)
    row_delta = jnp.sum(grad_attended_wide.transpose(0, 2, 1, 3) * exact_attended, -1)

    def backward_turn(key_values, pair_grads, query_grad, source):
        scores = masked_scores(key_values, source)
        probs = jnp.exp(scores - log_total[..., None])
        keys_here = key_values[:, :, 0].reshape(seq_count, group_rows, local_heads, HD)
        values_here = key_values[:, :, 1].reshape(seq_count, group_rows, local_heads, HD)
        value_grad = jnp.einsum(
            "shqk,sqhd->skhd", probs, grad_attended_wide, preferred_element_type=jnp.float32
        )
        prob_grad = jnp.einsum(
            "sqhd,skhd->shqk", grad_attended, values_here, preferred_element_type=jnp.float32
        )
        score_grad = (probs * (prob_grad - row_delta[..., None])).astype(jnp.bfloat16)
        query_grad = (
            query_grad
            + jnp.einsum(
                "shqk,skhd->sqhd", score_grad, keys_here, preferred_element_type=jnp.float32
            )
            * 0.125
        )
        key_grad = (
            jnp.einsum("shqk,sqhd->skhd", score_grad, queries, preferred_element_type=jnp.float32)
            * 0.125
        )
        pair_grads = pair_grads + jnp.stack(
            [
                key_grad.reshape(seq_count, group_rows, group_width),
                value_grad.reshape(seq_count, group_rows, group_width),
            ],
            2,
        )
        return (pair_grads, query_grad)

    def backward_hop(hop_index, loop_state):
        key_values, pair_grads, query_grad = loop_state
        source = (block_index - hop_index) % block_count
        current_pairs = key_values
        pair_grads, query_grad = backward_turn(current_pairs, pair_grads, query_grad, source)
        pair_grads = from_behind(pair_grads.astype(jnp.bfloat16), "blk", 1).astype(pair_grads.dtype)
        key_values = from_behind(key_values, "blk", 1)
        return (key_values, pair_grads, query_grad)

    start_grads = (
        own_pairs,
        jnp.zeros((seq_count, group_rows, 2, group_width), jnp.float32),
        jnp.zeros((seq_count, group_rows, local_heads, HD), jnp.float32),
    )
    last_pairs, pair_grads, query_grad = lax.fori_loop(0, block_count, backward_hop, start_grads)
    grad_grouped = jnp.concatenate(
        [query_grad.reshape(seq_count, group_rows, 1, group_width), pair_grads], 2
    ).astype(jnp.bfloat16)
    grad_projected = lax.all_to_all(
        grad_grouped, "head", split_axis=1, concat_axis=3, tiled=True
    ).reshape(-1, 3 * model_width)
    input_grad_term = outer_product(flat_tokens, grad_projected)
    projected_sums = jnp.sum(grad_projected.astype(jnp.float32), 0)
    query_bias_term = projected_sums[:model_width]
    value_bias_term = projected_sums[2 * model_width :]
    input_grad = (
        (grad_residual + back_product(grad_projected, full_input))
        .astype(jnp.bfloat16)
        .reshape(layer_input.shape)
    )
    weight_shards = (
        lax.psum_scatter(input_grad_term, ("head", "blk"), scatter_dimension=0, tiled=True),
        lax.psum_scatter(output_grad, ("head", "blk"), scatter_dimension=0, tiled=True),
        lax.psum_scatter(up_grad, ("head", "blk"), scatter_dimension=0, tiled=True),
        lax.psum_scatter(down_grad, ("head", "blk"), scatter_dimension=0, tiled=True),
        lax.psum_scatter(query_bias_term, ("head", "blk"), scatter_dimension=0, tiled=True),
        lax.psum_scatter(value_bias_term, ("head", "blk"), scatter_dimension=0, tiled=True),
        lax.psum_scatter(output_bias_term, ("head", "blk"), scatter_dimension=0, tiled=True),
        lax.psum_scatter(up_bias_term, ("head", "blk"), scatter_dimension=0, tiled=True),
        lax.psum_scatter(down_bias_term, ("head", "blk"), scatter_dimension=0, tiled=True),
    )
    alphas_grad = lax.psum(alpha_terms, ("head", "blk"))
    rms_values = jnp.sqrt(squares / (seq_count * group_rows * block_count * model_width))
    layer_output = stream.astype(jnp.bfloat16).reshape(layer_input.shape)
    return (
        layer_output,
        input_grad,
        weight_shards[0],
        weight_shards[1],
        weight_shards[2],
        weight_shards[3],
        weight_shards[4],
        weight_shards[5],
        weight_shards[6],
        weight_shards[7],
        weight_shards[8],
        alphas_grad,
        rms_values,
    )


def solution(mesh):
    return jax.shard_map(
        local,
        mesh=mesh,
        in_specs=(
            P(None, ("head", "blk"), None),
            P(None, ("head", "blk")),
            P(("head", "blk"), None),
            P(("head", "blk"), None),
            P(("head", "blk"), None),
            P(("head", "blk"), None),
            P(("head", "blk")),
            P(("head", "blk")),
            P(("head", "blk")),
            P(("head", "blk")),
            P(("head", "blk")),
            P(),
            P(None, ("head", "blk"), None),
        ),
        out_specs=(
            P(None, ("head", "blk"), None),
            P(None, ("head", "blk"), None),
            P(("head", "blk"), None),
            P(("head", "blk"), None),
            P(("head", "blk"), None),
            P(("head", "blk"), None),
            P(("head", "blk")),
            P(("head", "blk")),
            P(("head", "blk")),
            P(("head", "blk")),
            P(("head", "blk")),
            P(),
            P(),
        ),
        check_vma=False,
    )
```

profile of v0, /device:TPU:0, one launch (start us, length us, event | category | flops | bytes accessed | tf_op | source)
XLA Modules:
  0.0 1093.9 jit_solution(6580635390784442079)
XLA Ops:
  15.0 42.1 %all-reduce.11 = (bf16[512]{0:T(512)(128)(2,1)S(1)}, bf16[512]{0:T(512)(128)(2,1)S(1)}, bf16[512]{0:T(512)(128)(2,1)S(1)}, bf16[2048]{0:T(1024)(128)(2,1)S(1)}, bf16[512]{0:T(512)(128)(2,1)S(1)}) all-reduce(bf16[512]{0:T(512)(128)(2,1)S(1)} %dynamic-update-slice.2, ...), channel_id=1, replica_groups=mesh['head'=4,'blk'=8] {'head','blk'}, use_global_device_ids=true, to_apply=%add.2 | all-reduce | flops 4096 | bytes 16384
  57.1 66.3 %all_gather.33 = s32[2,4096]{1,0:T(2,128)S(1)} all-gather(s32[2,128]{1,0:T(2,128)} %param.18), channel_id=1, replica_groups=mesh['head'=4,'blk'=8] {'head','blk'}, dimensions={1}, use_global_device_ids=true | all-gather | bytes 33792 | tf_op jit(solution)/shard_map/all_gather | solution.py:89
  130.4 3.5 all-to-all-start
  134.4 67.5 %all_gather.34 = bf16[512,512]{1,0:T(8,128)(2,1)S(1)} all-gather(bf16[16,512]{1,0:T(8,128)(2,1)S(1)} %copy-done.23), channel_id=1, replica_groups=mesh['head'=4,'blk'=8] {'head','blk'}, dimensions={0}, use_global_device_ids=true | all-gather | bytes 540672 | tf_op jit(solution)/shard_map/all_gather | solution.py:69
  214.9 124.8 %while.42 = (s32[]{:T(128)}, bf16[2,512,2,128]{1,3,0,2:T(8,128)(2,1)}, f32[2,2,512]{2,1,0:T(2,128)S(1)}, f32[2,2,512]{2,1,0:T(2,128)S(1)}, f32[2,2,512,64]{2,3,1...) while((s32[]{:T(128)}, ...), condition=%wide.region_5.6_spmd.clone, body=%wide.region_2.5_spmd.clone.sunk | while | flops 280499232 | bytes 21406080 | solution.py:162
  217.7 11.1 %collective-permute-done = bf16[2,512,2,128]{1,3,0,2:T(8,128)(2,1)S(1)} collective-permute-done((bf16[2,512,2,128]{1,3,0,2:T(8,128)(2,1)}, bf16[2,512,2,128]{1,3,0,2:T(8,128)(2,1)S(1)}, u32[]{:S(2)}, u32[]{:S(2)}) %collective-permute-start) | collective-permute-done | bytes 524320 | tf_op jit(solution)/shard_map/while/body/eval_jaxpr/ppermute | solution.py:15
  233.8 12.0 %collective-permute-done = bf16[2,512,2,128]{1,3,0,2:T(8,128)(2,1)S(1)} collective-permute-done((bf16[2,512,2,128]{1,3,0,2:T(8,128)(2,1)}, bf16[2,512,2,128]{1,3,0,2:T(8,128)(2,1)S(1)}, u32[]{:S(2)}, u32[]{:S(2)}) %collective-permute-start) | collective-permute-done | bytes 524320 | tf_op jit(solution)/shard_map/while/body/eval_jaxpr/ppermute | solution.py:15
  250.9 11.3 %collective-permute-done = bf16[2,512,2,128]{1,3,0,2:T(8,128)(2,1)S(1)} collective-permute-done((bf16[2,512,2,128]{1,3,0,2:T(8,128)(2,1)}, bf16[2,512,2,128]{1,3,0,2:T(8,128)(2,1)S(1)}, u32[]{:S(2)}, u32[]{:S(2)}) %collective-permute-start) | collective-permute-done | bytes 524320 | tf_op jit(solution)/shard_map/while/body/eval_jaxpr/ppermute | solution.py:15
  267.1 11.3 %collective-permute-done = bf16[2,512,2,128]{1,3,0,2:T(8,128)(2,1)S(1)} collective-permute-done((bf16[2,512,2,128]{1,3,0,2:T(8,128)(2,1)}, bf16[2,512,2,128]{1,3,0,2:T(8,128)(2,1)S(1)}, u32[]{:S(2)}, u32[]{:S(2)}) %collective-permute-start) | collective-permute-done | bytes 524320 | tf_op jit(solution)/shard_map/while/body/eval_jaxpr/ppermute | solution.py:15
  283.4 14.9 %collective-permute-done = bf16[2,512,2,128]{1,3,0,2:T(8,128)(2,1)S(1)} collective-permute-done((bf16[2,512,2,128]{1,3,0,2:T(8,128)(2,1)}, bf16[2,512,2,128]{1,3,0,2:T(8,128)(2,1)S(1)}, u32[]{:S(2)}, u32[]{:S(2)}) %collective-permute-start) | collective-permute-done | bytes 524320 | tf_op jit(solution)/shard_map/while/body/eval_jaxpr/ppermute | solution.py:15
  303.4 14.0 %collective-permute-done = bf16[2,512,2,128]{1,3,0,2:T(8,128)(2,1)S(1)} collective-permute-done((bf16[2,512,2,128]{1,3,0,2:T(8,128)(2,1)}, bf16[2,512,2,128]{1,3,0,2:T(8,128)(2,1)S(1)}, u32[]{:S(2)}, u32[]{:S(2)}) %collective-permute-start) | collective-permute-done | bytes 524320 | tf_op jit(solution)/shard_map/while/body/eval_jaxpr/ppermute | solution.py:15
  322.4 13.1 %collective-permute-done = bf16[2,512,2,128]{1,3,0,2:T(8,128)(2,1)S(1)} collective-permute-done((bf16[2,512,2,128]{1,3,0,2:T(8,128)(2,1)}, bf16[2,512,2,128]{1,3,0,2:T(8,128)(2,1)S(1)}, u32[]{:S(2)}, u32[]{:S(2)}) %collective-permute-start) | collective-permute-done | bytes 524320 | tf_op jit(solution)/shard_map/while/body/eval_jaxpr/ppermute | solution.py:15
  340.6 3.6 all-to-all-start.1
  344.3 5.8 all-to-all-done.1
  352.1 3.9 multiply_convert_fusion.1
  356.0 4.1 convert_reduce_fusion
  360.9 3.6 multiply_reduce_fusion.2
  365.7 3.4 all-to-all-start.2
  370.5 4.6 all-to-all-done.2
  377.2 294.1 %while.43 = (s32[]{:T(128)}, bf16[2,512,2,128]{1,3,0,2:T(8,128)(2,1)}, f32[2,512,2,128]{1,3,0,2:T(8,128)}, f32[2,512,2,64]{1,3,2,0:T(8,128)}, s32[2,4,128]{2,1,0...) while((s32[]{:T(128)}, ...), condition=%wide.region_8.9_spmd.clone, body=%wide.region_7.8_spmd.clone.sunk | while | flops 683672576 | bytes 56427008 | solution.py:260
  381.9 3.8 fusion.136
  391.4 17.0 %collective-permute-done.2 = bf16[2,512,2,128]{1,3,0,2:T(8,128)(2,1)} collective-permute-done((bf16[2,512,2,128]{1,3,0,2:T(8,128)(2,1)}, bf16[2,512,2,128]{1,3,0,2:T(8,128)(2,1)}, u32[]{:S(2)}, u32[]{:S(2)}) %collective-permute-start.2) | collective-permute-done | bytes 524320 | tf_op jit(solution)/shard_map/while/body/eval_jaxpr/ppermute | solution.py:15
  410.7 7.9 collective-permute-done.1
  423.2 3.8 fusion.136
  433.8 15.4 %collective-permute-done.2 = bf16[2,512,2,128]{1,3,0,2:T(8,128)(2,1)} collective-permute-done((bf16[2,512,2,128]{1,3,0,2:T(8,128)(2,1)}, bf16[2,512,2,128]{1,3,0,2:T(8,128)(2,1)}, u32[]{:S(2)}, u32[]{:S(2)}) %collective-permute-start.2) | collective-permute-done | bytes 524320 | tf_op jit(solution)/shard_map/while/body/eval_jaxpr/ppermute | solution.py:15
  451.5 6.9 collective-permute-done.1
  463.0 3.8 fusion.136
  473.6 15.4 %collective-permute-done.2 = bf16[2,512,2,128]{1,3,0,2:T(8,128)(2,1)} collective-permute-done((bf16[2,512,2,128]{1,3,0,2:T(8,128)(2,1)}, bf16[2,512,2,128]{1,3,0,2:T(8,128)(2,1)}, u32[]{:S(2)}, u32[]{:S(2)}) %collective-permute-start.2) | collective-permute-done | bytes 524320 | tf_op jit(solution)/shard_map/while/body/eval_jaxpr/ppermute | solution.py:15
  491.3 6.1 collective-permute-done.1
  502.1 3.8 fusion.136
  512.7 15.4 %collective-permute-done.2 = bf16[2,512,2,128]{1,3,0,2:T(8,128)(2,1)} collective-permute-done((bf16[2,512,2,128]{1,3,0,2:T(8,128)(2,1)}, bf16[2,512,2,128]{1,3,0,2:T(8,128)(2,1)}, u32[]{:S(2)}, u32[]{:S(2)}) %collective-permute-start.2) | collective-permute-done | bytes 524320 | tf_op jit(solution)/shard_map/while/body/eval_jaxpr/ppermute | solution.py:15
  530.3 5.3 collective-permute-done.1
  540.2 3.8 fusion.136
  550.8 14.9 %collective-permute-done.2 = bf16[2,512,2,128]{1,3,0,2:T(8,128)(2,1)} collective-permute-done((bf16[2,512,2,128]{1,3,0,2:T(8,128)(2,1)}, bf16[2,512,2,128]{1,3,0,2:T(8,128)(2,1)}, u32[]{:S(2)}, u32[]{:S(2)}) %collective-permute-start.2) | collective-permute-done | bytes 524320 | tf_op jit(solution)/shard_map/while/body/eval_jaxpr/ppermute | solution.py:15
  568.0 4.0 collective-permute-done.1
  576.6 3.8 fusion.136
  587.2 13.5 %collective-permute-done.2 = bf16[2,512,2,128]{1,3,0,2:T(8,128)(2,1)} collective-permute-done((bf16[2,512,2,128]{1,3,0,2:T(8,128)(2,1)}, bf16[2,512,2,128]{1,3,0,2:T(8,128)(2,1)}, u32[]{:S(2)}, u32[]{:S(2)}) %collective-permute-start.2) | collective-permute-done | bytes 524320 | tf_op jit(solution)/shard_map/while/body/eval_jaxpr/ppermute | solution.py:15
  602.9 3.7 collective-permute-done.1
  611.2 3.8 fusion.136
  621.8 11.9 %collective-permute-done.2 = bf16[2,512,2,128]{1,3,0,2:T(8,128)(2,1)} collective-permute-done((bf16[2,512,2,128]{1,3,0,2:T(8,128)(2,1)}, bf16[2,512,2,128]{1,3,0,2:T(8,128)(2,1)}, u32[]{:S(2)}, u32[]{:S(2)}) %collective-permute-start.2) | collective-permute-done | bytes 524320 | tf_op jit(solution)/shard_map/while/body/eval_jaxpr/ppermute | solution.py:15
  644.0 3.8 fusion.136
  654.9 10.7 collective-permute-done.2
  675.2 15.3 %all_to_all.63 = bf16[2,512,3,128]{3,0,2,1:T(2,128)(2,1)S(1)} all-to-all(bf16[2,512,3,128]{3,0,2,1:T(2,128)(2,1)S(1)} %pad_maximum_fusion), channel_id=1, replica_groups=mesh['head'=4,'blk'=8] {'head'}, dimensions={1} | all-to-all | bytes 1572864 | tf_op jit(solution)/shard_map/all_to_all | solution.py:264
  697.4 4.0 fusion.58
  710.0 38.9 %all-reduce.10 = (f32[512]{0:T(512)S(1)}, f32[512]{0:T(512)S(1)}, f32[512]{0:T(512)S(1)}, f32[2048]{0:T(1024)S(1)}, f32[512]{0:T(512)S(1)}, /*index=5*/f32[2]{0:T(128)}, f32[3]{0:T(128)S(1)}) all-reduce(f32[512]{0:T(512)S(1)} %get-tuple-element.920, ...), channel_id=6, replica_groups=mesh['head'=4,'blk'=8] {'head','blk'}, use_global_device_ids=true, to_apply=%region_14.15.clone | all-reduce | flops 4101 | bytes 32808
  754.7 42.0 %reduce-scatter.13.cloned.1.call-done = f32[16,1536]{1,0:T(8,128)} async-done(((f32[512,1536]{1,0:T(8,128)}), f32[16,1536]{1,0:T(8,128)}) %reduce-scatter.13.cloned.1.call-update) | async-done | bytes 98320
  796.7 145.6 %reduce-scatter.9.cloned.1.call-done = f32[16,2048]{1,0:T(8,128)} async-done(((f32[512,2048]{1,0:T(8,128)}), f32[16,2048]{1,0:T(8,128)}) %reduce-scatter.9.cloned.1.call-update) | async-done | bytes 131088 | tf_op jit(solution)/shard_map/reduce_scatter | solution.py:279
  942.3 144.7 %reduce-scatter.11.cloned.1.call-done = f32[64,512]{1,0:T(8,128)} async-done(((f32[2048,512]{1,0:T(8,128)}), f32[64,512]{1,0:T(8,128)}) %reduce-scatter.11.cloned.1.call-update) | async-done | bytes 131088 | tf_op jit(solution)/shard_map/reduce_scatter | solution.py:280
  (427 shorter events, 213.2 us)
Async XLA Ops:
  7.2 118.3 %all-gather.4.cloned.1.call-start = ((), (), s32[]{:S(2)}) async-start(), calls=%async_computation.8 | async-start | bytes 1622016 | tf_op jit(solution)/shard_map/all_gather | solution.py:68
  7.9 344.2 %all-gather.6.cloned.1.call-start = ((), (), s32[]{:S(2)}) async-start(), calls=%async_computation.9 | async-start | bytes 2162688 | tf_op jit(solution)/shard_map/all_gather | solution.py:70
  8.7 347.3 %all-gather.8.cloned.1.call-start = ((), (), s32[]{:S(2)}) async-start(), calls=%async_computation.10 | async-start | bytes 2162688 | tf_op jit(solution)/shard_map/all_gather | solution.py:71
  125.4 230.6 %copy-start.16 = (bf16[256,512]{1,0:T(8,128)(2,1)}, bf16[256,512]{1,0:T(8,128)(2,1)S(1)}, u32[]{:S(2)}) copy-start(bf16[256,512]{1,0:T(8,128)(2,1)S(1)} %fusion.40) | copy-start | bytes 786436
  125.4 9.0 copy-start.23
  130.4 71.6 %all-to-all-start = ((bf16[2,128,3,512]{1,0,2,3:T(2,128)(2,1)}), bf16[2,128,3,512]{1,0,2,3:T(2,128)(2,1)S(1)}, u32[]{:S(2)}, u32[]{:S(2)}) async-start(bf16[2,128,3,512]{1,0,2,3:T(2,128)(2,1)} %copy.98), calls=%async_computation | async-start | bytes 1572864 | tf_op jit(solution)/shard_map/all_to_all | solution.py:116
  214.9 135.4 %copy-start.14 = (bf16[2,128,512]{2,1,0:T(8,128)(2,1)S(1)}, bf16[2,128,512]{2,1,0:T(8,128)(2,1)}, u32[]{:S(2)}) copy-start(bf16[2,128,512]{2,1,0:T(8,128)(2,1)} %param.17) | copy-start | bytes 786436
  215.0 13.8 %collective-permute-start = (bf16[2,512,2,128]{1,3,0,2:T(8,128)(2,1)}, bf16[2,512,2,128]{1,3,0,2:T(8,128)(2,1)S(1)}, u32[]{:S(2)}, u32[]{:S(2)}) collective-permute-start(bf16[2,512,2,128]{1,3,0,2:T(8,128)(2,1)} %get-tuple-element.1110), channel_id=1, source_target_pairs={{7,0},{0,1},{1,2},{2,3},{3,4},{4,5},{5,6},{6,7},{15,8},{8,9},{9,10... | collective-permute-start | bytes 1572872 | tf_op jit(solution)/shard_map/while/body/eval_jaxpr/ppermute | solution.py:15
  233.0 12.9 %collective-permute-start = (bf16[2,512,2,128]{1,3,0,2:T(8,128)(2,1)}, bf16[2,512,2,128]{1,3,0,2:T(8,128)(2,1)S(1)}, u32[]{:S(2)}, u32[]{:S(2)}) collective-permute-start(bf16[2,512,2,128]{1,3,0,2:T(8,128)(2,1)} %get-tuple-element.1110), channel_id=1, source_target_pairs={{7,0},{0,1},{1,2},{2,3},{3,4},{4,5},{5,6},{6,7},{15,8},{8,9},{9,10... | collective-permute-start | bytes 1572872 | tf_op jit(solution)/shard_map/while/body/eval_jaxpr/ppermute | solution.py:15
  250.0 12.1 %collective-permute-start = (bf16[2,512,2,128]{1,3,0,2:T(8,128)(2,1)}, bf16[2,512,2,128]{1,3,0,2:T(8,128)(2,1)S(1)}, u32[]{:S(2)}, u32[]{:S(2)}) collective-permute-start(bf16[2,512,2,128]{1,3,0,2:T(8,128)(2,1)} %get-tuple-element.1110), channel_id=1, source_target_pairs={{7,0},{0,1},{1,2},{2,3},{3,4},{4,5},{5,6},{6,7},{15,8},{8,9},{9,10... | collective-permute-start | bytes 1572872 | tf_op jit(solution)/shard_map/while/body/eval_jaxpr/ppermute | solution.py:15
  266.3 12.1 %collective-permute-start = (bf16[2,512,2,128]{1,3,0,2:T(8,128)(2,1)}, bf16[2,512,2,128]{1,3,0,2:T(8,128)(2,1)S(1)}, u32[]{:S(2)}, u32[]{:S(2)}) collective-permute-start(bf16[2,512,2,128]{1,3,0,2:T(8,128)(2,1)} %get-tuple-element.1110), channel_id=1, source_target_pairs={{7,0},{0,1},{1,2},{2,3},{3,4},{4,5},{5,6},{6,7},{15,8},{8,9},{9,10... | collective-permute-start | bytes 1572872 | tf_op jit(solution)/shard_map/while/body/eval_jaxpr/ppermute | solution.py:15
  282.6 15.8 %collective-permute-start = (bf16[2,512,2,128]{1,3,0,2:T(8,128)(2,1)}, bf16[2,512,2,128]{1,3,0,2:T(8,128)(2,1)S(1)}, u32[]{:S(2)}, u32[]{:S(2)}) collective-permute-start(bf16[2,512,2,128]{1,3,0,2:T(8,128)(2,1)} %get-tuple-element.1110), channel_id=1, source_target_pairs={{7,0},{0,1},{1,2},{2,3},{3,4},{4,5},{5,6},{6,7},{15,8},{8,9},{9,10... | collective-permute-start | bytes 1572872 | tf_op jit(solution)/shard_map/while/body/eval_jaxpr/ppermute | solution.py:15
  302.5 14.8 %collective-permute-start = (bf16[2,512,2,128]{1,3,0,2:T(8,128)(2,1)}, bf16[2,512,2,128]{1,3,0,2:T(8,128)(2,1)S(1)}, u32[]{:S(2)}, u32[]{:S(2)}) collective-permute-start(bf16[2,512,2,128]{1,3,0,2:T(8,128)(2,1)} %get-tuple-element.1110), channel_id=1, source_target_pairs={{7,0},{0,1},{1,2},{2,3},{3,4},{4,5},{5,6},{6,7},{15,8},{8,9},{9,10... | collective-permute-start | bytes 1572872 | tf_op jit(solution)/shard_map/while/body/eval_jaxpr/ppermute | solution.py:15
  321.6 13.9 %collective-permute-start = (bf16[2,512,2,128]{1,3,0,2:T(8,128)(2,1)}, bf16[2,512,2,128]{1,3,0,2:T(8,128)(2,1)S(1)}, u32[]{:S(2)}, u32[]{:S(2)}) collective-permute-start(bf16[2,512,2,128]{1,3,0,2:T(8,128)(2,1)} %get-tuple-element.1110), channel_id=1, source_target_pairs={{7,0},{0,1},{1,2},{2,3},{3,4},{4,5},{5,6},{6,7},{15,8},{8,9},{9,10... | collective-permute-start | bytes 1572872 | tf_op jit(solution)/shard_map/while/body/eval_jaxpr/ppermute | solution.py:15
  339.7 10.4 copy-start.11
  340.6 9.4 all-to-all-start.1
  352.1 8.0 copy-start.8
  356.0 4.9 copy-start.2
  356.0 4.9 copy-start.21
  356.0 4.9 copy-start.24
  364.5 11.7 %copy-start.12 = (f32[2,2,512,64]{2,3,1,0:T(8,128)S(1)}, f32[2,2,512,64]{2,3,1,0:T(8,128)}, u32[]{:S(2)}) copy-start(f32[2,2,512,64]{2,3,1,0:T(8,128)} %copy-done.11) | copy-start | bytes 1572868
  365.7 9.4 all-to-all-start.2
  369.1 385.6 %reduce-scatter.7.cloned.1.call-start = ((), (), s32[]{:S(2)}) async-start(), calls=%async_computation.11 | async-start | bytes 1081344 | tf_op jit(solution)/shard_map/reduce_scatter | solution.py:278
  370.5 426.2 %reduce-scatter.13.cloned.1.call-start = ((), (), s32[]{:S(2)}) async-start(), calls=%async_computation.14 | async-start | bytes 3244032
  381.2 4.5 copy-start
  389.8 18.6 %collective-permute-start.2 = (bf16[2,512,2,128]{1,3,0,2:T(8,128)(2,1)}, bf16[2,512,2,128]{1,3,0,2:T(8,128)(2,1)}, u32[]{:S(2)}, u32[]{:S(2)}) collective-permute-start(bf16[2,512,2,128]{1,3,0,2:T(8,128)(2,1)} %fusion.137), channel_id=1, source_target_pairs={{7,0},{0,1},{1,2},{2,3},{3,4},{4,5},{5,6},{6,7},{15,8},{8,9},{9,10... | collective-permute-start | bytes 1572872 | tf_op jit(solution)/shard_map/while/body/eval_jaxpr/ppermute | solution.py:15
  389.9 28.8 %collective-permute-start.1 = (bf16[2,512,2,128]{1,3,0,2:T(8,128)(2,1)S(1)}, bf16[2,512,2,128]{1,3,0,2:T(8,128)(2,1)}, u32[]{:S(2)}, u32[]{:S(2)}) collective-permute-start(bf16[2,512,2,128]{1,3,0,2:T(8,128)(2,1)S(1)} %copy.184), channel_id=1, source_target_pairs={{7,0},{0,1},{1,2},{2,3},{3,4},{4,5},{5,6},{6,7},{15,8},{8,9},{9,10... | collective-permute-start | bytes 1572872 | tf_op jit(solution)/shard_map/while/body/eval_jaxpr/ppermute | solution.py:15
  431.2 18.0 %collective-permute-start.2 = (bf16[2,512,2,128]{1,3,0,2:T(8,128)(2,1)}, bf16[2,512,2,128]{1,3,0,2:T(8,128)(2,1)}, u32[]{:S(2)}, u32[]{:S(2)}) collective-permute-start(bf16[2,512,2,128]{1,3,0,2:T(8,128)(2,1)} %fusion.137), channel_id=1, source_target_pairs={{7,0},{0,1},{1,2},{2,3},{3,4},{4,5},{5,6},{6,7},{15,8},{8,9},{9,10... | collective-permute-start | bytes 1572872 | tf_op jit(solution)/shard_map/while/body/eval_jaxpr/ppermute | solution.py:15
  431.2 27.2 %collective-permute-start.1 = (bf16[2,512,2,128]{1,3,0,2:T(8,128)(2,1)S(1)}, bf16[2,512,2,128]{1,3,0,2:T(8,128)(2,1)}, u32[]{:S(2)}, u32[]{:S(2)}) collective-permute-start(bf16[2,512,2,128]{1,3,0,2:T(8,128)(2,1)S(1)} %copy.184), channel_id=1, source_target_pairs={{7,0},{0,1},{1,2},{2,3},{3,4},{4,5},{5,6},{6,7},{15,8},{8,9},{9,10... | collective-permute-start | bytes 1572872 | tf_op jit(solution)/shard_map/while/body/eval_jaxpr/ppermute | solution.py:15
  471.0 18.0 %collective-permute-start.2 = (bf16[2,512,2,128]{1,3,0,2:T(8,128)(2,1)}, bf16[2,512,2,128]{1,3,0,2:T(8,128)(2,1)}, u32[]{:S(2)}, u32[]{:S(2)}) collective-permute-start(bf16[2,512,2,128]{1,3,0,2:T(8,128)(2,1)} %fusion.137), channel_id=1, source_target_pairs={{7,0},{0,1},{1,2},{2,3},{3,4},{4,5},{5,6},{6,7},{15,8},{8,9},{9,10... | collective-permute-start | bytes 1572872 | tf_op jit(solution)/shard_map/while/body/eval_jaxpr/ppermute | solution.py:15
  471.0 26.4 %collective-permute-start.1 = (bf16[2,512,2,128]{1,3,0,2:T(8,128)(2,1)S(1)}, bf16[2,512,2,128]{1,3,0,2:T(8,128)(2,1)}, u32[]{:S(2)}, u32[]{:S(2)}) collective-permute-start(bf16[2,512,2,128]{1,3,0,2:T(8,128)(2,1)S(1)} %copy.184), channel_id=1, source_target_pairs={{7,0},{0,1},{1,2},{2,3},{3,4},{4,5},{5,6},{6,7},{15,8},{8,9},{9,10... | collective-permute-start | bytes 1572872 | tf_op jit(solution)/shard_map/while/body/eval_jaxpr/ppermute | solution.py:15
  510.0 18.0 %collective-permute-start.2 = (bf16[2,512,2,128]{1,3,0,2:T(8,128)(2,1)}, bf16[2,512,2,128]{1,3,0,2:T(8,128)(2,1)}, u32[]{:S(2)}, u32[]{:S(2)}) collective-permute-start(bf16[2,512,2,128]{1,3,0,2:T(8,128)(2,1)} %fusion.137), channel_id=1, source_target_pairs={{7,0},{0,1},{1,2},{2,3},{3,4},{4,5},{5,6},{6,7},{15,8},{8,9},{9,10... | collective-permute-start | bytes 1572872 | tf_op jit(solution)/shard_map/while/body/eval_jaxpr/ppermute | solution.py:15
  510.0 25.6 %collective-permute-start.1 = (bf16[2,512,2,128]{1,3,0,2:T(8,128)(2,1)S(1)}, bf16[2,512,2,128]{1,3,0,2:T(8,128)(2,1)}, u32[]{:S(2)}, u32[]{:S(2)}) collective-permute-start(bf16[2,512,2,128]{1,3,0,2:T(8,128)(2,1)S(1)} %copy.184), channel_id=1, source_target_pairs={{7,0},{0,1},{1,2},{2,3},{3,4},{4,5},{5,6},{6,7},{15,8},{8,9},{9,10... | collective-permute-start | bytes 1572872 | tf_op jit(solution)/shard_map/while/body/eval_jaxpr/ppermute | solution.py:15
  548.2 17.6 %collective-permute-start.2 = (bf16[2,512,2,128]{1,3,0,2:T(8,128)(2,1)}, bf16[2,512,2,128]{1,3,0,2:T(8,128)(2,1)}, u32[]{:S(2)}, u32[]{:S(2)}) collective-permute-start(bf16[2,512,2,128]{1,3,0,2:T(8,128)(2,1)} %fusion.137), channel_id=1, source_target_pairs={{7,0},{0,1},{1,2},{2,3},{3,4},{4,5},{5,6},{6,7},{15,8},{8,9},{9,10... | collective-permute-start | bytes 1572872 | tf_op jit(solution)/shard_map/while/body/eval_jaxpr/ppermute | solution.py:15
  548.2 23.8 %collective-permute-start.1 = (bf16[2,512,2,128]{1,3,0,2:T(8,128)(2,1)S(1)}, bf16[2,512,2,128]{1,3,0,2:T(8,128)(2,1)}, u32[]{:S(2)}, u32[]{:S(2)}) collective-permute-start(bf16[2,512,2,128]{1,3,0,2:T(8,128)(2,1)S(1)} %copy.184), channel_id=1, source_target_pairs={{7,0},{0,1},{1,2},{2,3},{3,4},{4,5},{5,6},{6,7},{15,8},{8,9},{9,10... | collective-permute-start | bytes 1572872 | tf_op jit(solution)/shard_map/while/body/eval_jaxpr/ppermute | solution.py:15
  575.9 4.5 copy-start
  584.6 16.1 %collective-permute-start.2 = (bf16[2,512,2,128]{1,3,0,2:T(8,128)(2,1)}, bf16[2,512,2,128]{1,3,0,2:T(8,128)(2,1)}, u32[]{:S(2)}, u32[]{:S(2)}) collective-permute-start(bf16[2,512,2,128]{1,3,0,2:T(8,128)(2,1)} %fusion.137), channel_id=1, source_target_pairs={{7,0},{0,1},{1,2},{2,3},{3,4},{4,5},{5,6},{6,7},{15,8},{8,9},{9,10... | collective-permute-start | bytes 1572872 | tf_op jit(solution)/shard_map/while/body/eval_jaxpr/ppermute | solution.py:15
  584.6 22.0 %collective-permute-start.1 = (bf16[2,512,2,128]{1,3,0,2:T(8,128)(2,1)S(1)}, bf16[2,512,2,128]{1,3,0,2:T(8,128)(2,1)}, u32[]{:S(2)}, u32[]{:S(2)}) collective-permute-start(bf16[2,512,2,128]{1,3,0,2:T(8,128)(2,1)S(1)} %copy.184), channel_id=1, source_target_pairs={{7,0},{0,1},{1,2},{2,3},{3,4},{4,5},{5,6},{6,7},{15,8},{8,9},{9,10... | collective-permute-start | bytes 1572872 | tf_op jit(solution)/shard_map/while/body/eval_jaxpr/ppermute | solution.py:15
  619.2 14.6 %collective-permute-start.2 = (bf16[2,512,2,128]{1,3,0,2:T(8,128)(2,1)}, bf16[2,512,2,128]{1,3,0,2:T(8,128)(2,1)}, u32[]{:S(2)}, u32[]{:S(2)}) collective-permute-start(bf16[2,512,2,128]{1,3,0,2:T(8,128)(2,1)} %fusion.137), channel_id=1, source_target_pairs={{7,0},{0,1},{1,2},{2,3},{3,4},{4,5},{5,6},{6,7},{15,8},{8,9},{9,10... | collective-permute-start | bytes 1572872 | tf_op jit(solution)/shard_map/while/body/eval_jaxpr/ppermute | solution.py:15
  619.2 20.2 %collective-permute-start.1 = (bf16[2,512,2,128]{1,3,0,2:T(8,128)(2,1)S(1)}, bf16[2,512,2,128]{1,3,0,2:T(8,128)(2,1)}, u32[]{:S(2)}, u32[]{:S(2)}) collective-permute-start(bf16[2,512,2,128]{1,3,0,2:T(8,128)(2,1)S(1)} %copy.184), channel_id=1, source_target_pairs={{7,0},{0,1},{1,2},{2,3},{3,4},{4,5},{5,6},{6,7},{15,8},{8,9},{9,10... | collective-permute-start | bytes 1572872 | tf_op jit(solution)/shard_map/while/body/eval_jaxpr/ppermute | solution.py:15
  652.0 13.6 %collective-permute-start.2 = (bf16[2,512,2,128]{1,3,0,2:T(8,128)(2,1)}, bf16[2,512,2,128]{1,3,0,2:T(8,128)(2,1)}, u32[]{:S(2)}, u32[]{:S(2)}) collective-permute-start(bf16[2,512,2,128]{1,3,0,2:T(8,128)(2,1)} %fusion.137), channel_id=1, source_target_pairs={{7,0},{0,1},{1,2},{2,3},{3,4},{4,5},{5,6},{6,7},{15,8},{8,9},{9,10... | collective-permute-start | bytes 1572872 | tf_op jit(solution)/shard_map/while/body/eval_jaxpr/ppermute | solution.py:15
  652.0 19.3 %collective-permute-start.1 = (bf16[2,512,2,128]{1,3,0,2:T(8,128)(2,1)S(1)}, bf16[2,512,2,128]{1,3,0,2:T(8,128)(2,1)}, u32[]{:S(2)}, u32[]{:S(2)}) collective-permute-start(bf16[2,512,2,128]{1,3,0,2:T(8,128)(2,1)S(1)} %copy.184), channel_id=1, source_target_pairs={{7,0},{0,1},{1,2},{2,3},{3,4},{4,5},{5,6},{6,7},{15,8},{8,9},{9,10... | collective-permute-start | bytes 1572872 | tf_op jit(solution)/shard_map/while/body/eval_jaxpr/ppermute | solution.py:15
  672.8 20.4 %copy-start.15 = (bf16[2,128,512]{2,1,0:T(8,128)(2,1)S(1)}, bf16[2,128,512]{2,1,0:T(8,128)(2,1)}, u32[]{:S(2)}) copy-start(bf16[2,128,512]{2,1,0:T(8,128)(2,1)} %param.17) | copy-start | bytes 786436
  697.4 244.9 %reduce-scatter.9.cloned.1.call-start = ((), (), s32[]{:S(2)}) async-start(), calls=%async_computation.12 | async-start | bytes 4325376 | tf_op jit(solution)/shard_map/reduce_scatter | solution.py:279
  701.5 385.6 %reduce-scatter.11.cloned.1.call-start = ((), (), s32[]{:S(2)}) async-start(), calls=%async_computation.13 | async-start | bytes 4325376 | tf_op jit(solution)/shard_map/reduce_scatter | solution.py:280
  704.3 5.2 copy-start.6
  704.3 48.1 %copy-start.4 = (bf16[256,1536]{1,0:T(8,128)(2,1)S(1)}, bf16[256,1536]{1,0:T(8,128)(2,1)}, u32[]{:S(2)}) copy-start(bf16[256,1536]{1,0:T(8,128)(2,1)} %reshape.358) | copy-start | bytes 2359300
  704.3 48.1 %copy-start.13 = (bf16[512,1536]{1,0:T(8,128)(2,1)S(1)}, bf16[512,1536]{1,0:T(8,128)(2,1)}, u32[]{:S(2)}) copy-start(bf16[512,1536]{1,0:T(8,128)(2,1)} %all-gather.4.cloned.1.call-done) | copy-start | bytes 4718596
  (24 other events, 82.9 us)
Sparse Core Ops, SparseCore 0:
  10.9 57.8 all-gather.3
  71.7 55.4 all-gather.5
  130.2 55.7 all-gather.7
  372.5 235.4 reduce-scatter.6
  697.5 99.1 reduce-scatter.12
  799.5 142.7 reduce-scatter.8
  945.3 141.7 reduce-scatter.10
where the time goes:
time: 1100 us; the launch traced here: 1090 us
  waiting for transfers between devices  587 us (53%)
  blocking collectives  230 us (21%)
  matrix products  146 us (13%)
  other arithmetic  57.5 us (5%)
  local copies, waits for them, and re-layouts  44.4 us (4%)
  between operations  14.7 us (1%)
  starting transfers between devices  13.1 us (1%)
    ppermute x23, waiting for transfers between devices, from_behind(): return lax.ppermute(block, axis, route)  243 us
    reduce_scatter x1, waiting for transfers between devices, local(): lax.psum_scatter(up_grad, ('head', 'blk'), scatter_dimension=0, tiled=True)  146 us
    reduce_scatter x1, waiting for transfers between devices, local(): lax.psum_scatter(down_grad, ('head', 'blk'), scatter_dimension=0, tiled=T...  145 us
    unnamed x2, blocking collectives  81 us
    all_gather x1, blocking collectives, local(): lax.all_gather(output_weight, ('head', 'blk'), axis=0, tiled=True)  67.5 us
    all_gather x1, blocking collectives, local(): all_numbers = lax.all_gather(segments, ('head', 'blk'), axis=1, tiled=True)  66.3 us
    unnamed x8, waiting for transfers between devices  44.1 us
    dot_general x8, matrix products, backward_turn(): jnp.einsum('shqk,sqhd->skhd', probs, grad_attended_wide, preferred_elemen...  30.2 us
  transfers between devices with their start and end apart: 33, of which 28 were waited for; matrix products, arithmetic and copies ran while one was open for 21% of the time, Pallas kernels for 0%

commit v1 on v0

v1 whole, which is shorter than its diff:
```python
import functools
import math

import jax
import jax.numpy as jnp
from jax import lax
from jax.experimental import pallas as pl
from jax.experimental.pallas import tpu as pltpu
from jax.sharding import PartitionSpec as P

HEADS = 8
HD = 64
LANES = 128
GROUP = 16
BLOCK = 256
VMEM_BYTES = 56 * 1024 * 1024
F32 = jnp.float32
BF16 = jnp.bfloat16
VMEM = pltpu.VMEM
NEG = -1e30


class Place:
    def __init__(self, blocks):
        self.blocks = blocks
        self.depth = blocks // 2
        head = lax.axis_index("head")
        block = lax.axis_index("blk")
        self.x, self.core = lax.div(head, 2), lax.rem(head, 2)
        self.z, self.y = lax.div(block, 2), lax.rem(block, 2)
        flat = head * blocks + block
        self.part, self.slot = lax.div(flat, GROUP), lax.rem(flat, GROUP)

    def at(self, x=None, core=None, z=None, y=None):
        x = self.x if x is None else x
        core = self.core if core is None else core
        z = self.z if z is None else z
        y = self.y if y is None else y
        return (x * 2 + core, z * 2 + y)

    def deeper(self, offset):
        return lax.rem(self.z + offset + self.depth, self.depth)

    def member(self, slot, part=None):
        part = self.part if part is None else part
        flat = part * GROUP + slot
        return (lax.div(flat, self.blocks), lax.rem(flat, self.blocks))

    def other_slot(self, offset):
        return lax.rem(self.slot + offset + GROUP, GROUP)


def remote(src, dst, send, recv, device):
    return pltpu.make_async_remote_copy(
        src_ref=src,
        dst_ref=dst,
        send_sem=send,
        recv_sem=recv,
        device_id=device,
        device_id_type=pl.DeviceIdType.MESH,
    )


def greet(place, parts, tree):
    barrier = pltpu.get_barrier_semaphore()

    def hello(device):
        pl.semaphore_signal(barrier, inc=1, device_id=device, device_id_type=pl.DeviceIdType.MESH)

    def group(offset, carry):
        hello(place.member(place.other_slot(offset)))
        return carry

    lax.fori_loop(1, GROUP, group, 0)
    total = GROUP - 1
    if tree:

        def line(offset, carry):
            hello(place.at(z=place.deeper(offset)))
            return carry

        lax.fori_loop(1, place.depth, line, 0)
        hello(place.at(x=1 - place.x))
        hello(place.at(y=1 - place.y))
        hello(place.at(core=1 - place.core))
        total += place.depth + 2
    if parts > 1 and tree:

        @pl.when(place.part > 0)
        def _():
            hello(place.member(place.slot, place.part - 1))

        @pl.when(place.part < parts - 1)
        def _():
            hello(place.member(place.slot, place.part + 1))

        total += jnp.where(place.part > 0, 1, 0) + jnp.where(place.part < parts - 1, 1, 0)
    pl.semaphore_wait(barrier, total)


def halves_of(columns):
    if columns < 2 * LANES:
        return ((0, columns, "yx"),)
    return ((0, columns // 2, "yx"), (columns // 2, columns // 2, "xy"))


class Gather:
    def __init__(self, place, src, dst, send, recv, local):
        self.place, self.src, self.dst = place, src, dst
        self.send, self.recv, self.local = send, recv, local
        self.halves = halves_of(dst.shape[-1])
        self.lines = place.depth - 1

    @staticmethod
    def semaphores(depth):
        return depth + 8

    def cut(self, half, *index):
        start, width, _ = half
        return self.dst.at[index + (slice(None), pl.ds(start, width))]

    def pair(self, half, first, x, y):
        place, every = self.place, slice(None)
        if first:
            return self.cut(half, x, place.core, every, y)
        if half[2] == "yx":
            return self.cut(half, x, place.core, every, every)
        return self.cut(half, every, place.core, every, y)

    def across(self, half, first):
        place = self.place
        if (half[2] == "yx") == first:
            return place.x, 1 - place.y
        return 1 - place.x, place.y

    def line(self, offset, come):
        place = self.place
        z = place.deeper(-offset) if come else place.z
        return remote(
            self.src,
            self.dst.at[place.x, place.core, z, place.y],
            self.send.at[offset - 1],
            self.recv.at[offset - 1],
            place.at(z=place.deeper(offset)),
        )

    def own(self):
        place = self.place
        return pltpu.make_async_copy(
            self.src, self.dst.at[place.x, place.core, place.z, place.y], self.local
        )

    def exchange(self, number, first, come):
        half = self.halves[number]
        place = self.place
        x, y = self.across(half, first)
        slot = self.lines + (0 if first else 2) + number
        mine = self.pair(half, first, place.x, place.y)
        landing = self.pair(half, first, x, y) if come else mine
        return remote(
            mine, landing, self.send.at[slot], self.recv.at[slot], place.at(x=x, y=y)
        )

    def hand(self, which, come):
        place, every = self.place, slice(None)
        slot = self.lines + 4 + which
        core = 1 - place.core if come else place.core

        def region(core):
            if which == 0:
                return self.dst.at[place.x, core, every, place.y]
            number = (which - 1) % 2
            half = self.halves[number]
            first = which < 3
            x, y = self.across(half, first)
            if first:
                return self.cut(half, x, core, every, y)
            if half[2] == "yx":
                return self.cut(half, x, core, every, every)
            return self.cut(half, every, core, every, y)

        return remote(
            region(place.core),
            region(core),
            self.send.at[slot],
            self.recv.at[slot],
            place.at(core=1 - place.core),
        )

    def start_line(self):
        for offset in range(1, self.lines + 1):
            self.line(offset, False).start()
        self.own().start()

    def start_first(self):
        self.own().wait()
        for offset in range(1, self.lines + 1):
            self.line(offset, True).wait_recv()
        for number in range(len(self.halves)):
            self.exchange(number, True, False).start()
        self.hand(0, False).start()

    def start_second(self):
        for number in range(len(self.halves)):
            self.exchange(number, True, True).wait_recv()
            self.exchange(number, False, False).start()
            self.hand(1 + number, False).start()

    def start_last(self):
        for number in range(len(self.halves)):
            self.exchange(number, False, True).wait_recv()
            self.hand(3 + number, False).start()

    def hands(self):
        for number in range(len(self.halves)):
            yield 1 + number
            yield 3 + number

    def finish(self):
        self.hand(0, True).wait_recv()
        for which in self.hands():
            self.hand(which, True).wait_recv()

    def drain(self):
        for offset in range(1, self.lines + 1):
            self.line(offset, False).wait_send()
        for number in range(len(self.halves)):
            self.exchange(number, True, False).wait_send()
            self.exchange(number, False, False).wait_send()
        self.hand(0, False).wait_send()
        for which in self.hands():
            self.hand(which, False).wait_send()


class Reduce:
    def __init__(self, place, part, out, rc, total, ra, rb, fa, fb, rz, send, recv):
        self.place, self.part, self.out = place, part, out
        self.rc, self.total, self.rz = rc, total, rz
        self.second, self.first = (ra, rb), (fa, fb)
        self.send, self.recv = send, recv
        self.halves = halves_of(part.shape[-1])
        self.lines = place.depth - 1

    @staticmethod
    def semaphores(depth):
        return depth + 4

    @staticmethod
    def scratch(depth, rows, cols, dtype):
        wide = halves_of(cols)[0][1]
        return [
            VMEM((2, depth, 2, rows, cols), dtype),
            VMEM((2, depth, 2, rows, cols), dtype),
            VMEM((depth, 2, rows, wide), dtype),
            VMEM((2, depth, rows, wide), dtype),
            VMEM((depth, rows, wide), dtype),
            VMEM((depth, rows, wide), dtype),
            VMEM((depth - 1, rows, cols), dtype),
            pltpu.SemaphoreType.DMA((Reduce.semaphores(depth),)),
            pltpu.SemaphoreType.DMA((Reduce.semaphores(depth),)),
        ]

    def core(self):
        place, every = self.place, slice(None)
        return remote(
            self.part.at[every, 1 - place.core],
            self.rc,
            self.send.at[0],
            self.recv.at[0],
            place.at(core=1 - place.core),
        )

    def cut(self, half, *index):
        start, width, _ = half
        return index + (slice(None), pl.ds(start, width))

    def exchange(self, number, second):
        place, every = self.place, slice(None)
        half = self.halves[number]
        slot = (1 if second else 3) + number
        over_x = (half[2] == "yx") == second
        device = place.at(x=1 - place.x) if over_x else place.at(y=1 - place.y)
        if second:
            index = (1 - place.x, every, every) if over_x else (every, every, 1 - place.y)
            landing = self.second[number]
        else:
            index = (1 - place.x, every, place.y) if over_x else (place.x, every, 1 - place.y)
            landing = self.first[number]
        return remote(
            self.total.at[self.cut(half, *index)],
            landing,
            self.send.at[slot],
            self.recv.at[slot],
            device,
        )

    def line(self, offset):
        place = self.place
        return remote(
            self.total.at[place.x, place.deeper(offset), place.y],
            self.rz.at[offset - 1],
            self.send.at[4 + offset],
            self.recv.at[4 + offset],
            place.at(z=place.deeper(offset)),
        )

    def start_core(self):
        self.core().start()

    def start_second(self):
        place = self.place
        self.core().wait_recv()
        dtype = self.total.dtype

        def add(z, carry):
            for x in range(2):
                for y in range(2):
                    self.total[x, z, y] = (
                        self.part[x, place.core, z, y].astype(F32) + self.rc[x, z, y].astype(F32)
                    ).astype(dtype)
            return carry

        lax.fori_loop(0, place.depth, add, 0)
        for number in range(len(self.halves)):
            self.exchange(number, True).start()

    def accumulate(self, index, value):
        self.total[index] = (self.total[index].astype(F32) + value.astype(F32)).astype(
            self.total.dtype
        )

    def start_first(self):
        place = self.place
        for number, half in enumerate(self.halves):
            self.exchange(number, True).wait_recv()
            landed = self.second[number]

            def add(z, carry):
                for other in range(2):
                    if half[2] == "yx":
                        self.accumulate(self.cut(half, place.x, z, other), landed[z, other])
                    else:
                        self.accumulate(self.cut(half, other, z, place.y), landed[other, z])
                return carry

            lax.fori_loop(0, place.depth, add, 0)
            self.exchange(number, False).start()

    def start_line(self):
        place = self.place
        for number, half in enumerate(self.halves):
            self.exchange(number, False).wait_recv()
            landed = self.first[number]

            def add(z, carry):
                self.accumulate(self.cut(half, place.x, z, place.y), landed[z])
                return carry

            lax.fori_loop(0, place.depth, add, 0)
        for offset in range(1, self.lines + 1):
            self.line(offset).start()

    def finish(self):
        place = self.place
        for offset in range(1, self.lines + 1):
            self.line(offset).wait_recv()
        result = self.total[place.x, place.z, place.y].astype(F32)
        for offset in range(1, self.lines + 1):
            result = result + self.rz[offset - 1].astype(F32)
        self.out[...] = result

    def drain(self):
        self.core().wait_send()
        for number in range(len(self.halves)):
            self.exchange(number, True).wait_send()
            self.exchange(number, False).wait_send()
        for offset in range(1, self.lines + 1):
            self.line(offset).wait_send()


def iota(shape, dim):
    return lax.broadcasted_iota(jnp.int32, shape, dim)


def dot(left, right):
    return lax.dot_general(left, right, (((1,), (0,)), ((), ())), preferred_element_type=F32)


def dot_nt(left, right):
    return lax.dot_general(left, right, (((1,), (1,)), ((), ())), preferred_element_type=F32)


def dot_tn(left, right):
    return lax.dot_general(left, right, (((0,), (0,)), ((), ())), preferred_element_type=F32)


def shift_of(size):
    assert size & (size - 1) == 0
    return size.bit_length() - 1


def spread_bias(gathered, offset, per, total):
    rows = gathered.shape[0]
    column = iota((LANES, total), 1)
    pick = iota((LANES, total), 0) == offset + (column & (per - 1))
    spread = dot(gathered.astype(BF16), pick.astype(BF16))
    owner = jnp.right_shift(iota((rows, total), 1), shift_of(per)) * 8
    return jnp.sum(jnp.where(iota((rows, total), 0) == owner, spread, 0.0), axis=0, keepdims=True)


def fold_bias(row, rows, offset, per):
    total = row.shape[1]
    owner = jnp.right_shift(iota((rows, total), 1), shift_of(per)) * 8
    chosen = jnp.where(iota((rows, total), 0) == owner, row, 0.0)
    column = iota((total, LANES), 0)
    put = iota((total, LANES), 1) == offset + (column & (per - 1))
    return lax.dot_general(
        chosen,
        put.astype(F32),
        (((1,), (0,)), ((), ())),
        precision=lax.Precision.HIGHEST,
        preferred_element_type=F32,
    )


def bias_places(devices, width, hidden):
    per, per_up = width // devices, hidden // devices
    return {
        "query": (0, per),
        "value": (per, per),
        "output": (2 * per, per),
        "down": (3 * per, per),
        "up": (4 * per, per_up),
    }


def project_kernel(
    blocks,
    parts,
    window,
    docs,
    places,
    x_ref,
    seg_ref,
    aux_ref,
    win_ref,
    wo_ref,
    wup_ref,
    wdown_ref,
    qt_ref,
    kv_ref,
    starts_ref,
    gwin,
    gwo,
    gwup,
    gwdown,
    gaux,
    segs,
    tile,
    qs,
    ks,
    *sems,
):
    place = Place(blocks)
    (
        win_s,
        win_r,
        aux_s,
        aux_r,
        wo_s,
        wo_r,
        wup_s,
        wup_r,
        wdown_s,
        wdown_r,
        seg_s,
        seg_r,
        q_s,
        q_r,
        k_s,
        k_r,
        halo_s,
        halo_r,
        local,
    ) = sems
    greet(place, parts, True)
    g_win = Gather(place, win_ref, gwin, win_s, win_r, local.at[0])
    g_aux = Gather(place, aux_ref, gaux, aux_s, aux_r, local.at[1])
    g_wo = Gather(place, wo_ref, gwo, wo_s, wo_r, local.at[2])
    g_wup = Gather(place, wup_ref, gwup, wup_s, wup_r, local.at[3])
    g_wdown = Gather(place, wdown_ref, gwdown, wdown_s, wdown_r, local.at[4])
    rest = (g_wo, g_wup, g_wdown)
    g_win.start_line()
    g_aux.start_line()

    row = iota((16, LANES), 0)
    numbers = seg_ref[...].astype(F32)
    tile[...] = jnp.where(row == 0, numbers[0:1], numbers[1:2]).astype(BF16)
    segs[window + place.slot] = tile[...]

    def seg_copy(offset, come):
        landing = place.other_slot(-offset) if come else place.slot
        return remote(
            tile,
            segs.at[window + landing],
            seg_s.at[offset],
            seg_r.at[offset],
            place.member(place.other_slot(offset)),
        )

    def seg_start(offset, carry):
        seg_copy(offset, False).start()
        return carry

    lax.fori_loop(1, GROUP, seg_start, 0)

    g_win.start_first()
    g_aux.start_first()
    for gather in rest:
        gather.start_line()
    g_win.start_second()
    g_aux.start_second()

    def seg_wait(offset, carry):
        seg_copy(offset, True).wait_recv()
        return carry

    lax.fori_loop(1, GROUP, seg_wait, 0)

    def seg_halo(part):
        return remote(
            segs.at[pl.ds(GROUP, window)],
            segs.at[pl.ds(0, window)],
            halo_s.at[window],
            halo_r.at[window],
            place.member(place.slot, part),
        )

    if parts > 1:

        @pl.when(place.part < parts - 1)
        def _():
            seg_halo(place.part + 1).start()

    g_win.start_last()
    g_aux.start_last()
    g_win.finish()
    g_aux.finish()

    width = x_ref.shape[-1]
    devices = gaux.shape[0] * gaux.shape[1] * gaux.shape[2] * gaux.shape[3]
    aux = gaux[...].reshape(devices * 8, LANES)
    bias_q = spread_bias(aux, *places["query"], width)
    bias_v = spread_bias(aux, *places["value"], width)
    tokens = x_ref[...].reshape(2 * LANES, width)
    low_lane = iota((LANES, LANES), 1) < HD
    wide = 2 * LANES
    for t in range(width // wide):

        def column(kind):
            weight = gwin[:, :, :, :, :, pl.ds(kind * width + t * wide, wide)]
            return dot(tokens, weight.reshape(width, wide))

        cols = slice(t * wide, (t + 1) * wide)
        q = (column(0) + bias_q[:, cols]).astype(BF16).astype(F32) * 0.125
        k = column(1).astype(BF16).astype(F32)
        v = (column(2) + bias_v[:, cols]).astype(BF16).astype(F32)
        for s in range(2):
            for u in range(2):
                first = s * HEADS + t * 4 + u * 2
                here = (slice(s * LANES, (s + 1) * LANES), slice(u * LANES, (u + 1) * LANES))
                turned = q[here].T.astype(BF16)
                qs[first] = turned[:HD]
                qs[first + 1] = turned[HD:]
                k_here, v_here = k[here], v[here]
                ks[first] = jnp.where(low_lane, k_here, pltpu.roll(v_here, HD, 1)).astype(BF16)
                ks[first + 1] = jnp.where(low_lane, pltpu.roll(k_here, HD, 1), v_here).astype(BF16)

    def q_copy(offset, come):
        landing = place.other_slot(-offset) if come else place.slot
        target = place.other_slot(offset)
        return remote(
            qs.at[target], qt_ref.at[landing], q_s.at[offset], q_r.at[offset], place.member(target)
        )

    def k_copy(offset, come):
        landing = place.other_slot(-offset) if come else place.slot
        target = place.other_slot(offset)
        return remote(
            ks.at[target],
            kv_ref.at[window + landing],
            k_s.at[offset],
            k_r.at[offset],
            place.member(target),
        )

    def qk_start(offset, carry):
        k_copy(offset, False).start()
        q_copy(offset, False).start()
        return carry

    lax.fori_loop(1, GROUP, qk_start, 0)
    qt_ref[place.slot] = qs[place.slot]
    kv_ref[window + place.slot] = ks[place.slot]

    for gather in rest:
        gather.start_first()

    if parts > 1:

        @pl.when(place.part < parts - 1)
        def _():
            seg_halo(place.part + 1).wait_send()

        @pl.when(place.part > 0)
        def _():
            seg_halo(place.part - 1).wait_recv()

    span = window + GROUP
    sequence = lax.div(place.slot, HEADS)
    chosen = jnp.where(iota((span, 16, LANES), 1) == sequence, segs[...].astype(F32), 0.0)
    seen = jnp.sum(chosen, axis=1)
    outside = (iota((span, LANES), 0) < window) & (place.part == 0)
    seen = jnp.where(outside, -1.0, seen)
    own = seen[window:]
    start = jnp.zeros((GROUP, LANES), F32)
    for number in range(docs):
        count = jnp.sum(jnp.where(seen == number - 1, 1.0, 0.0), axis=0, keepdims=True)
        count = jnp.sum(count, axis=1, keepdims=True)
        start = start + jnp.where(own >= number, count, 0.0)
    starts_ref[...] = start.astype(jnp.int32)

    for gather in rest:
        gather.start_second()

    def halo_copy(entry, part):
        return remote(
            kv_ref.at[GROUP + entry],
            kv_ref.at[entry],
            halo_s.at[entry],
            halo_r.at[entry],
            place.member(place.slot, part),
        )

    def pass_on(source):
        if parts > 1:

            @pl.when((place.part < parts - 1) & (source >= GROUP - window))
            def _():
                halo_copy(source - (GROUP - window), place.part + 1).start()

    pass_on(place.slot)

    def qk_wait(offset, carry):
        k_copy(offset, True).wait_recv()
        q_copy(offset, True).wait_recv()
        pass_on(place.other_slot(-offset))
        return carry

    lax.fori_loop(1, GROUP, qk_wait, 0)
    for gather in rest:
        gather.start_last()
    if parts > 1:

        @pl.when(place.part > 0)
        def _():
            def wait(entry, carry):
                halo_copy(entry, place.part - 1).wait_recv()
                return carry

            lax.fori_loop(0, window, wait, 0)

    for gather in rest:
        gather.finish()

    if parts > 1:

        @pl.when(place.part < parts - 1)
        def _():
            def wait(entry, carry):
                halo_copy(entry, place.part + 1).wait_send()
                return carry

            lax.fori_loop(0, window, wait, 0)

    def sent(offset, carry):
        seg_copy(offset, False).wait_send()
        q_copy(offset, False).wait_send()
        k_copy(offset, False).wait_send()
        return carry

    lax.fori_loop(1, GROUP, sent, 0)
    for gather in (g_win, g_aux) + rest:
        gather.drain()


def block_scores(kv, q_wide, u, start, q_place):
    scores = dot(kv, q_wide)
    k_place = u * BLOCK + iota((BLOCK, BLOCK), 0)
    visible = (k_place >= start) & (k_place <= q_place)
    return jnp.where(visible, scores, NEG)


def two(ref, index):
    return jnp.concatenate([ref[index], ref[index + 1]], axis=1)


def two_rows(ref, index):
    return jnp.concatenate([ref[pl.ds(index, 1)], ref[pl.ds(index + 1, 1)]], axis=1)


def attend_kernel(window, qt_ref, kv_ref, starts_ref, first_ref, ot_ref, of_ref, lse_ref, kvt):
    span = window + GROUP

    def turn(c, carry):
        kvt[c] = kv_ref[c].T
        return carry

    lax.fori_loop(0, span, turn, 0)

    def q_block(m, carry):
        q_wide = jnp.concatenate([two(qt_ref, 2 * m), jnp.zeros((HD, BLOCK), BF16)], axis=0)
        start = two_rows(starts_ref, 2 * m)
        diagonal = window // 2 + m
        q_place = diagonal * BLOCK + iota((1, BLOCK), 1)
        lowest = lax.div(first_ref[2 * m, 0], BLOCK)

        def k_block(step, state):
            peak, total, out = state
            u = diagonal - step
            kv = kv_ref[pl.ds(2 * u, 2)].reshape(BLOCK, LANES)
            scores = block_scores(kv, q_wide, u, start, q_place)
            newest = jnp.maximum(peak, jnp.max(scores, axis=0, keepdims=True))
            weights = jnp.exp(scores - newest)
            factor = jnp.exp(peak - newest)
            values = two(kvt, 2 * u)[HD:]
            out = out * factor + dot(values, weights.astype(BF16))
            total = total * factor + jnp.sum(weights, axis=0, keepdims=True)
            return newest, total, out

        state = (
            jnp.full((1, BLOCK), NEG, F32),
            jnp.zeros((1, BLOCK), F32),
            jnp.zeros((HD, BLOCK), F32),
        )
        peak, total, out = lax.fori_loop(0, diagonal - lowest + 1, k_block, state)
        out = out / total
        lse = peak + jnp.log(total)
        for side in range(2):
            lanes = slice(side * LANES, (side + 1) * LANES)
            of_ref[2 * m + side] = out[:, lanes]
            ot_ref[2 * m + side] = out[:, lanes].astype(BF16)
            lse_ref[pl.ds(2 * m + side, 1)] = lse[:, lanes]
        return carry

    lax.fori_loop(0, GROUP // 2, q_block, 0)


def middle_kernel(
    blocks,
    parts,
    places,
    ot_ref,
    x_ref,
    grad_ref,
    alphas_ref,
    wo_ref,
    wup_ref,
    wdown_ref,
    gaux_ref,
    out_ref,
    doct_ref,
    gres_ref,
    gup_ref,
    gdown_ref,
    gout_ref,
    rows_ref,
    up_row_ref,
    mixed_t,
    dos,
    act_s,
    gpre_s,
    o_s,
    o_r,
    d_s,
    d_r,
):
    place = Place(blocks)
    greet(place, parts, False)

    def o_copy(offset, come):
        landing = place.other_slot(-offset) if come else place.slot
        target = place.other_slot(offset)
        return remote(
            ot_ref.at[target], mixed_t.at[landing], o_s.at[offset], o_r.at[offset], place.member(target)
        )

    def d_copy(offset, come):
        landing = place.other_slot(-offset) if come else place.slot
        target = place.other_slot(offset)
        return remote(
            dos.at[target], doct_ref.at[landing], d_s.at[offset], d_r.at[offset], place.member(target)
        )

    def loop(call):
        def step(offset, carry):
            call(offset)
            return carry

        lax.fori_loop(1, GROUP, step, 0)

    loop(lambda offset: o_copy(offset, False).start())
    mixed_t[place.slot] = ot_ref[place.slot]

    width, hidden = wup_ref.shape
    a0, a1 = alphas_ref[0], alphas_ref[1]
    bias_out = spread_bias(gaux_ref[...], *places["output"], width)
    bias_down = spread_bias(gaux_ref[...], *places["down"], width)
    bias_up = spread_bias(gaux_ref[...], *places["up"], hidden)
    rows = 2 * LANES
    tokens = x_ref[...].reshape(rows, width).astype(F32)
    grads = grad_ref[...].reshape(rows, width).astype(F32)
    grad_ffn = (a1 * grads).astype(BF16)

    loop(lambda offset: o_copy(offset, True).wait_recv())

    mixed_turned = mixed_t[...].reshape(2, width, LANES)
    mixed = jnp.concatenate([mixed_turned[0].T, mixed_turned[1].T], axis=0)
    branch = dot(mixed, wo_ref[...]) + bias_out
    attn_term = a0 * branch
    residual = tokens + attn_term
    hidden_in = residual.astype(BF16)

    ffn = jnp.zeros((rows, width), F32) + bias_down
    grad_res = grads
    wide = 512
    for t in range(hidden // wide):
        cols = pl.ds(t * wide, wide)
        w_up = wup_ref[:, cols]
        w_down = wdown_ref[cols, :]
        pre = dot(hidden_in, w_up) + bias_up[:, t * wide : (t + 1) * wide]
        phi = 0.5 * (1.0 + lax.erf(pre * (1.0 / math.sqrt(2.0))))
        act = (pre * phi).astype(BF16)
        act_s[:, cols] = act
        ffn = ffn + dot(act, w_down)
        slope = phi + pre * jnp.exp(-0.5 * pre * pre) * (1.0 / math.sqrt(2.0 * math.pi))
        gpre = (dot_nt(grad_ffn, w_down) * slope).astype(BF16)
        gpre_s[:, cols] = gpre
        grad_res = grad_res + dot_nt(gpre, w_up)
    gres_ref[...] = grad_res
    grad_branch = (a0 * grad_res).astype(BF16)
    grad_mixed = dot_nt(grad_branch, wo_ref[...]).astype(BF16).astype(F32)
    for s in range(2):
        turned = grad_mixed[s * LANES : (s + 1) * LANES].T.astype(BF16)
        dos[pl.ds(s * HEADS, HEADS)] = turned.reshape(HEADS, HD, LANES)
    loop(lambda offset: d_copy(offset, False).start())
    doct_ref[place.slot] = dos[place.slot]

    ffn_term = a1 * ffn
    stream = residual + ffn_term
    out_ref[...] = stream.astype(BF16).reshape(2, LANES, width)

    def whole(values):
        return jnp.sum(jnp.sum(values, axis=0, keepdims=True), axis=1, keepdims=True)

    sums = (
        whole(stream * stream),
        whole(attn_term * attn_term),
        whole(ffn_term * ffn_term),
        whole(grad_res * branch),
        whole(grads * ffn),
    )
    lane = iota((1, width), 1)
    scalars = jnp.zeros((1, width), F32)
    for number, value in enumerate(sums):
        scalars = scalars + jnp.where(lane == number, value, 0.0)
    down_row = jnp.sum(grad_ffn.astype(F32), axis=0, keepdims=True)
    out_row = jnp.sum(grad_branch.astype(F32), axis=0, keepdims=True)
    row = iota((8, width), 0)
    rows_ref[...] = jnp.where(
        row == 0, down_row, jnp.where(row == 1, out_row, jnp.where(row == 2, scalars, 0.0))
    )
    gout_ref[...] = dot(
        jnp.concatenate([mixed_turned[0], mixed_turned[1]], axis=1), grad_branch
    ).astype(BF16)
    for t in range(hidden // wide):
        cols = pl.ds(t * wide, wide)
        gpre = gpre_s[:, cols]
        up_row_ref[:, cols] = jnp.zeros((8, wide), F32) + jnp.sum(
            gpre.astype(F32), axis=0, keepdims=True
        )
        gup_ref[:, cols] = dot_tn(hidden_in, gpre).astype(BF16)
        gdown_ref[cols, :] = dot_tn(act_s[:, cols], grad_ffn).astype(BF16)

    loop(lambda offset: d_copy(offset, True).wait_recv())
    loop(lambda offset: o_copy(offset, False).wait_send())
    loop(lambda offset: d_copy(offset, False).wait_send())


def attend_back_kernel(
    window, qt_ref, kv_ref, starts_ref, first_ref, of_ref, lse_ref, dot_ref, dqt_ref, dkv_ref, kvt, acc
):
    span = window + GROUP

    def turn(c, carry):
        kvt[c] = kv_ref[c].T
        acc[c] = jnp.zeros((LANES, LANES), F32)
        return carry

    lax.fori_loop(0, span, turn, 0)
    low_lane = iota((BLOCK, LANES), 1) < HD

    def q_block(m, carry):
        qt, dt = two(qt_ref, 2 * m), two(dot_ref, 2 * m)
        blank = jnp.zeros((HD, BLOCK), BF16)
        q_wide = jnp.concatenate([qt, blank], axis=0)
        d_wide = jnp.concatenate([blank, dt], axis=0)
        both = jnp.concatenate([qt, dt], axis=0).astype(F32).T
        q_rows = jnp.where(low_lane, both, 0.0).astype(BF16)
        d_rows = jnp.where(low_lane, 0.0, both).astype(BF16)
        start = two_rows(starts_ref, 2 * m)
        lse = two_rows(lse_ref, 2 * m)
        delta = jnp.sum(dt.astype(F32) * two(of_ref, 2 * m), axis=0, keepdims=True)
        diagonal = window // 2 + m
        q_place = diagonal * BLOCK + iota((1, BLOCK), 1)
        lowest = lax.div(first_ref[2 * m, 0], BLOCK)

        def k_block(step, dq):
            u = diagonal - step
            kv = kv_ref[pl.ds(2 * u, 2)].reshape(BLOCK, LANES)
            probs = jnp.exp(block_scores(kv, q_wide, u, start, q_place) - lse)
            grad_probs = dot(kv, d_wide)
            grad_scores = (probs * (grad_probs - delta)).astype(BF16)
            grad = dot(grad_scores, q_rows) + dot(probs.astype(BF16), d_rows)
            acc[pl.ds(2 * u, 2)] += grad.reshape(2, LANES, LANES)
            return dq + dot(two(kvt, 2 * u)[:HD], grad_scores)

        dq = lax.fori_loop(0, diagonal - lowest + 1, k_block, jnp.zeros((HD, BLOCK), F32))
        for side in range(2):
            lanes = slice(side * LANES, (side + 1) * LANES)
            dqt_ref[2 * m + side] = (dq[:, lanes] * 0.125).astype(BF16)
        return carry

    lax.fori_loop(0, GROUP // 2, q_block, 0)

    def put(c, carry):
        dkv_ref[c] = acc[c].astype(BF16)
        return carry

    lax.fori_loop(0, span, put, 0)


def finish_kernel(
    blocks,
    parts,
    window,
    places,
    dqt_ref,
    dkv_ref,
    x_ref,
    gres_ref,
    win_ref,
    rows_ref,
    up_row_ref,
    p_out,
    p_up,
    p_down,
    gx_ref,
    r_win,
    r_out,
    r_up,
    r_down,
    r_aux,
    p_win,
    p_aux,
    dq_in,
    dkv_in,
    halo_in,
    dkv_sum,
    gp,
    *more,
):
    place = Place(blocks)
    greet(place, parts, True)
    depth = place.depth
    count = 9
    trees = []
    for number, (part, out) in enumerate(
        ((p_out, r_out), (p_up, r_up), (p_down, r_down), (p_win, r_win), (p_aux, r_aux))
    ):
        trees.append(Reduce(place, part, out, *more[number * count : (number + 1) * count]))
    t_out, t_up, t_down, t_win, t_aux = trees
    q_s, q_r, k_s, k_r, halo_s, halo_r = more[5 * count :]
    early = (t_out, t_up, t_down)
    for tree in early:
        tree.start_core()

    def halo_copy(part):
        return remote(
            dkv_ref.at[pl.ds(0, window)],
            halo_in,
            halo_s.at[0],
            halo_r.at[0],
            place.member(place.slot, part),
        )

    if parts > 1:

        @pl.when(place.part > 0)
        def _():
            halo_copy(place.part - 1).start()

    def q_copy(offset, come):
        landing = place.other_slot(-offset) if come else place.slot
        target = place.other_slot(offset)
        return remote(
            dqt_ref.at[target], dq_in.at[landing], q_s.at[offset], q_r.at[offset], place.member(target)
        )

    def k_copy(offset, come):
        landing = place.other_slot(-offset) if come else place.slot
        target = place.other_slot(offset)
        return remote(
            dkv_sum.at[target],
            dkv_in.at[landing],
            k_s.at[offset],
            k_r.at[offset],
            place.member(target),
        )

    def loop(call):
        def step(offset, carry):
            call(offset)
            return carry

        lax.fori_loop(1, GROUP, step, 0)

    loop(lambda offset: q_copy(offset, False).start())
    dq_in[place.slot] = dqt_ref[place.slot]
    dkv_sum[...] = dkv_ref[pl.ds(window, GROUP)]
    if window < GROUP:

        def early_k(offset):
            @pl.when(place.other_slot(offset) < GROUP - window)
            def _():
                k_copy(offset, False).start()

        loop(early_k)

    for tree in early:
        tree.start_second()

    if parts > 1:

        @pl.when(place.part < parts - 1)
        def _():
            halo_copy(place.part + 1).wait_recv()

            def add(entry, carry):
                here = GROUP - window + entry
                dkv_sum[here] = (
                    dkv_sum[here].astype(F32) + halo_in[entry].astype(F32)
                ).astype(BF16)
                return carry

            lax.fori_loop(0, window, add, 0)

    def late_k(offset):
        @pl.when(place.other_slot(offset) >= GROUP - window)
        def _():
            k_copy(offset, False).start()

    loop(late_k)
    dkv_in[place.slot] = dkv_sum[place.slot]

    for tree in early:
        tree.start_first()

    loop(lambda offset: q_copy(offset, True).wait_recv())
    loop(lambda offset: k_copy(offset, True).wait_recv())

    width = x_ref.shape[-1]
    low_lane = iota((LANES, LANES), 1) < HD
    for s in range(2):
        rows = slice(s * LANES, (s + 1) * LANES)
        turned = dq_in[pl.ds(s * HEADS, HEADS)].reshape(width, LANES).astype(F32)
        gp[rows, 0:width] = turned.T.astype(BF16)
        for pair in range(HEADS // 2):
            even = dkv_in[s * HEADS + 2 * pair].astype(F32)
            odd = dkv_in[s * HEADS + 2 * pair + 1].astype(F32)
            keys = jnp.where(low_lane, even, pltpu.roll(odd, HD, 1))
            values = jnp.where(low_lane, pltpu.roll(even, HD, 1), odd)
            at = pair * LANES
            gp[rows, width + at : width + at + LANES] = keys.astype(BF16)
            gp[rows, 2 * width + at : 2 * width + at + LANES] = values.astype(BF16)

    tokens = x_ref[...].reshape(2 * LANES, width)
    tokens_turned = tokens.T
    wide = 512
    for t in range(3 * width // wide):
        cols = slice(t * wide, (t + 1) * wide)
        part = dot(tokens_turned, gp[:, cols]).astype(BF16)
        p_win[:, :, :, :, :, cols] = part.reshape(2, 2, depth, 2, width // (8 * depth), wide)
    t_win.start_core()

    devices = 8 * depth
    query_row = jnp.sum(gp[:, 0:width].astype(F32), axis=0, keepdims=True)
    value_row = jnp.sum(gp[:, 2 * width :].astype(F32), axis=0, keepdims=True)
    folded = (
        fold_bias(query_row, devices * 8, *places["query"])
        + fold_bias(value_row, devices * 8, *places["value"])
        + fold_bias(rows_ref[1:2], devices * 8, *places["output"])
        + fold_bias(rows_ref[0:1], devices * 8, *places["down"])
        + fold_bias(up_row_ref[0:1], devices * 8, *places["up"])
    )
    scalars = rows_ref[2:3, 0:LANES]
    folded = folded + jnp.where((iota((devices * 8, LANES), 0) & 7) == 1, scalars, 0.0)
    p_aux[...] = folded.reshape(2, 2, depth, 2, 8, LANES)
    t_aux.start_core()

    gx = gres_ref[...]
    for t in range(3 * width // wide):
        cols = slice(t * wide, (t + 1) * wide)
        gx = gx + dot_nt(gp[:, cols], win_ref[:, cols])
    gx_ref[...] = gx.astype(BF16).reshape(2, LANES, width)

    t_win.start_second()
    t_aux.start_second()
    for tree in early:
        tree.start_line()
    t_win.start_first()
    t_aux.start_first()
    t_win.start_line()
    t_aux.start_line()
    for tree in trees:
        tree.finish()

    loop(lambda offset: q_copy(offset, False).wait_send())
    loop(lambda offset: k_copy(offset, False).wait_send())
    if parts > 1:

        @pl.when(place.part > 0)
        def _():
            halo_copy(place.part - 1).wait_send()

    for tree in trees:
        tree.drain()


def call(kernel, out_shape, in_specs, out_specs, scratch, collective=None):
    return pl.pallas_call(
        kernel,
        out_shape=out_shape,
        in_specs=in_specs,
        out_specs=out_specs,
        scratch_shapes=scratch,
        compiler_params=pltpu.CompilerParams(
            collective_id=collective,
            has_side_effects=collective is not None,
            vmem_limit_bytes=VMEM_BYTES,
        ),
    )


def local(
    layer_input,
    segments,
    input_weight,
    output_weight,
    up_weight,
    down_weight,
    query_bias,
    value_bias,
    output_bias,
    up_bias,
    down_bias,
    alphas,
    out_grad,
):
    heads, blocks = lax.axis_size("head"), lax.axis_size("blk")
    depth, devices = blocks // 2, heads * blocks
    seqs, rows, width = layer_input.shape
    hidden = up_weight.shape[1]
    seq_len = rows * devices
    assert heads == 4 and seqs * HEADS == GROUP and rows == LANES
    longest = 16 * math.isqrt(seq_len)
    window, parts = longest // rows, devices // GROUP
    docs = 2 * seq_len // longest
    assert window <= GROUP and window % 2 == 0
    span = window + GROUP
    places = bias_places(devices, width, hidden)

    def shape(*dims, dtype=BF16):
        return jax.ShapeDtypeStruct(dims, dtype)

    vmem, smem, anywhere = (
        pl.BlockSpec(memory_space=VMEM),
        pl.BlockSpec(memory_space=pltpu.SMEM),
        pl.BlockSpec(memory_space=pl.ANY),
    )
    dma = pltpu.SemaphoreType.DMA

    aux = jnp.concatenate(
        [query_bias, value_bias, output_bias, down_bias, up_bias]
    ).astype(F32)
    aux = jnp.broadcast_to(jnp.pad(aux, (0, LANES - aux.shape[0]))[None], (8, LANES))
    lead = (2, 2, depth, 2)
    in_rows, up_rows = input_weight.shape[0], down_weight.shape[0]
    sems = Gather.semaphores(depth)
    queries, pairs, starts, g_win, g_wo, g_wup, g_wdown, g_aux = call(
        functools.partial(project_kernel, blocks, parts, window, docs, places),
        (
            shape(GROUP, HD, LANES),
            shape(span, LANES, LANES),
            shape(GROUP, LANES, dtype=jnp.int32),
            shape(*lead, in_rows, 3 * width),
            shape(*lead, in_rows, width),
            shape(*lead, in_rows, hidden),
            shape(*lead, up_rows, width),
            shape(*lead, 8, LANES, dtype=F32),
        ),
        [vmem] * 7,
        (vmem, vmem, vmem, vmem, anywhere, anywhere, anywhere, vmem),
        [
            VMEM((span, 16, LANES), BF16),
            VMEM((16, LANES), BF16),
            VMEM((GROUP, HD, LANES), BF16),
            VMEM((GROUP, LANES, LANES), BF16),
        ]
        + [dma((sems,))] * 10
        + [dma((GROUP,))] * 6
        + [dma((window + 1,))] * 2
        + [dma((5,))],
        collective=0,
    )(layer_input, segments, aux, input_weight, output_weight, up_weight, down_weight)

    attended, attended_wide, lse = call(
        functools.partial(attend_kernel, window),
        (
            shape(GROUP, HD, LANES),
            shape(GROUP, HD, LANES, dtype=F32),
            shape(GROUP, LANES, dtype=F32),
        ),
        [vmem, vmem, vmem, smem],
        (vmem, vmem, vmem),
        [VMEM((span, LANES, LANES), BF16)],
    )(queries, pairs, starts, starts)

    full_in = g_win.reshape(width, 3 * width)
    full_out = g_wo.reshape(width, width)
    full_up = g_wup.reshape(width, hidden)
    full_down = g_wdown.reshape(hidden, width)
    flat_aux = g_aux.reshape(devices * 8, LANES)
    layer_output, grad_attended, grad_res, p_up, p_down, p_out, bias_rows, up_row = call(
        functools.partial(middle_kernel, blocks, parts, places),
        (
            shape(seqs, rows, width),
            shape(GROUP, HD, LANES),
            shape(seqs * rows, width, dtype=F32),
            shape(width, hidden),
            shape(hidden, width),
            shape(width, width),
            shape(8, width, dtype=F32),
            shape(8, hidden, dtype=F32),
        ),
        [vmem, vmem, vmem, smem, vmem, vmem, vmem, vmem],
        (vmem,) * 8,
        [
            VMEM((GROUP, HD, LANES), BF16),
            VMEM((GROUP, HD, LANES), BF16),
            VMEM((seqs * rows, hidden), BF16),
            VMEM((seqs * rows, hidden), BF16),
        ]
        + [dma((GROUP,))] * 4,
        collective=1,
    )(attended, layer_input, out_grad, alphas, full_out, full_up, full_down, flat_aux)

    grad_queries, grad_pairs = call(
        functools.partial(attend_back_kernel, window),
        (shape(GROUP, HD, LANES), shape(span, LANES, LANES)),
        [vmem, vmem, vmem, smem, vmem, vmem, vmem],
        (vmem, vmem),
        [VMEM((span, LANES, LANES), BF16), VMEM((span, LANES, LANES), F32)],
    )(queries, pairs, starts, starts, attended_wide, lse, grad_attended)

    reduced = (
        (in_rows, width, BF16),
        (in_rows, hidden, BF16),
        (up_rows, width, BF16),
        (in_rows, 3 * width, BF16),
        (8, LANES, F32),
    )
    scratch = [
        VMEM((*lead, in_rows, 3 * width), BF16),
        VMEM((*lead, 8, LANES), F32),
        VMEM((GROUP, HD, LANES), BF16),
        VMEM((GROUP, LANES, LANES), BF16),
        VMEM((window, LANES, LANES), BF16),
        VMEM((GROUP, LANES, LANES), BF16),
        VMEM((seqs * rows, 3 * width), BF16),
    ]
    for sizes in reduced:
        scratch += Reduce.scratch(depth, *sizes)
    scratch += [dma((GROUP,))] * 4 + [dma((1,))] * 2
    input_grad, win_grad, out_weight_grad, up_grad, down_grad, sums = call(
        functools.partial(finish_kernel, blocks, parts, window, places),
        (
            shape(seqs, rows, width),
            shape(in_rows, 3 * width, dtype=F32),
            shape(in_rows, width, dtype=F32),
            shape(in_rows, hidden, dtype=F32),
            shape(up_rows, width, dtype=F32),
            shape(8, LANES, dtype=F32),
        ),
        [vmem] * 10,
        (vmem,) * 6,
        scratch,
        collective=2,
    )(
        grad_queries,
        grad_pairs,
        layer_input,
        grad_res,
        full_in,
        bias_rows,
        up_row,
        p_out.reshape(*lead, in_rows, width),
        p_up.reshape(*lead, in_rows, hidden),
        p_down.reshape(*lead, up_rows, width),
    )

    def bias_grad(name):
        offset, per = places[name]
        return sums[0, offset : offset + per]

    rms_values = jnp.sqrt(sums[1, 0:3] / (seqs * seq_len * width))
    return (
        layer_output,
        input_grad,
        win_grad,
        out_weight_grad,
        up_grad,
        down_grad,
        bias_grad("query"),
        bias_grad("value"),
        bias_grad("output"),
        bias_grad("up"),
        bias_grad("down"),
        sums[1, 3:5],
        rms_values,
    )


def solution(mesh):
    tokens = P(None, ("head", "blk"), None)
    rows, flat = P(("head", "blk"), None), P(("head", "blk"))
    return jax.shard_map(
        local,
        mesh=mesh,
        in_specs=(
            tokens,
            P(None, ("head", "blk")),
            rows,
            rows,
            rows,
            rows,
            flat,
            flat,
            flat,
            flat,
            flat,
            P(),
            tokens,
        ),
        out_specs=(
            tokens,
            tokens,
            rows,
            rows,
            rows,
            rows,
            flat,
            flat,
            flat,
            flat,
            flat,
            P(),
            P(),
        ),
        check_vma=False,
    )
```

time: 1100 us -> 189 us (0.17)
  waiting for transfers between devices: 587 us -> 0 us
  blocking collectives: 230 us -> 0 us
  Pallas kernels: 0 us -> 170 us
  matrix products: 146 us -> 0 us
  other arithmetic: 57.5 us -> 1.2 us
  local copies, waits for them, and re-layouts: 44.4 us -> 16.4 us
  between operations: 14.7 us -> 0.68 us
  starting transfers between devices: 13.1 us -> 0 us
    reduce_scatter x3 -> x0, waiting for transfers between devices: 290 us -> none  [the longest x1 146 us: local(): lax.psum_scatter(up_grad, ('head', 'blk'), scatter_dimension=0, tiled=True)]
    ppermute x23 -> x0, waiting for transfers between devices: 243 us -> none  [from_behind(): return lax.ppermute(block, axis, route)]
    pallas_call x0 -> x5, Pallas kernels: none -> 170 us  [the longest x1 59.9 us: local(): call(functools.partial(finish_kernel, blocks, parts, window, places), (sh...]
    dot_general x68 -> x0, matrix products: 146 us -> none  [the longest x8 30.2 us: backward_turn(): jnp.einsum('shqk,sqhd->skhd', probs, grad_attended_wide, preferred_elemen...]
    all_gather x2 -> x0, blocking collectives: 134 us -> none  [the longest x1 67.5 us: local(): lax.all_gather(output_weight, ('head', 'blk'), axis=0, tiled=True)]
    unnamed x2 -> x0, blocking collectives: 81 us -> none
    unnamed x8 -> x0, waiting for transfers between devices: 44.1 us -> none
    convert_element_type x23 -> x0, other arithmetic: 28.1 us -> none  [the longest x8 17.9 us: backward_hop(): from_behind(pair_grads.astype(jnp.bfloat16), 'blk', 1)]
  transfers between devices with their start and end apart: 33 -> 0, of which waited for: 28 -> 0; matrix products, arithmetic and copies ran while one was open for 21% -> 0% of each run, Pallas kernels for 0% -> 0%
where the time goes in v1:
time: 189 us; the launch traced here: 188 us
  Pallas kernels  170 us (90%)
  local copies, waits for them, and re-layouts  16.4 us (9%)
    pallas_call x1, Pallas kernels, local(): call(functools.partial(finish_kernel, blocks, parts, window, places), (sh...  59.9 us
    pallas_call x1, Pallas kernels, local(): call(functools.partial(project_kernel, blocks, parts, window, docs, place...  58.8 us
    pallas_call x1, Pallas kernels, local(): call(functools.partial(middle_kernel, blocks, parts, places), (shape(seqs...  28.8 us
    pallas_call x1, Pallas kernels, local(): call(functools.partial(attend_back_kernel, window), (shape(GROUP, HD, LAN...  11.5 us
    pallas_call x1, Pallas kernels, local(): call(functools.partial(attend_kernel, window), (shape(GROUP, HD, LANES),...  10.6 us
    unnamed x8, local copies, waits for them, and re-layouts  8.42 us

profile of v1, /device:TPU:0, one launch (start us, length us, event | category | flops | bytes accessed | tf_op | source)
XLA Modules:
  0.0 187.8 jit_solution(12852285892054210197)
XLA Ops:
  0.6 3.4 %concatenate.7 = bf16[128]{0:T(256)(128)(2,1)S(1)} concatenate(bf16[16]{0:T(256)(128)(2,1)} %param.19, bf16[16]{0:T(256)(128)(2,1)} %param.20, bf16[16]{0:T(256)(128)(2,1)} %param.21, bf16[16]{0:T(256)(128)(2,1)} %param.23, bf16[64]{0:T(256)(128)(2,1)} %param.22), dimensions={0} | concatenate | bytes 512 | tf_op jit(solution)/shard_map/concatenate | solution.py:1203
  4.1 0.6 broadcast_in_dim.2.aux_ref
  4.7 58.8 %shard_map.228 = (bf16[16,64,128]{2,1,0:T(8,128)(2,1)}, bf16[24,128,128]{2,1,0:T(8,128)(2,1)}, s32[16,128]{1,0:T(8,128)}, bf16[2,2,4,2,16,1536]{5,4,3,2,1,0:T(8,...) custom-call(bf16[2,128,512]{2,1,0:T(8,128)(2,1)} %x_ref.5, ...), custom_call_target="tpu_custom_call" | custom-call | tf_op jit(solution)/shard_map/pallas_call | solution.py:1210
  63.5 10.6 %shard_map.229 = (bf16[16,64,128]{2,1,0:T(8,128)(2,1)}, f32[16,64,128]{2,1,0:T(8,128)}, f32[16,128]{1,0:T(8,128)}) custom-call(bf16[16,64,128]{2,1,0:T(8,128)(2,1)} %get-tuple-element.40.qt_ref, bf16[24,128,128]{2,1,0:T(8,128)(2,1)} %get-tuple-element.41.kv_ref, s32[16,128]{1,0:T(8,128)} %get-tuple-element.42.starts_ref.first_ref, ...), custom_call_target="tpu_custom_call" | custom-call | tf_op jit(solution)/shard_map/pallas_call | solution.py:1237
  74.1 28.8 %shard_map.230 = (bf16[2,128,512]{2,1,0:T(8,128)(2,1)}, bf16[16,64,128]{2,1,0:T(8,128)(2,1)}, f32[256,512]{1,0:T(8,128)}, bf16[512,2048]{1,0:T(8,128)(2,1)}, bf1...) custom-call(bf16[16,64,128]{2,1,0:T(8,128)(2,1)} %get-tuple-element.43.ot_ref, ...), custom_call_target="tpu_custom_call" | custom-call | tf_op jit(solution)/shard_map/pallas_call | solution.py:1254
  102.9 11.5 %shard_map.231 = (bf16[16,64,128]{2,1,0:T(8,128)(2,1)}, bf16[24,128,128]{2,1,0:T(8,128)(2,1)}) custom-call(bf16[16,64,128]{2,1,0:T(8,128)(2,1)} %get-tuple-element.40.qt_ref, bf16[24,128,128]{2,1,0:T(8,128)(2,1)} %get-tuple-element.41.kv_ref, s32[16,128]{1,0:T(8,128)} %get-tuple-element.42.starts_ref.first_ref, ...), custom_call_target="tpu_custom_call" | custom-call | tf_op jit(solution)/shard_map/pallas_call | solution.py:1278
  114.4 0.0 copy-start
  114.4 59.9 %shard_map.232 = (bf16[2,128,512]{2,1,0:T(8,128)(2,1)}, f32[16,1536]{1,0:T(8,128)}, f32[16,512]{1,0:T(8,128)}, f32[16,2048]{1,0:T(8,128)}, f32[64,512]{1,0:T(8,128)}, /*index=5*/f32[8,128]{1,0:T(8,128)}) custom-call(bf16[16,64,128]{2,1,0:T(8,128)(2,1)} %get-tuple-element.52.dqt_ref, bf16[24,128,128]{2,1,0:T(8,128)(2,1)} %get-tuple-element.53.dkv_ref, ...), custom_call_target="tpu_custom_call" | custom-call | tf_op jit(solution)/shard_map/pallas_call | solution.py:1305
  174.3 1.3 slice_bitcast_fusion.2
  175.5 1.2 sqrt_bitcast_fusion
  176.7 1.3 slice_bitcast_fusion
  178.0 1.4 slice_bitcast_fusion.1
  179.4 0.0 copy-done
  179.4 0.7 copy.32
  180.1 1.7 copy.33
  181.8 1.5 copy.34
  183.3 1.4 copy.35
  184.7 1.6 copy.36
  186.2 1.6 copy.37
Async XLA Ops:
  114.4 65.0 %copy-start = (bf16[2,128,512]{2,1,0:T(8,128)(2,1)S(1)}, bf16[2,128,512]{2,1,0:T(8,128)(2,1)}, u32[]{:S(2)}) copy-start(bf16[2,128,512]{2,1,0:T(8,128)(2,1)} %get-tuple-element.84) | copy-start | bytes 786436

commit v2 on v1

v2 whole, which is shorter than its diff:
```python
import functools
import math

import jax
import jax.numpy as jnp
from jax import lax
from jax.experimental import pallas as pl
from jax.experimental.pallas import tpu as pltpu
from jax.sharding import PartitionSpec as P

HEADS = 8
HD = 64
LANES = 128
GROUP = 16
BLOCK = 256
VMEM_BYTES = 60 * 1024 * 1024
F32 = jnp.float32
BF16 = jnp.bfloat16
VMEM = pltpu.VMEM
NEG = -1e30


class Place:
    def __init__(self, blocks):
        self.blocks = blocks
        self.depth = blocks // 2
        head = lax.axis_index("head")
        block = lax.axis_index("blk")
        self.x, self.core = lax.div(head, 2), lax.rem(head, 2)
        self.z, self.y = lax.div(block, 2), lax.rem(block, 2)
        flat = head * blocks + block
        self.part, self.slot = lax.div(flat, GROUP), lax.rem(flat, GROUP)

    def at(self, x=None, core=None, z=None, y=None):
        x = self.x if x is None else x
        core = self.core if core is None else core
        z = self.z if z is None else z
        y = self.y if y is None else y
        return (x * 2 + core, z * 2 + y)

    def deeper(self, offset):
        return lax.rem(self.z + offset + self.depth, self.depth)

    def member(self, slot, part=None):
        part = self.part if part is None else part
        flat = part * GROUP + slot
        return (lax.div(flat, self.blocks), lax.rem(flat, self.blocks))

    def other_slot(self, offset):
        return lax.rem(self.slot + offset + GROUP, GROUP)


def remote(src, dst, send, recv, device):
    return pltpu.make_async_remote_copy(
        src_ref=src,
        dst_ref=dst,
        send_sem=send,
        recv_sem=recv,
        device_id=device,
        device_id_type=pl.DeviceIdType.MESH,
    )


def greet(place, parts, tree):
    barrier = pltpu.get_barrier_semaphore()

    def hello(device):
        pl.semaphore_signal(barrier, inc=1, device_id=device, device_id_type=pl.DeviceIdType.MESH)

    def group(offset, carry):
        hello(place.member(place.other_slot(offset)))
        return carry

    lax.fori_loop(1, GROUP, group, 0)
    total = GROUP - 1
    if tree:

        def line(offset, carry):
            hello(place.at(z=place.deeper(offset)))
            return carry

        lax.fori_loop(1, place.depth, line, 0)
        hello(place.at(x=1 - place.x))
        hello(place.at(y=1 - place.y))
        hello(place.at(core=1 - place.core))
        total += place.depth + 2
    if parts > 1 and tree:

        @pl.when(place.part > 0)
        def _():
            hello(place.member(place.slot, place.part - 1))

        @pl.when(place.part < parts - 1)
        def _():
            hello(place.member(place.slot, place.part + 1))

        total += jnp.where(place.part > 0, 1, 0) + jnp.where(place.part < parts - 1, 1, 0)
    pl.semaphore_wait(barrier, total)


def halves_of(columns):
    if columns < 2 * LANES:
        return ((0, columns, "yx"),)
    return ((0, columns // 2, "yx"), (columns // 2, columns // 2, "xy"))


class Gather:
    def __init__(self, place, src, dst, send, recv, local, cols=None):
        self.place, self.src, self.dst = place, src, dst
        self.send, self.recv, self.local = send, recv, local
        self.start, self.width = cols or (0, dst.shape[-1])
        self.halves = halves_of(self.width)
        self.lines = place.depth - 1

    @staticmethod
    def semaphores(depth):
        return depth + 8

    def cut(self, half, *index):
        start, width, _ = half
        return self.dst.at[index + (slice(None), pl.ds(self.start + start, width))]

    def shard(self):
        return self.src.at[:, pl.ds(self.start, self.width)]

    def whole(self, *index):
        return self.dst.at[index + (slice(None), pl.ds(self.start, self.width))]

    def pair(self, half, first, x, y):
        place, every = self.place, slice(None)
        if first:
            return self.cut(half, x, place.core, every, y)
        if half[2] == "yx":
            return self.cut(half, x, place.core, every, every)
        return self.cut(half, every, place.core, every, y)

    def across(self, half, first):
        place = self.place
        if (half[2] == "yx") == first:
            return place.x, 1 - place.y
        return 1 - place.x, place.y

    def line(self, offset, come):
        place = self.place
        z = place.deeper(-offset) if come else place.z
        return remote(
            self.shard(),
            self.whole(place.x, place.core, z, place.y),
            self.send.at[offset - 1],
            self.recv.at[offset - 1],
            place.at(z=place.deeper(offset)),
        )

    def own(self):
        place = self.place
        return pltpu.make_async_copy(
            self.shard(), self.whole(place.x, place.core, place.z, place.y), self.local
        )

    def exchange(self, number, first, come):
        half = self.halves[number]
        place = self.place
        x, y = self.across(half, first)
        slot = self.lines + (0 if first else 2) + number
        mine = self.pair(half, first, place.x, place.y)
        landing = self.pair(half, first, x, y) if come else mine
        return remote(
            mine, landing, self.send.at[slot], self.recv.at[slot], place.at(x=x, y=y)
        )

    def hand(self, which, come):
        place, every = self.place, slice(None)
        slot = self.lines + 4 + which
        core = 1 - place.core if come else place.core

        def region(core):
            if which == 0:
                return self.whole(place.x, core, every, place.y)
            number = (which - 1) % 2
            half = self.halves[number]
            first = which < 3
            x, y = self.across(half, first)
            if first:
                return self.cut(half, x, core, every, y)
            if half[2] == "yx":
                return self.cut(half, x, core, every, every)
            return self.cut(half, every, core, every, y)

        return remote(
            region(place.core),
            region(core),
            self.send.at[slot],
            self.recv.at[slot],
            place.at(core=1 - place.core),
        )

    def start_line(self):
        for offset in range(1, self.lines + 1):
            self.line(offset, False).start()
        self.own().start()

    def start_first(self):
        self.own().wait()
        for offset in range(1, self.lines + 1):
            self.line(offset, True).wait_recv()
        for number in range(len(self.halves)):
            self.exchange(number, True, False).start()
        self.hand(0, False).start()

    def start_second(self):
        for number in range(len(self.halves)):
            self.exchange(number, True, True).wait_recv()
            self.exchange(number, False, False).start()
            self.hand(1 + number, False).start()

    def start_last(self):
        for number in range(len(self.halves)):
            self.exchange(number, False, True).wait_recv()
            self.hand(3 + number, False).start()

    def hands(self):
        for number in range(len(self.halves)):
            yield 1 + number
            yield 3 + number

    def finish(self):
        self.hand(0, True).wait_recv()
        for which in self.hands():
            self.hand(which, True).wait_recv()

    def drain(self):
        for offset in range(1, self.lines + 1):
            self.line(offset, False).wait_send()
        for number in range(len(self.halves)):
            self.exchange(number, True, False).wait_send()
            self.exchange(number, False, False).wait_send()
        self.hand(0, False).wait_send()
        for which in self.hands():
            self.hand(which, False).wait_send()


class Reduce:
    def __init__(self, place, part, out, rc, total, ra, rb, fa, fb, rz, send, recv):
        self.place, self.part, self.out = place, part, out
        self.rc, self.total, self.rz = rc, total, rz
        self.second, self.first = (ra, rb), (fa, fb)
        self.send, self.recv = send, recv
        self.halves = halves_of(part.shape[-1])
        self.lines = place.depth - 1

    @staticmethod
    def semaphores(depth):
        return depth + 4

    @staticmethod
    def scratch(depth, rows, cols, dtype):
        wide = halves_of(cols)[0][1]
        return [
            VMEM((2, depth, 2, rows, cols), dtype),
            VMEM((2, depth, 2, rows, cols), dtype),
            VMEM((depth, 2, rows, wide), dtype),
            VMEM((2, depth, rows, wide), dtype),
            VMEM((depth, rows, wide), dtype),
            VMEM((depth, rows, wide), dtype),
            VMEM((depth - 1, rows, cols), dtype),
            pltpu.SemaphoreType.DMA((Reduce.semaphores(depth),)),
            pltpu.SemaphoreType.DMA((Reduce.semaphores(depth),)),
        ]

    def core(self):
        place, every = self.place, slice(None)
        return remote(
            self.part.at[every, 1 - place.core],
            self.rc,
            self.send.at[0],
            self.recv.at[0],
            place.at(core=1 - place.core),
        )

    def cut(self, half, *index):
        start, width, _ = half
        return index + (slice(None), pl.ds(start, width))

    def exchange(self, number, second):
        place, every = self.place, slice(None)
        half = self.halves[number]
        slot = (1 if second else 3) + number
        over_x = (half[2] == "yx") == second
        device = place.at(x=1 - place.x) if over_x else place.at(y=1 - place.y)
        if second:
            index = (1 - place.x, every, every) if over_x else (every, every, 1 - place.y)
            landing = self.second[number]
        else:
            index = (1 - place.x, every, place.y) if over_x else (place.x, every, 1 - place.y)
            landing = self.first[number]
        return remote(
            self.total.at[self.cut(half, *index)],
            landing,
            self.send.at[slot],
            self.recv.at[slot],
            device,
        )

    def line(self, offset):
        place = self.place
        return remote(
            self.total.at[place.x, place.deeper(offset), place.y],
            self.rz.at[offset - 1],
            self.send.at[4 + offset],
            self.recv.at[4 + offset],
            place.at(z=place.deeper(offset)),
        )

    def start_core(self):
        self.core().start()

    def start_second(self):
        place = self.place
        self.core().wait_recv()
        dtype = self.total.dtype

        def add(z, carry):
            for x in range(2):
                for y in range(2):
                    self.total[x, z, y] = (
                        self.part[x, place.core, z, y].astype(F32) + self.rc[x, z, y].astype(F32)
                    ).astype(dtype)
            return carry

        lax.fori_loop(0, place.depth, add, 0)
        for number in range(len(self.halves)):
            self.exchange(number, True).start()

    def accumulate(self, index, value):
        self.total[index] = (self.total[index].astype(F32) + value.astype(F32)).astype(
            self.total.dtype
        )

    def start_first(self):
        place = self.place
        for number, half in enumerate(self.halves):
            self.exchange(number, True).wait_recv()
            landed = self.second[number]

            def add(z, carry):
                for other in range(2):
                    if half[2] == "yx":
                        self.accumulate(self.cut(half, place.x, z, other), landed[z, other])
                    else:
                        self.accumulate(self.cut(half, other, z, place.y), landed[other, z])
                return carry

            lax.fori_loop(0, place.depth, add, 0)
            self.exchange(number, False).start()

    def start_line(self):
        place = self.place
        for number, half in enumerate(self.halves):
            self.exchange(number, False).wait_recv()
            landed = self.first[number]

            def add(z, carry):
                self.accumulate(self.cut(half, place.x, z, place.y), landed[z])
                return carry

            lax.fori_loop(0, place.depth, add, 0)
        for offset in range(1, self.lines + 1):
            self.line(offset).start()

    def finish(self):
        place = self.place
        for offset in range(1, self.lines + 1):
            self.line(offset).wait_recv()
        result = self.total[place.x, place.z, place.y].astype(F32)
        for offset in range(1, self.lines + 1):
            result = result + self.rz[offset - 1].astype(F32)
        self.out[...] = result

    def drain(self):
        self.core().wait_send()
        for number in range(len(self.halves)):
            self.exchange(number, True).wait_send()
            self.exchange(number, False).wait_send()
        for offset in range(1, self.lines + 1):
            self.line(offset).wait_send()


def iota(shape, dim):
    return lax.broadcasted_iota(jnp.int32, shape, dim)


def dot(left, right):
    return lax.dot_general(left, right, (((1,), (0,)), ((), ())), preferred_element_type=F32)


def dot_nt(left, right):
    return lax.dot_general(left, right, (((1,), (1,)), ((), ())), preferred_element_type=F32)


def dot_tn(left, right):
    return lax.dot_general(left, right, (((0,), (0,)), ((), ())), preferred_element_type=F32)


def shift_of(size):
    assert size & (size - 1) == 0
    return size.bit_length() - 1


BIASES = ("query", "value", "output", "down", "up")
SCALARS = len(BIASES)


def spread_bias(gathered, name, per, total):
    rows = gathered.shape[0]
    pick = iota((LANES, total), 0) == (iota((LANES, total), 1) & (per - 1))
    spread = dot(gathered.astype(BF16), pick.astype(BF16))
    owner = jnp.right_shift(iota((rows, total), 1), shift_of(per)) * 8 + BIASES.index(name)
    return jnp.sum(jnp.where(iota((rows, total), 0) == owner, spread, 0.0), axis=0, keepdims=True)


def fold_bias(row, rows, name, per):
    total = row.shape[1]
    owner = jnp.right_shift(iota((rows, total), 1), shift_of(per)) * 8 + BIASES.index(name)
    chosen = jnp.where(iota((rows, total), 0) == owner, row, 0.0)
    put = iota((total, LANES), 1) == (iota((total, LANES), 0) & (per - 1))
    return lax.dot_general(
        chosen,
        put.astype(F32),
        (((1,), (0,)), ((), ())),
        precision=lax.Precision.HIGHEST,
        preferred_element_type=F32,
    )


def layer_kernel(
    blocks,
    parts,
    window,
    docs,
    x_ref,
    seg_ref,
    win_ref,
    wo_ref,
    wup_ref,
    wdown_ref,
    bias_refs,
    alphas_ref,
    grad_ref,
    out_ref,
    gx_ref,
    r_win,
    r_out,
    r_up,
    r_down,
    r_aux,
    gathered,
    gather_sems,
    local,
    trees,
    exchange_sems,
    halo_sems,
    segs,
    tile,
    aux_ref,
    qs,
    ks,
    qt_ref,
    kv_ref,
    kvt,
    starts_ref,
    ot_ref,
    of_ref,
    lse_ref,
    mixed_t,
    dos,
    doct_ref,
    act_s,
    gpre_s,
    gres_ref,
    acc,
    dqt_ref,
    dkv_sum,
    dq_in,
    dkv_in,
    halo_out,
    halo_in,
    gp,
    partials,
):
    place = Place(blocks)
    depth, devices = place.depth, 4 * blocks
    gwin, gwo, gwup, gwdown, gaux = gathered
    p_win, p_out, p_up, p_down, p_aux = partials
    width, hidden = gwin.shape[-1] // 3, gwup.shape[-1]
    per, per_up = width // devices, hidden // devices
    span, pairs_of_chunks, reach = window + GROUP, GROUP // 2, window // 2
    free = pairs_of_chunks - reach

    def loop(call, low=1, high=GROUP):
        def step(number, carry):
            call(number)
            return carry

        lax.fori_loop(low, high, step, 0)

    def exchange(src, dst, number):
        send, recv = exchange_sems[2 * number : 2 * number + 2]

        def copy(offset, come):
            landing = place.other_slot(-offset) if come else place.slot
            target = place.other_slot(offset)
            return remote(
                src(target), dst(landing), send.at[offset], recv.at[offset], place.member(target)
            )

        return copy

    def entry(ref, base=0):
        return lambda index: ref.at[base + index]

    seg_copy = exchange(lambda target: tile, entry(segs, window), 0)
    k_copy = exchange(entry(ks), entry(kv_ref, window), 1)
    q_copy = exchange(entry(qs), entry(qt_ref), 2)
    o_copy = exchange(entry(ot_ref), entry(mixed_t), 3)
    d_copy = exchange(entry(dos), entry(doct_ref), 4)
    dq_copy = exchange(entry(dqt_ref), entry(dq_in), 5)
    dkv_copy = exchange(entry(dkv_sum), entry(dkv_in), 6)
    seg_hs, seg_hr, kv_hs, kv_hr, back_hs, back_hr = halo_sems

    def send_to(copy, target):
        offset = lax.rem(target - place.slot + GROUP, GROUP)

        @pl.when(offset != 0)
        def _():
            copy(offset, False).start()

    def await_from(copy, source):
        offset = lax.rem(place.slot - source + GROUP, GROUP)

        @pl.when(offset != 0)
        def _():
            copy(offset, True).wait_recv()

    greet(place, parts, True)

    row = iota((16, LANES), 0)
    numbers = seg_ref[...].astype(F32)
    tile[...] = jnp.where(row == 0, numbers[0:1], numbers[1:2]).astype(BF16)
    segs[window + place.slot] = tile[...]
    aux_ref[...] = jnp.zeros_like(aux_ref)
    for index, ref in enumerate(bias_refs):
        aux_ref[index : index + 1, 0 : ref.shape[-1]] = ref[...].astype(F32).reshape(1, ref.shape[-1])
    if window:

        @pl.when(place.part == 0)
        def _():
            kv_ref[pl.ds(0, window)] = jnp.zeros((window, LANES, LANES), BF16)

    plan = (
        (aux_ref, gaux, None),
        (win_ref, gwin, (width, 2 * width)),
        (win_ref, gwin, (0, width)),
        (wo_ref, gwo, None),
        (wup_ref, gwup, None),
        (wdown_ref, gwdown, None),
    )
    gathers = [
        Gather(place, src, dst, gather_sems[2 * i], gather_sems[2 * i + 1], local.at[i], cols)
        for i, (src, dst, cols) in enumerate(plan)
    ]
    first, rest = gathers[:3], gathers[3:]
    g_aux, g_kv, g_q = first
    for gather in first:
        gather.start_line()
    loop(lambda offset: seg_copy(offset, False).start())
    for gather in first:
        gather.start_first()
    for gather in rest:
        gather.start_line()
    for gather in first:
        gather.start_second()

    loop(lambda offset: seg_copy(offset, True).wait_recv())

    def seg_halo(part):
        return remote(
            segs.at[pl.ds(GROUP, window)],
            segs.at[pl.ds(0, window)],
            seg_hs.at[0],
            seg_hr.at[0],
            place.member(place.slot, part),
        )

    if parts > 1:

        @pl.when(place.part < parts - 1)
        def _():
            seg_halo(place.part + 1).start()

    for gather in first:
        gather.start_last()
    g_aux.finish()
    g_kv.finish()

    aux = gaux[...].reshape(devices * 8, LANES)
    bias_q = spread_bias(aux, "query", per, width)
    bias_v = spread_bias(aux, "value", per, width)
    tokens = x_ref[...].reshape(2 * LANES, width)
    low_lane = iota((LANES, LANES), 1) < HD
    wide = 2 * LANES

    def column(kind, t):
        weight = gwin[:, :, :, :, :, pl.ds(kind * width + t * wide, wide)]
        return dot(tokens, weight.reshape(width, wide))

    def corners(t):
        for s in range(2):
            for u in range(2):
                at = (slice(s * LANES, (s + 1) * LANES), slice(u * LANES, (u + 1) * LANES))
                yield s * HEADS + t * 4 + u * 2, at

    for t in range(width // wide):
        k = column(1, t).astype(BF16).astype(F32)
        v = (column(2, t) + bias_v[:, t * wide : (t + 1) * wide]).astype(BF16).astype(F32)
        for head, at in corners(t):
            k_at, v_at = k[at], v[at]
            ks[head] = jnp.where(low_lane, k_at, pltpu.roll(v_at, HD, 1)).astype(BF16)
            ks[head + 1] = jnp.where(low_lane, pltpu.roll(k_at, HD, 1), v_at).astype(BF16)
    loop(lambda offset: k_copy(offset, False).start())
    kv_ref[window + place.slot] = ks[place.slot]
    g_q.finish()
    for t in range(width // wide):
        q = (column(0, t) + bias_q[:, t * wide : (t + 1) * wide]).astype(BF16).astype(F32) * 0.125
        for head, at in corners(t):
            turned = q[at].T.astype(BF16)
            qs[head] = turned[:HD]
            qs[head + 1] = turned[HD:]
    loop(lambda offset: q_copy(offset, False).start())
    qt_ref[place.slot] = qs[place.slot]

    for gather in rest:
        gather.start_first()

    if parts > 1:

        @pl.when(place.part < parts - 1)
        def _():
            seg_halo(place.part + 1).wait_send()

        @pl.when(place.part > 0)
        def _():
            seg_halo(place.part - 1).wait_recv()

    sequence = lax.div(place.slot, HEADS)
    chosen = jnp.where(iota((span, 16, LANES), 1) == sequence, segs[...].astype(F32), 0.0)
    seen = jnp.sum(chosen, axis=1)
    outside = (iota((span, LANES), 0) < window) & (place.part == 0)
    seen = jnp.where(outside, -1.0, seen)
    own = seen[window:]
    start = jnp.zeros((GROUP, LANES), F32)
    for number in range(docs):
        count = jnp.sum(jnp.where(seen == number - 1, 1.0, 0.0), axis=0, keepdims=True)
        count = jnp.sum(count, axis=1, keepdims=True)
        start = start + jnp.where(own >= number, count, 0.0)
    starts_ref[...] = start.astype(jnp.int32)

    for gather in rest:
        gather.start_second()

    def kv_halo(number, part):
        return remote(
            kv_ref.at[GROUP + number],
            kv_ref.at[number],
            kv_hs.at[number],
            kv_hr.at[number],
            place.member(place.slot, part),
        )

    def arrived(source):
        kvt[window + source] = kv_ref[window + source].T
        if parts > 1:

            @pl.when((place.part < parts - 1) & (source >= GROUP - window))
            def _():
                kv_halo(source - (GROUP - window), place.part + 1).start()

    arrived(place.slot)

    def kv_wait(offset):
        k_copy(offset, True).wait_recv()
        arrived(place.other_slot(-offset))

    loop(kv_wait)
    loop(lambda offset: q_copy(offset, True).wait_recv())

    many = window + 2
    older = window * LANES

    def q_rows_of(ref, m):
        return jnp.concatenate([ref[pl.ds(2 * m, 1)], ref[pl.ds(2 * m + 1, 1)]], axis=1)

    def turned_window(m):
        return jnp.concatenate([kvt[2 * m + i] for i in range(many)], axis=1)

    def masked(scores, start, q_place, block, base):
        k_place = base + block * BLOCK + iota((BLOCK, BLOCK), 0)
        visible = k_place >= start
        if block == reach:
            visible = visible & (k_place <= q_place)
        return jnp.where(visible, scores, NEG)

    blank = jnp.zeros((HD, BLOCK), BF16)

    def attend(step, carry):
        for number, gather in enumerate(rest):

            @pl.when(step == 1 + 2 * number)
            def _():
                gather.start_last()

        if parts > 1:

            @pl.when((step == free) & (place.part > 0))
            def _():
                loop(lambda number: kv_halo(number, place.part - 1).wait_recv(), 0, window)

        @pl.when(step == free)
        def _():
            def turn(number):
                kvt[number] = kv_ref[number].T

            loop(turn, 0, window)

        turnover = place.slot
        late = lax.rem(step - free + GROUP + turnover, reach)
        if free:
            m = jnp.where(step < free, reach + lax.rem(step + turnover, free), late)
        else:
            m = late
        q_wide = jnp.concatenate([two(qt_ref, 2 * m), blank], axis=0)
        start = q_rows_of(starts_ref, m)
        base = m * BLOCK
        q_place = base + older + iota((1, BLOCK), 1)
        scores = [
            masked(
                dot(kv_ref[pl.ds(2 * (m + block), 2)].reshape(BLOCK, LANES), q_wide),
                start,
                q_place,
                block,
                base,
            )
            for block in range(reach + 1)
        ]
        peak = functools.reduce(jnp.maximum, scores)
        peak = jnp.max(peak, axis=0, keepdims=True)
        weights = [jnp.exp(score - peak) for score in scores]
        total = functools.reduce(jnp.add, weights)
        total = jnp.sum(total, axis=0, keepdims=True)
        weights = jnp.concatenate([weight.astype(BF16) for weight in weights], axis=0)
        out = dot(turned_window(m)[HD:], weights) / total
        lse = peak + jnp.log(total)
        for side in range(2):
            lanes = slice(side * LANES, (side + 1) * LANES)
            of_ref[2 * m + side] = out[:, lanes]
            ot_ref[2 * m + side] = out[:, lanes].astype(BF16)
            lse_ref[pl.ds(2 * m + side, 1)] = lse[:, lanes]
            send_to(o_copy, 2 * m + side)
        return carry

    lax.fori_loop(0, pairs_of_chunks, attend, 0)
    mixed_t[place.slot] = ot_ref[place.slot]

    a0, a1 = alphas_ref[0], alphas_ref[1]
    bias_out = spread_bias(aux, "output", per, width)
    bias_down = spread_bias(aux, "down", per, width)
    bias_up = spread_bias(aux, "up", per_up, hidden)
    rows = 2 * LANES
    wide_tokens = tokens.astype(F32)
    grads = grad_ref[...].reshape(rows, width).astype(F32)
    grad_ffn = (a1 * grads).astype(BF16)
    for gather in rest:
        gather.finish()
    full_out = gwo[...].reshape(width, width)

    loop(lambda offset: o_copy(offset, True).wait_recv())
    mixed_turned = mixed_t[...].reshape(2, width, LANES)
    mixed = jnp.concatenate([mixed_turned[0].T, mixed_turned[1].T], axis=0)
    branch = dot(mixed, full_out) + bias_out
    attn_term = a0 * branch
    residual = wide_tokens + attn_term
    hidden_in = residual.astype(BF16)

    ffn = jnp.zeros((rows, width), F32) + bias_down
    grad_res = grads
    tile_up = 512
    whole_up = gwup.reshape(width, hidden)
    whole_down = gwdown.reshape(hidden, width)
    for t in range(hidden // tile_up):
        cols = pl.ds(t * tile_up, tile_up)
        w_up = whole_up[:, cols]
        w_down = whole_down[cols, :]
        pre = dot(hidden_in, w_up) + bias_up[:, t * tile_up : (t + 1) * tile_up]
        phi = 0.5 * (1.0 + lax.erf(pre * (1.0 / math.sqrt(2.0))))
        act = (pre * phi).astype(BF16)
        act_s[:, cols] = act
        ffn = ffn + dot(act, w_down)
        slope = phi + pre * jnp.exp(-0.5 * pre * pre) * (1.0 / math.sqrt(2.0 * math.pi))
        gpre = (dot_nt(grad_ffn, w_down) * slope).astype(BF16)
        gpre_s[:, cols] = gpre
        grad_res = grad_res + dot_nt(gpre, w_up)
    gres_ref[...] = grad_res
    grad_branch = (a0 * grad_res).astype(BF16)
    grad_mixed = dot_nt(grad_branch, full_out).astype(BF16).astype(F32)
    for s in range(2):
        turned = grad_mixed[s * LANES : (s + 1) * LANES].T.astype(BF16)
        dos[pl.ds(s * HEADS, HEADS)] = turned.reshape(HEADS, HD, LANES)
    loop(lambda offset: d_copy(offset, False).start())
    doct_ref[place.slot] = dos[place.slot]

    t_out, t_up, t_down, t_kv, t_q, t_aux = [
        Reduce(place, part, out, *scratch)
        for (part, out), scratch in zip(
            (
                (p_out, r_out),
                (p_up, r_up),
                (p_down, r_down),
                (p_win[1], r_win.at[:, pl.ds(width, 2 * width)]),
                (p_win[0], r_win.at[:, pl.ds(0, width)]),
                (p_aux, r_aux),
            ),
            trees,
        )
    ]
    lead = (2, 2, depth, 2)
    for t in range(hidden // tile_up):
        cols = pl.ds(t * tile_up, tile_up)
        block = dot_tn(act_s[:, cols], grad_ffn).astype(BF16)
        p_down.reshape(hidden, width)[cols, :] = block
    t_down.start_core()
    for t in range(hidden // tile_up):
        cols = pl.ds(t * tile_up, tile_up)
        block = dot_tn(hidden_in, gpre_s[:, cols]).astype(BF16)
        p_up.reshape(width, hidden)[:, cols] = block
    t_up.start_core()
    p_out.reshape(width, width)[...] = dot(
        jnp.concatenate([mixed_turned[0], mixed_turned[1]], axis=1), grad_branch
    ).astype(BF16)
    t_out.start_core()

    ffn_term = a1 * ffn
    stream = residual + ffn_term
    out_ref[...] = stream.astype(BF16).reshape(2, LANES, width)

    def whole(values):
        return jnp.sum(jnp.sum(values, axis=0, keepdims=True), axis=1, keepdims=True)

    sums = (
        whole(stream * stream),
        whole(attn_term * attn_term),
        whole(ffn_term * ffn_term),
        whole(grad_res * branch),
        whole(grads * ffn),
    )
    lane = iota((devices * 8, LANES), 1)
    scalars = jnp.zeros((devices * 8, LANES), F32)
    for number, value in enumerate(sums):
        scalars = scalars + jnp.where(lane == number, value, 0.0)
    up_row = jnp.sum(gpre_s[...].astype(F32), axis=0, keepdims=True)
    down_row = jnp.sum(grad_ffn.astype(F32), axis=0, keepdims=True)
    out_row = jnp.sum(grad_branch.astype(F32), axis=0, keepdims=True)
    folded = (
        fold_bias(out_row, devices * 8, "output", per)
        + fold_bias(down_row, devices * 8, "down", per)
        + fold_bias(up_row, devices * 8, "up", per_up)
        + jnp.where((iota((devices * 8, LANES), 0) & 7) == SCALARS, scalars, 0.0)
    )
    p_aux[...] = folded.reshape(*lead, 8, LANES)

    early = (t_down, t_up, t_out)
    low_block = iota((BLOCK, LANES), 1) < HD

    def clear(number):
        acc[number] = jnp.zeros((LANES, LANES), F32)

    loop(clear, 0, span)

    def back_halo(part):
        return remote(
            halo_out, halo_in, back_hs.at[0], back_hr.at[0], place.member(place.slot, part)
        )

    def settle(number):
        dkv_sum[number] = acc[window + number].astype(BF16)

    def attend_back(m, carry):
        for number, tree in enumerate(early):

            @pl.when(m == 1 + number)
            def _():
                tree.start_second()

            @pl.when(m == pairs_of_chunks - 3 + number)
            def _():
                tree.start_first()

        await_from(d_copy, 2 * m)
        await_from(d_copy, 2 * m + 1)
        qt, dt = two(qt_ref, 2 * m), two(doct_ref, 2 * m)
        q_wide = jnp.concatenate([qt, blank], axis=0)
        d_wide = jnp.concatenate([blank, dt], axis=0)
        both = jnp.concatenate([qt, dt], axis=0).astype(F32).T
        q_and_d = jnp.concatenate(
            [jnp.where(low_block, both, 0.0), jnp.where(low_block, 0.0, both)], axis=0
        ).astype(BF16)
        start = q_rows_of(starts_ref, m)
        lse = q_rows_of(lse_ref, m)
        delta = jnp.sum(dt.astype(F32) * two(of_ref, 2 * m), axis=0, keepdims=True)
        base = m * BLOCK
        q_place = base + older + iota((1, BLOCK), 1)
        grad_scores = []
        for block in range(reach + 1):
            here = pl.ds(2 * (m + block), 2)
            kv = kv_ref[here].reshape(BLOCK, LANES)
            scores = masked(dot(kv, q_wide), start, q_place, block, base)
            probs = jnp.exp(scores - lse)
            grad_score = (probs * (dot(kv, d_wide) - delta)).astype(BF16)
            grad_scores.append(grad_score)
            both_scores = jnp.concatenate([grad_score, probs.astype(BF16)], axis=1)
            acc[here] += dot(both_scores, q_and_d).reshape(2, LANES, LANES)
        dq = dot(turned_window(m)[:HD], jnp.concatenate(grad_scores, axis=0)) * 0.125
        for side in range(2):
            dqt_ref[2 * m + side] = dq[:, side * LANES : (side + 1) * LANES].astype(BF16)
            send_to(dq_copy, 2 * m + side)
        if parts > 1:

            @pl.when((m == reach - 1) & (place.part > 0))
            def _():
                def put(number):
                    halo_out[number] = acc[number].astype(BF16)

                loop(put, 0, window)
                back_halo(place.part - 1).start()

        if free:

            @pl.when(m >= reach)
            def _():
                for side in range(2):
                    chunk = 2 * (m - reach) + side
                    settle(chunk)
                    send_to(dkv_copy, chunk)

        return carry

    lax.fori_loop(0, pairs_of_chunks, attend_back, 0)
    dq_in[place.slot] = dqt_ref[place.slot]
    loop(settle, GROUP - window, GROUP)
    if parts > 1:

        @pl.when(place.part < parts - 1)
        def _():
            back_halo(place.part + 1).wait_recv()

            def add(number):
                chunk = GROUP - window + number
                total = acc[window + chunk] + halo_in[number].astype(F32)
                dkv_sum[chunk] = total.astype(BF16)

            loop(add, 0, window)

    def late(offset):
        @pl.when(place.other_slot(offset) >= GROUP - window)
        def _():
            dkv_copy(offset, False).start()

    loop(late)
    dkv_in[place.slot] = dkv_sum[place.slot]

    tokens_turned = tokens.T
    loop(lambda offset: dq_copy(offset, True).wait_recv())
    for s in range(2):
        turned = dq_in[pl.ds(s * HEADS, HEADS)].reshape(width, LANES).astype(F32)
        gp[s * LANES : (s + 1) * LANES, 0:width] = turned.T.astype(BF16)
    query_row = jnp.sum(gp[:, 0:width].astype(F32), axis=0, keepdims=True)
    p_win[0][...] = (
        dot(tokens_turned, gp[:, 0:width])
        .astype(BF16)
        .reshape(*lead, width // devices, width)
    )
    t_q.start_core()
    full_in = gwin.reshape(width, 3 * width)
    gx = gres_ref[...] + dot_nt(gp[:, 0:width], full_in[:, 0:width])
    for tree in early:
        tree.start_line()
    t_q.start_second()

    loop(lambda offset: dkv_copy(offset, True).wait_recv())
    for s in range(2):
        at_rows = slice(s * LANES, (s + 1) * LANES)
        for pair in range(HEADS // 2):
            even = dkv_in[s * HEADS + 2 * pair].astype(F32)
            odd = dkv_in[s * HEADS + 2 * pair + 1].astype(F32)
            keys = jnp.where(low_lane, even, pltpu.roll(odd, HD, 1))
            values = jnp.where(low_lane, pltpu.roll(even, HD, 1), odd)
            at = width + pair * LANES
            gp[at_rows, at : at + LANES] = keys.astype(BF16)
            gp[at_rows, width + at : width + at + LANES] = values.astype(BF16)
    for t in range(2):
        part = dot(tokens_turned, gp[:, (1 + t) * width : (2 + t) * width]).astype(BF16)
        p_win[1][:, :, :, :, :, t * width : (t + 1) * width] = part.reshape(
            *lead, width // devices, width
        )
    t_kv.start_core()
    value_row = jnp.sum(gp[:, 2 * width :].astype(F32), axis=0, keepdims=True)
    folded = fold_bias(query_row, devices * 8, "query", per) + fold_bias(
        value_row, devices * 8, "value", per
    )
    p_aux[...] += folded.reshape(*lead, 8, LANES)
    t_aux.start_core()
    t_q.start_first()
    t_kv.start_second()
    t_aux.start_second()
    for t in range(1, 3):
        cols = slice(t * width, (t + 1) * width)
        gx = gx + dot_nt(gp[:, cols], full_in[:, cols])
    gx_ref[...] = gx.astype(BF16).reshape(2, LANES, width)
    for tree in early:
        tree.finish()
    t_q.start_line()
    t_aux.start_first()
    t_kv.start_first()
    t_aux.start_line()
    t_kv.start_line()
    t_q.finish()
    t_aux.finish()
    t_kv.finish()

    def sent(offset):
        for copy in (seg_copy, q_copy, k_copy, o_copy, d_copy, dq_copy, dkv_copy):
            copy(offset, False).wait_send()

    loop(sent)
    if parts > 1:

        @pl.when(place.part < parts - 1)
        def _():
            loop(lambda number: kv_halo(number, place.part + 1).wait_send(), 0, window)

        @pl.when(place.part > 0)
        def _():
            back_halo(place.part - 1).wait_send()

    for gather in gathers:
        gather.drain()
    for tree in early + (t_q, t_kv, t_aux):
        tree.drain()


def two(ref, index):
    return jnp.concatenate([ref[index], ref[index + 1]], axis=1)


def hand_out_kernel(
    tokens_all, out_ref, gx_ref, win_ref, wo_ref, wup_ref, wdown_ref, sums_ref, *results
):
    for src, dst in zip((out_ref, gx_ref, win_ref, wo_ref, wup_ref, wdown_ref), results[:6]):
        dst[...] = src[...]
    named = dict(zip(("query", "value", "output", "up", "down"), results[6:11]))
    for name, ref in named.items():
        ref[...] = sums_ref[BIASES.index(name), 0 : ref.shape[0]]
    results[11][...] = sums_ref[SCALARS, 3:5]
    results[12][...] = jnp.sqrt(sums_ref[SCALARS, 0:3] * (1.0 / tokens_all))


def call(kernel, out_shape, in_specs, out_specs, scratch, collective=None):
    return pl.pallas_call(
        kernel,
        out_shape=out_shape,
        in_specs=in_specs,
        out_specs=out_specs,
        scratch_shapes=scratch,
        compiler_params=pltpu.CompilerParams(
            collective_id=collective,
            has_side_effects=collective is not None,
            vmem_limit_bytes=VMEM_BYTES,
        ),
    )


def local(
    layer_input,
    segments,
    input_weight,
    output_weight,
    up_weight,
    down_weight,
    query_bias,
    value_bias,
    output_bias,
    up_bias,
    down_bias,
    alphas,
    out_grad,
):
    heads, blocks = lax.axis_size("head"), lax.axis_size("blk")
    depth, devices = blocks // 2, heads * blocks
    seqs, rows, width = layer_input.shape
    hidden = up_weight.shape[1]
    seq_len = rows * devices
    assert heads == 4 and seqs * HEADS == GROUP and rows == LANES
    longest = 16 * math.isqrt(seq_len)
    window, parts = longest // rows, devices // GROUP
    docs = 2 * seq_len // longest
    assert window <= GROUP and window % 2 == 0
    span = window + GROUP

    def shape(*dims, dtype=BF16):
        return jax.ShapeDtypeStruct(dims, dtype)

    vmem, smem = pl.BlockSpec(memory_space=VMEM), pl.BlockSpec(memory_space=pltpu.SMEM)
    dma = pltpu.SemaphoreType.DMA
    lead = (2, 2, depth, 2)
    in_rows, up_rows = input_weight.shape[0], down_weight.shape[0]
    gather_sems = Gather.semaphores(depth)
    reduced = (
        (in_rows, width, BF16),
        (in_rows, hidden, BF16),
        (up_rows, width, BF16),
        (in_rows, 2 * width, BF16),
        (in_rows, width, BF16),
        (8, LANES, F32),
    )
    tokens = seqs * rows
    results = (
        shape(seqs, rows, width),
        shape(seqs, rows, width),
        shape(in_rows, 3 * width, dtype=F32),
        shape(in_rows, width, dtype=F32),
        shape(in_rows, hidden, dtype=F32),
        shape(up_rows, width, dtype=F32),
    )
    carried = call(
        functools.partial(layer_kernel, blocks, parts, window, docs),
        results + (shape(8, LANES, dtype=F32),),
        [vmem] * 6 + [(vmem,) * 5] + [smem, vmem],
        (vmem,) * 7,
        [
            [
                VMEM((*lead, in_rows, 3 * width), BF16),
                VMEM((*lead, in_rows, width), BF16),
                VMEM((*lead, in_rows, hidden), BF16),
                VMEM((*lead, up_rows, width), BF16),
                VMEM((*lead, 8, LANES), F32),
            ],
            [dma((gather_sems,))] * 12,
            dma((6,)),
            [Reduce.scratch(depth, *sizes) for sizes in reduced],
            [dma((GROUP,))] * 14,
            [dma((1,)), dma((1,)), dma((window,)), dma((window,)), dma((1,)), dma((1,))],
            VMEM((span, 16, LANES), BF16),
            VMEM((16, LANES), BF16),
            VMEM((8, LANES), F32),
            VMEM((GROUP, HD, LANES), BF16),
            VMEM((GROUP, LANES, LANES), BF16),
            VMEM((GROUP, HD, LANES), BF16),
            VMEM((span, LANES, LANES), BF16),
            VMEM((span, LANES, LANES), BF16),
            VMEM((GROUP, LANES), jnp.int32),
            VMEM((GROUP, HD, LANES), BF16),
            VMEM((GROUP, HD, LANES), F32),
            VMEM((GROUP, LANES), F32),
            VMEM((GROUP, HD, LANES), BF16),
            VMEM((GROUP, HD, LANES), BF16),
            VMEM((GROUP, HD, LANES), BF16),
            VMEM((tokens, hidden), BF16),
            VMEM((tokens, hidden), BF16),
            VMEM((tokens, width), F32),
            VMEM((span, LANES, LANES), F32),
            VMEM((GROUP, HD, LANES), BF16),
            VMEM((GROUP, LANES, LANES), BF16),
            VMEM((GROUP, HD, LANES), BF16),
            VMEM((GROUP, LANES, LANES), BF16),
            VMEM((window, LANES, LANES), BF16),
            VMEM((window, LANES, LANES), BF16),
            VMEM((tokens, 3 * width), BF16),
            [
                [
                    VMEM((*lead, in_rows, width), BF16),
                    VMEM((*lead, in_rows, 2 * width), BF16),
                ],
                VMEM((*lead, in_rows, width), BF16),
                VMEM((*lead, in_rows, hidden), BF16),
                VMEM((*lead, up_rows, width), BF16),
                VMEM((*lead, 8, LANES), F32),
            ],
        ],
        collective=0,
    )(
        layer_input,
        segments,
        input_weight,
        output_weight,
        up_weight,
        down_weight,
        (query_bias, value_bias, output_bias, down_bias, up_bias),
        alphas,
        out_grad,
    )
    per, per_up = width // devices, hidden // devices
    return call(
        functools.partial(hand_out_kernel, seqs * seq_len * width),
        results
        + tuple(
            shape(size, dtype=F32) for size in (per, per, per, per_up, per, 2, 3)
        ),
        [vmem] * 7,
        (vmem,) * 13,
        [],
    )(*carried)


def solution(mesh):
    tokens = P(None, ("head", "blk"), None)
    rows, flat = P(("head", "blk"), None), P(("head", "blk"))
    return jax.shard_map(
        local,
        mesh=mesh,
        in_specs=(
            tokens,
            P(None, ("head", "blk")),
            rows,
            rows,
            rows,
            rows,
            flat,
            flat,
            flat,
            flat,
            flat,
            P(),
            tokens,
        ),
        out_specs=(
            tokens,
            tokens,
            rows,
            rows,
            rows,
            rows,
            flat,
            flat,
            flat,
            flat,
            flat,
            P(),
            P(),
        ),
        check_vma=False,
    )
```

time: 189 us -> 139 us (0.74)
  Pallas kernels: 170 us -> 138 us
  local copies, waits for them, and re-layouts: 16.4 us -> 0 us
    pallas_call x5 -> x2, Pallas kernels: 170 us -> 138 us  [the longest x1 136 us: local(): call(functools.partial(layer_kernel, blocks, parts, window, docs), result...]
    unnamed x8 -> x0, local copies, waits for them, and re-layouts: 8.42 us -> none
    squeeze x3 -> x0, local copies, waits for them, and re-layouts: 3.92 us -> none  [the longest x2 2.67 us: bias_grad(): return sums[0, offset:offset + per]]
    concatenate x1 -> x0, local copies, waits for them, and re-layouts: 3.43 us -> none  [local(): jnp.concatenate([query_bias, value_bias, output_bias, down_bias, up_bias])]
where the time goes in v2:
time: 139 us
  Pallas kernels  138 us (99%)
    pallas_call x1, Pallas kernels, local(): call(functools.partial(layer_kernel, blocks, parts, window, docs), result...  136 us

profile of v2, /device:TPU:0, one launch (start us, length us, event | category | flops | bytes accessed | tf_op | source)
XLA Modules:
  0.0 138.8 jit_solution(214750901119521299)
XLA Ops:
  0.6 135.9 %shard_map.228 = (bf16[2,128,512]{2,1,0:T(8,128)(2,1)}, bf16[2,128,512]{2,1,0:T(8,128)(2,1)}, f32[16,1536]{1,0:T(8,128)}, f32[16,512]{1,0:T(8,128)}, f32[16,2048...) custom-call(bf16[2,128,512]{2,1,0:T(8,128)(2,1)} %x_ref.1, s32[2,128]{1,0:T(2,128)} %seg_ref.1, ...), custom_call_target="tpu_custom_call" | custom-call | tf_op jit(solution)/shard_map/pallas_call | solution.py:1142
  136.5 2.1 %shard_map.229 = (bf16[2,128,512]{2,1,0:T(8,128)(2,1)}, bf16[2,128,512]{2,1,0:T(8,128)(2,1)}, f32[16,1536]{1,0:T(8,128)}, f32[16,512]{1,0:T(8,128)}, f32[16,2048...) custom-call(bf16[2,128,512]{2,1,0:T(8,128)(2,1)} %get-tuple-element., ...), custom_call_target="tpu_custom_call" | custom-call | tf_op jit(solution)/shard_map/pallas_call | solution.py:1210

commit v3 on v2

--- a/solution.py
+++ b/solution.py
@@ -18,6 +18,7 @@
 BF16 = jnp.bfloat16
 VMEM = pltpu.VMEM
 NEG = -1e30
+MOST = 2
 
 
 class Place:
@@ -82,8 +83,9 @@
         lax.fori_loop(1, place.depth, line, 0)
         hello(place.at(x=1 - place.x))
         hello(place.at(y=1 - place.y))
+        hello(place.at(x=1 - place.x, y=1 - place.y))
         hello(place.at(core=1 - place.core))
-        total += place.depth + 2
+        total += place.depth + 3
     if parts > 1 and tree:
 
         @pl.when(place.part > 0)
@@ -101,38 +103,113 @@
 def halves_of(columns):
     if columns < 2 * LANES:
         return ((0, columns, "yx"),)
-    return ((0, columns // 2, "yx"), (columns // 2, columns // 2, "xy"))
+    most = max(columns // 2, columns * MOST // 4)
+    return ((0, most, "yx"), (most, columns - most, "xy"))
+
+
+def wait_received(place, dst, sem):
+    remote(dst, dst, sem, sem, place.at(core=1 - place.core)).wait_recv()
+
+
+def wait_sent(place, src, sem):
+    remote(src, src, sem, sem, place.at(core=1 - place.core)).wait_send()
 
 
 class Gather:
-    def __init__(self, place, src, dst, send, recv, local, cols=None):
-        self.place, self.src, self.dst = place, src, dst
-        self.send, self.recv, self.local = send, recv, local
-        self.start, self.width = cols or (0, dst.shape[-1])
-        self.halves = halves_of(self.width)
-        self.lines = place.depth - 1
-
-    @staticmethod
-    def semaphores(depth):
-        return depth + 8
+    COUNT = 9
+
+    def __init__(self, place, src, dst, sems, cols=None):
+        self.place, self.src, self.dst, self.sems = place, src, dst, sems
+        start, width = cols or (0, dst.shape[-1])
+        self.cols = pl.ds(start, width)
+
+    def part(self, *index):
+        return self.dst.at[index + (slice(None), self.cols)]
+
+    def column(self, core, x, y):
+        return self.part(x, core, slice(None), y)
+
+    def others(self):
+        place = self.place
+        return ((1 - place.x, place.y), (place.x, 1 - place.y), (1 - place.x, 1 - place.y))
+
+    def own(self):
+        place = self.place
+        mine = self.part(place.x, place.core, place.z, place.y)
+        return pltpu.make_async_copy(self.src.at[:, self.cols], mine, self.sems.at[0])
+
+    def start_line(self):
+        place = self.place
+        for offset in range(1, place.depth):
+            remote(
+                self.src.at[:, self.cols],
+                self.part(place.x, place.core, place.z, place.y),
+                self.sems.at[1],
+                self.sems.at[2],
+                place.at(z=place.deeper(offset)),
+            ).start()
+        self.own().start()
+
+    def lines(self):
+        return self.part(0, 0, pl.ds(0, self.place.depth - 1), 0)
+
+    def hand(self, x, y):
+        place = self.place
+        column = self.column(place.core, x, y)
+        remote(
+            column, column, self.sems.at[7], self.sems.at[8], place.at(core=1 - place.core)
+        ).start()
+
+    def start_columns(self):
+        place = self.place
+        self.own().wait()
+        wait_received(place, self.lines(), self.sems.at[2])
+        mine = self.column(place.core, place.x, place.y)
+        for number, (x, y) in enumerate(self.others()):
+            remote(
+                mine, mine, self.sems.at[3], self.sems.at[4 + number], place.at(x=x, y=y)
+            ).start()
+        self.hand(place.x, place.y)
+
+    def start_hands(self):
+        for number, (x, y) in enumerate(self.others()):
+            wait_received(
+                self.place, self.column(self.place.core, x, y), self.sems.at[4 + number]
+            )
+            self.hand(x, y)
+
+    def finish(self):
+        every = slice(None)
+        region = self.part(every, 1 - self.place.core, every, every)
+        wait_received(self.place, region, self.sems.at[8])
+
+    def drain(self):
+        place = self.place
+        wait_sent(place, self.lines(), self.sems.at[1])
+        every = slice(None)
+        wait_sent(
+            place, self.part(every, every, pl.ds(0, 3 * place.depth // 4), 0), self.sems.at[3]
+        )
+        wait_sent(place, self.part(every, 0, every, every), self.sems.at[7])
+
+
+def halves_of(columns):
+    if columns < 2 * LANES:
+        return ((0, columns, "yx"),)
+    most = max(columns // 2, columns * MOST // 4)
+    return ((0, most, "yx"), (most, columns - most, "xy"))
+
+
+class TreeGather:
+    COUNT = 13
+
+    def __init__(self, place, src, dst, sems):
+        self.place, self.src, self.dst, self.sems = place, src, dst, sems
+        self.halves = halves_of(dst.shape[-1])
 
     def cut(self, half, *index):
         start, width, _ = half
-        return self.dst.at[index + (slice(None), pl.ds(self.start + start, width))]
-
-    def shard(self):
-        return self.src.at[:, pl.ds(self.start, self.width)]
-
-    def whole(self, *index):
-        return self.dst.at[index + (slice(None), pl.ds(self.start, self.width))]
-
-    def pair(self, half, first, x, y):
-        place, every = self.place, slice(None)
-        if first:
-            return self.cut(half, x, place.core, every, y)
-        if half[2] == "yx":
-            return self.cut(half, x, place.core, every, every)
-        return self.cut(half, every, place.core, every, y)
+        return self.dst.at[index + (slice(None), pl.ds(start, width))]
 
     def across(self, half, first):
         place = self.place
@@ -140,142 +217,221 @@
             return place.x, 1 - place.y
         return 1 - place.x, place.y
 
-    def line(self, offset, come):
-        place = self.place
-        z = place.deeper(-offset) if come else place.z
+    def region(self, half, first, core, x, y):
+        every = slice(None)
+        if first:
+            return self.cut(half, x, core, every, y)
+        if half[2] == "yx":
+            return self.cut(half, x, core, every, every)
+        return self.cut(half, every, core, every, y)
+
+    def own(self):
+        place = self.place
+        mine = self.dst.at[place.x, place.core, place.z, place.y]
+        return pltpu.make_async_copy(self.src, mine, self.sems.at[0])
+
+    def start_line(self):
+        place = self.place
+        for offset in range(1, place.depth):
+            remote(
+                self.src,
+                self.dst.at[place.x, place.core, place.z, place.y],
+                self.sems.at[1],
+                self.sems.at[2],
+                place.at(z=place.deeper(offset)),
+            ).start()
+        self.own().start()
+
+    def lines(self):
+        return self.dst.at[0, 0, pl.ds(0, self.place.depth - 1), 0]
+
+    def exchange(self, number, first):
+        place, half = self.place, self.halves[number]
+        x, y = self.across(half, first)
+        mine = self.region(half, first, place.core, place.x, place.y)
+        base = 0 if first else 2
         return remote(
-            self.shard(),
-            self.whole(place.x, place.core, z, place.y),
-            self.send.at[offset - 1],
-            self.recv.at[offset - 1],
+            mine,
+            mine,
+            self.sems.at[3 + base + number],
+            self.sems.at[9 + base + number],
+            place.at(x=x, y=y),
+        )
+
+    def received(self, number, first):
+        half = self.halves[number]
+        x, y = self.across(half, first)
+        region = self.region(half, first, self.place.core, x, y)
+        wait_received(self.place, region, self.sems.at[(9 if first else 11) + number])
+        return region
+
+    def hand(self, region):
+        place = self.place
+        remote(
+            region, region, self.sems.at[7], self.sems.at[8], place.at(core=1 - place.core)
+        ).start()
+
+    def start_first(self):
+        place = self.place
+        self.own().wait()
+        wait_received(place, self.lines(), self.sems.at[2])
+        for number in range(len(self.halves)):
+            self.exchange(number, True).start()
+        self.hand(self.dst.at[place.x, place.core, slice(None), place.y])
+
+    def start_second(self):
+        for number in range(len(self.halves)):
+            region = self.received(number, True)
+            self.exchange(number, False).start()
+            self.hand(region)
+
+    def start_hands(self):
+        for number in range(len(self.halves)):
+            self.hand(self.received(number, False))
+
+    def finish(self):
+        wait_received(self.place, self.dst.at[:, 1 - self.place.core], self.sems.at[8])
+
+    def drain(self):
+        for number in range(len(self.halves)):
+            self.exchange(number, True).wait_send()
+            self.exchange(number, False).wait_send()
+        wait_sent(self.place, self.lines(), self.sems.at[1])
+        wait_sent(self.place, self.dst.at[:, 0], self.sems.at[7])
+
+
+class Reduce:
+    COUNT = 8
+
+    def __init__(self, place, part, out, rc, total, rn, rz, sems):
+        self.place, self.part, self.out = place, part, out
+        self.rc, self.total, self.rn, self.rz, self.sems = rc, total, rn, rz, sems
+
+    @staticmethod
+    def scratch(depth, rows, cols, dtype):
+        return [
+            VMEM((2, depth, 2, rows, cols), dtype),
+            VMEM((2, depth, 2, rows, cols), dtype),
+            VMEM((3, depth, rows, cols), dtype),
+            VMEM((depth - 1, rows, cols), dtype),
+            pltpu.SemaphoreType.DMA((Reduce.COUNT,)),
+        ]
+
+    def others(self):
+        place = self.place
+        return ((1 - place.x, place.y), (place.x, 1 - place.y), (1 - place.x, 1 - place.y))
+
+    def core(self):
+        place = self.place
+        return remote(
+            self.part.at[:, 1 - place.core],
+            self.rc,
+            self.sems.at[0],
+            self.sems.at[1],
+            place.at(core=1 - place.core),
+        )
+
+    def columns(self):
+        place = self.place
+        for number, (x, y) in enumerate(self.others()):
+            yield remote(
+                self.total.at[x, :, y],
+                self.rn.at[number],
+                self.sems.at[2],
+                self.sems.at[3 + number],
+                place.at(x=x, y=y),
+            )
+
+    def line(self, offset):
+        place = self.place
+        return remote(
+            self.total.at[place.x, place.deeper(offset), place.y],
+            self.rz.at[offset - 1],
+            self.sems.at[6],
+            self.sems.at[7],
             place.at(z=place.deeper(offset)),
         )
 
-    def own(self):
-        place = self.place
-        return pltpu.make_async_copy(
-            self.shard(), self.whole(place.x, place.core, place.z, place.y), self.local
-        )
-
-    def exchange(self, number, first, come):
-        half = self.halves[number]
-        place = self.place
-        x, y = self.across(half, first)
-        slot = self.lines + (0 if first else 2) + number
-        mine = self.pair(half, first, place.x, place.y)
-        landing = self.pair(half, first, x, y) if come else mine
-        return remote(
-            mine, landing, self.send.at[slot], self.recv.at[slot], place.at(x=x, y=y)
-        )
-
-    def hand(self, which, come):
-        place, every = self.place, slice(None)
-        slot = self.lines + 4 + which
-        core = 1 - place.core if come else place.core
-
-        def region(core):
-            if which == 0:
-                return self.whole(place.x, core, every, place.y)
-            number = (which - 1) % 2
-            half = self.halves[number]
-            first = which < 3
-            x, y = self.across(half, first)
-            if first:
-                return self.cut(half, x, core, every, y)
-            if half[2] == "yx":
-                return self.cut(half, x, core, every, every)
-            return self.cut(half, every, core, every, y)
-
-        return remote(
-            region(place.core),
-            region(core),
-            self.send.at[slot],
-            self.recv.at[slot],
-            place.at(core=1 - place.core),
-        )
+    def start_core(self):
+        self.core().start()
+
+    def add_core(self, x, z, y):
+        place = self.place
+        self.total[x, z, y] = (
+            self.part[x, place.core, z, y].astype(F32) + self.rc[x, z, y].astype(F32)
+        ).astype(self.total.dtype)
+
+    def start_columns(self):
+        place = self.place
+        self.core().wait_recv()
+        for copy, (x, y) in zip(self.columns(), self.others()):
+
+            def add(z, carry):
+                self.add_core(x, z, y)
+                return carry
+
+            lax.fori_loop(0, place.depth, add, 0)
+            copy.start()
+
+        def add(z, carry):
+            self.add_core(place.x, z, place.y)
+            return carry
+
+        lax.fori_loop(0, place.depth, add, 0)
 
     def start_line(self):
-        for offset in range(1, self.lines + 1):
-            self.line(offset, False).start()
-        self.own().start()
-
-    def start_first(self):
-        self.own().wait()
-        for offset in range(1, self.lines + 1):
-            self.line(offset, True).wait_recv()
-        for number in range(len(self.halves)):
-            self.exchange(number, True, False).start()
-        self.hand(0, False).start()
-
-    def start_second(self):
-        for number in range(len(self.halves)):
-            self.exchange(number, True, True).wait_recv()
-            self.exchange(number, False, False).start()
-            self.hand(1 + number, False).start()
-
-    def start_last(self):
-        for number in range(len(self.halves)):
-            self.exchange(number, False, True).wait_recv()
-            self.hand(3 + number, False).start()
-
-    def hands(self):
-        for number in range(len(self.halves)):
-            yield 1 + number
-            yield 3 + number
+        place = self.place
+        for copy in self.columns():
+            copy.wait_recv()
+        here = (place.x, slice(None), place.y)
+        total = self.total[here].astype(F32)
+        for number in range(3):
+            total = total + self.rn[number].astype(F32)
+        self.total[here] = total.astype(self.total.dtype)
+        for offset in range(1, place.depth):
+            self.line(offset).start()
 
     def finish(self):
-        self.hand(0, True).wait_recv()
-        for which in self.hands():
-            self.hand(which, True).wait_recv()
+        place = self.place
+        wait_received(place, self.rz, self.sems.at[7])
+        result = self.total[place.x, place.z, place.y].astype(F32)
+        for offset in range(1, place.depth):
+            result = result + self.rz[offset - 1].astype(F32)
+        self.out[...] = result
 
     def drain(self):
-        for offset in range(1, self.lines + 1):
-            self.line(offset, False).wait_send()
-        for number in range(len(self.halves)):
-            self.exchange(number, True, False).wait_send()
-            self.exchange(number, False, False).wait_send()
-        self.hand(0, False).wait_send()
-        for which in self.hands():
-            self.hand(which, False).wait_send()
-
-
-class Reduce:
-    def __init__(self, place, part, out, rc, total, ra, rb, fa, fb, rz, send, recv):
+        place = self.place
+        self.core().wait_send()
+        wait_sent(place, self.rn, self.sems.at[2])
+        wait_sent(place, self.rz, self.sems.at[6])
+
+
+class TreeReduce:
+    COUNT = 12
+
+    def __init__(self, place, part, out, rc, total, ra, rb, fa, fb, rz, sems):
         self.place, self.part, self.out = place, part, out
         self.rc, self.total, self.rz = rc, total, rz
         self.second, self.first = (ra, rb), (fa, fb)
-        self.send, self.recv = send, recv
+        self.sems = sems
         self.halves = halves_of(part.shape[-1])
-        self.lines = place.depth - 1
-
-    @staticmethod
-    def semaphores(depth):
-        return depth + 4
 
     @staticmethod
     def scratch(depth, rows, cols, dtype):
-        wide = halves_of(cols)[0][1]
+        wide, narrow = [half[1] for half in halves_of(cols)]
         return [
             VMEM((2, depth, 2, rows, cols), dtype),
             VMEM((2, depth, 2, rows, cols), dtype),
             VMEM((depth, 2, rows, wide), dtype),
-            VMEM((2, depth, rows, wide), dtype),
+            VMEM((2, depth, rows, narrow), dtype),
             VMEM((depth, rows, wide), dtype),
-            VMEM((depth, rows, wide), dtype),
+            VMEM((depth, rows, narrow), dtype),
             VMEM((depth - 1, rows, cols), dtype),
-            pltpu.SemaphoreType.DMA((Reduce.semaphores(depth),)),
-            pltpu.SemaphoreType.DMA((Reduce.semaphores(depth),)),
+            pltpu.SemaphoreType.DMA((TreeReduce.COUNT,)),
         ]
 
-    def core(self):
-        place, every = self.place, slice(None)
-        return remote(
-            self.part.at[every, 1 - place.core],
-            self.rc,
-            self.send.at[0],
-            self.recv.at[0],
-            place.at(core=1 - place.core),
-        )
+    core, line, start_core, add_core = Reduce.core, Reduce.line, Reduce.start_core, Reduce.add_core
+    finish = Reduce.finish
 
     def cut(self, half, *index):
         start, width, _ = half
@@ -284,7 +440,7 @@
     def exchange(self, number, second):
         place, every = self.place, slice(None)
         half = self.halves[number]
-        slot = (1 if second else 3) + number
+        slot = (2 if second else 8) + number
         over_x = (half[2] == "yx") == second
         device = place.at(x=1 - place.x) if over_x else place.at(y=1 - place.y)
         if second:
@@ -296,38 +452,21 @@
         return remote(
             self.total.at[self.cut(half, *index)],
             landing,
-            self.send.at[slot],
-            self.recv.at[slot],
+            self.sems.at[slot],
+            self.sems.at[slot + 2],
             device,
         )
 
-    def line(self, offset):
-        place = self.place
-        return remote(
-            self.total.at[place.x, place.deeper(offset), place.y],
-            self.rz.at[offset - 1],
-            self.send.at[4 + offset],
-            self.recv.at[4 + offset],
-            place.at(z=place.deeper(offset)),
-        )
-
-    def start_core(self):
-        self.core().start()
-
     def start_second(self):
-        place = self.place
         self.core().wait_recv()
-        dtype = self.total.dtype
 
         def add(z, carry):
             for x in range(2):
                 for y in range(2):
-                    self.total[x, z, y] = (
-                        self.part[x, place.core, z, y].astype(F32) + self.rc[x, z, y].astype(F32)
-                    ).astype(dtype)
+                    self.add_core(x, z, y)
             return carry
 
-        lax.fori_loop(0, place.depth, add, 0)
+        lax.fori_loop(0, self.place.depth, add, 0)
         for number in range(len(self.halves)):
             self.exchange(number, True).start()
 
@@ -364,25 +503,15 @@
                 return carry
 
             lax.fori_loop(0, place.depth, add, 0)
-        for offset in range(1, self.lines + 1):
+        for offset in range(1, place.depth):
             self.line(offset).start()
-
-    def finish(self):
-        place = self.place
-        for offset in range(1, self.lines + 1):
-            self.line(offset).wait_recv()
-        result = self.total[place.x, place.z, place.y].astype(F32)
-        for offset in range(1, self.lines + 1):
-            result = result + self.rz[offset - 1].astype(F32)
-        self.out[...] = result
 
     def drain(self):
         self.core().wait_send()
         for number in range(len(self.halves)):
             self.exchange(number, True).wait_send()
             self.exchange(number, False).wait_send()
-        for offset in range(1, self.lines + 1):
-            self.line(offset).wait_send()
+        wait_sent(self.place, self.rz, self.sems.at[6])
 
 
 def iota(shape, dim):
@@ -455,7 +584,6 @@
     r_aux,
     gathered,
     gather_sems,
-    local,
     trees,
     exchange_sems,
     halo_sems,
@@ -503,14 +631,16 @@
 
         lax.fori_loop(low, high, step, 0)
 
-    def exchange(src, dst, number):
-        send, recv = exchange_sems[2 * number : 2 * number + 2]
-
-        def copy(offset, come):
+    def exchange(src, dst, sems, each=False):
+        def copy(offset, come=False):
             landing = place.other_slot(-offset) if come else place.slot
             target = place.other_slot(offset)
             return remote(
-                src(target), dst(landing), send.at[offset], recv.at[offset], place.member(target)
+                src(target),
+                dst(landing),
+                sems.at[0],
+                sems.at[offset if each else 1],
+                place.member(target),
             )
 
         return copy
@@ -518,21 +648,28 @@
     def entry(ref, base=0):
         return lambda index: ref.at[base + index]
 
-    seg_copy = exchange(lambda target: tile, entry(segs, window), 0)
-    k_copy = exchange(entry(ks), entry(kv_ref, window), 1)
-    q_copy = exchange(entry(qs), entry(qt_ref), 2)
-    o_copy = exchange(entry(ot_ref), entry(mixed_t), 3)
-    d_copy = exchange(entry(dos), entry(doct_ref), 4)
-    dq_copy = exchange(entry(dqt_ref), entry(dq_in), 5)
-    dkv_copy = exchange(entry(dkv_sum), entry(dkv_in), 6)
+    seg_sems, k_sems, q_sems, o_sems, d_sems, dq_sems, dkv_sems = exchange_sems
+    seg_copy = exchange(lambda target: tile, entry(segs, window), seg_sems)
+    k_copy = exchange(entry(ks), entry(kv_ref, window), k_sems, True)
+    q_copy = exchange(entry(qs), entry(qt_ref), q_sems)
+    o_copy = exchange(entry(ot_ref), entry(mixed_t), o_sems)
+    d_copy = exchange(entry(dos), entry(doct_ref), d_sems, True)
+    dq_copy = exchange(entry(dqt_ref), entry(dq_in), dq_sems)
+    dkv_copy = exchange(entry(dkv_sum), entry(dkv_in), dkv_sems)
     seg_hs, seg_hr, kv_hs, kv_hr, back_hs, back_hr = halo_sems
+
+    def all_here(ref, sems):
+        wait_received(place, ref.at[pl.ds(0, GROUP - 1)], sems.at[1])
+
+    def all_sent(ref, sems):
+        wait_sent(place, ref.at[pl.ds(0, GROUP - 1)], sems.at[0])
 
     def send_to(copy, target):
         offset = lax.rem(target - place.slot + GROUP, GROUP)
 
         @pl.when(offset != 0)
         def _():
-            copy(offset, False).start()
+            copy(offset).start()
 
     def await_from(copy, source):
         offset = lax.rem(place.slot - source + GROUP, GROUP)
@@ -560,27 +697,28 @@
         (aux_ref, gaux, None),
         (win_ref, gwin, (width, 2 * width)),
         (win_ref, gwin, (0, width)),
-        (wo_ref, gwo, None),
-        (wup_ref, gwup, None),
-        (wdown_ref, gwdown, None),
     )
-    gathers = [
-        Gather(place, src, dst, gather_sems[2 * i], gather_sems[2 * i + 1], local.at[i], cols)
-        for i, (src, dst, cols) in enumerate(plan)
+    g_aux, g_kv, g_q = [
+        Gather(place, src, dst, sems, cols)
+        for (src, dst, cols), sems in zip(plan, gather_sems[:3])
     ]
-    first, rest = gathers[:3], gathers[3:]
-    g_aux, g_kv, g_q = first
-    for gather in first:
-        gather.start_line()
-    loop(lambda offset: seg_copy(offset, False).start())
-    for gather in first:
-        gather.start_first()
+    rest = [
+        TreeGather(place, src, dst, sems)
+        for (src, dst), sems in zip(
+            ((wo_ref, gwo), (wup_ref, gwup), (wdown_ref, gwdown)), gather_sems[3:]
+        )
+    ]
+    g_kv.start_line()
+    g_aux.start_line()
+    g_q.start_line()
+    loop(lambda offset: seg_copy(offset).start())
+    g_kv.start_columns()
+    g_aux.start_columns()
+    g_q.start_columns()
     for gather in rest:
         gather.start_line()
-    for gather in first:
-        gather.start_second()
-
-    loop(lambda offset: seg_copy(offset, True).wait_recv())
+
+    wait_received(place, segs.at[pl.ds(0, GROUP - 1)], seg_sems.at[1])
 
     def seg_halo(part):
         return remote(
@@ -597,8 +735,9 @@
         def _():
             seg_halo(place.part + 1).start()
 
-    for gather in first:
-        gather.start_last()
+    g_kv.start_hands()
+    g_aux.start_hands()
+    g_q.start_hands()
     g_aux.finish()
     g_kv.finish()
 
@@ -626,7 +765,7 @@
             k_at, v_at = k[at], v[at]
             ks[head] = jnp.where(low_lane, k_at, pltpu.roll(v_at, HD, 1)).astype(BF16)
             ks[head + 1] = jnp.where(low_lane, pltpu.roll(k_at, HD, 1), v_at).astype(BF16)
-    loop(lambda offset: k_copy(offset, False).start())
+    loop(lambda offset: k_copy(offset).start())
     kv_ref[window + place.slot] = ks[place.slot]
     g_q.finish()
     for t in range(width // wide):
@@ -635,7 +774,7 @@
             turned = q[at].T.astype(BF16)
             qs[head] = turned[:HD]
             qs[head + 1] = turned[HD:]
-    loop(lambda offset: q_copy(offset, False).start())
+    loop(lambda offset: q_copy(offset).start())
     qt_ref[place.slot] = qs[place.slot]
 
     for gather in rest:
@@ -691,7 +830,7 @@
         arrived(place.other_slot(-offset))
 
     loop(kv_wait)
-    loop(lambda offset: q_copy(offset, True).wait_recv())
+    all_here(qt_ref, q_sems)
 
     many = window + 2
     older = window * LANES
@@ -716,7 +855,7 @@
 
             @pl.when(step == 1 + 2 * number)
             def _():
-                gather.start_last()
+                gather.start_hands()
 
         if parts > 1:
 
@@ -782,7 +921,7 @@
         gather.finish()
     full_out = gwo[...].reshape(width, width)
 
-    loop(lambda offset: o_copy(offset, True).wait_recv())
+    all_here(mixed_t, o_sems)
     mixed_turned = mixed_t[...].reshape(2, width, LANES)
     mixed = jnp.concatenate([mixed_turned[0].T, mixed_turned[1].T], axis=0)
     branch = dot(mixed, full_out) + bias_out
@@ -814,12 +953,14 @@
     for s in range(2):
         turned = grad_mixed[s * LANES : (s + 1) * LANES].T.astype(BF16)
         dos[pl.ds(s * HEADS, HEADS)] = turned.reshape(HEADS, HD, LANES)
-    loop(lambda offset: d_copy(offset, False).start())
+    loop(lambda offset: d_copy(offset).start())
     doct_ref[place.slot] = dos[place.slot]
 
+    kinds = (TreeReduce, TreeReduce, TreeReduce, Reduce, Reduce, Reduce)
     t_out, t_up, t_down, t_kv, t_q, t_aux = [
-        Reduce(place, part, out, *scratch)
-        for (part, out), scratch in zip(
+        kind(place, part, out, *scratch)
+        for kind, (part, out), scratch in zip(
+            kinds,
             (
                 (p_out, r_out),
                 (p_up, r_up),
@@ -898,10 +1039,6 @@
             @pl.when(m == 1 + number)
             def _():
                 tree.start_second()
-
-            @pl.when(m == pairs_of_chunks - 3 + number)
-            def _():
-                tree.start_first()
 
         await_from(d_copy, 2 * m)
         await_from(d_copy, 2 * m + 1)
@@ -971,13 +1108,15 @@
     def late(offset):
         @pl.when(place.other_slot(offset) >= GROUP - window)
         def _():
-            dkv_copy(offset, False).start()
+            dkv_copy(offset).start()
 
     loop(late)
     dkv_in[place.slot] = dkv_sum[place.slot]
+    for tree in early:
+        tree.start_first()
 
     tokens_turned = tokens.T
-    loop(lambda offset: dq_copy(offset, True).wait_recv())
+    all_here(dq_in, dq_sems)
     for s in range(2):
         turned = dq_in[pl.ds(s * HEADS, HEADS)].reshape(width, LANES).astype(F32)
         gp[s * LANES : (s + 1) * LANES, 0:width] = turned.T.astype(BF16)
@@ -990,11 +1129,9 @@
     t_q.start_core()
     full_in = gwin.reshape(width, 3 * width)
     gx = gres_ref[...] + dot_nt(gp[:, 0:width], full_in[:, 0:width])
-    for tree in early:
-        tree.start_line()
-    t_q.start_second()
-
-    loop(lambda offset: dkv_copy(offset, True).wait_recv())
+    t_q.start_columns()
+
+    all_here(dkv_in, dkv_sems)
     for s in range(2):
         at_rows = slice(s * LANES, (s + 1) * LANES)
         for pair in range(HEADS // 2):
@@ -1011,35 +1148,36 @@
             *lead, width // devices, width
         )
     t_kv.start_core()
+    for tree in early:
+        tree.start_line()
     value_row = jnp.sum(gp[:, 2 * width :].astype(F32), axis=0, keepdims=True)
     folded = fold_bias(query_row, devices * 8, "query", per) + fold_bias(
         value_row, devices * 8, "value", per
     )
     p_aux[...] += folded.reshape(*lead, 8, LANES)
     t_aux.start_core()
-    t_q.start_first()
-    t_kv.start_second()
-    t_aux.start_second()
+    t_q.start_line()
+    t_kv.start_columns()
+    t_aux.start_columns()
     for t in range(1, 3):
         cols = slice(t * width, (t + 1) * width)
         gx = gx + dot_nt(gp[:, cols], full_in[:, cols])
     gx_ref[...] = gx.astype(BF16).reshape(2, LANES, width)
+    t_aux.start_line()
+    t_kv.start_line()
     for tree in early:
         tree.finish()
-    t_q.start_line()
-    t_aux.start_first()
-    t_kv.start_first()
-    t_aux.start_line()
-    t_kv.start_line()
     t_q.finish()
     t_aux.finish()
     t_kv.finish()
 
-    def sent(offset):
-        for copy in (seg_copy, q_copy, k_copy, o_copy, d_copy, dq_copy, dkv_copy):
-            copy(offset, False).wait_send()
-
-    loop(sent)
+    all_sent(segs, seg_sems)
+    all_sent(ks, k_sems)
+    all_sent(qs, q_sems)
+    all_sent(ot_ref, o_sems)
+    all_sent(dos, d_sems)
+    all_sent(dqt_ref, dq_sems)
+    all_sent(dkv_sum, dkv_sems)
     if parts > 1:
 
         @pl.when(place.part < parts - 1)
@@ -1050,7 +1188,7 @@
         def _():
             back_halo(place.part - 1).wait_send()
 
-    for gather in gathers:
+    for gather in (g_aux, g_kv, g_q, *rest):
         gather.drain()
     for tree in early + (t_q, t_kv, t_aux):
         tree.drain()
@@ -1121,7 +1259,6 @@
     dma = pltpu.SemaphoreType.DMA
     lead = (2, 2, depth, 2)
     in_rows, up_rows = input_weight.shape[0], down_weight.shape[0]
-    gather_sems = Gather.semaphores(depth)
     reduced = (
         (in_rows, width, BF16),
         (in_rows, hidden, BF16),
@@ -1152,10 +1289,10 @@
                 VMEM((*lead, up_rows, width), BF16),
                 VMEM((*lead, 8, LANES), F32),
             ],
-            [dma((gather_sems,))] * 12,
-            dma((6,)),
-            [Reduce.scratch(depth, *sizes) for sizes in reduced],
-            [dma((GROUP,))] * 14,
+            [dma((Gather.COUNT,))] * 3 + [dma((TreeGather.COUNT,))] * 3,
+            [TreeReduce.scratch(depth, *sizes) for sizes in reduced[:3]]
+            + [Reduce.scratch(depth, *sizes) for sizes in reduced[3:]],
+            [dma((2,)), dma((GROUP,)), dma((2,)), dma((2,)), dma((GROUP,)), dma((2,)), dma((2,))],
             [dma((1,)), dma((1,)), dma((window,)), dma((window,)), dma((1,)), dma((1,))],
             VMEM((span, 16, LANES), BF16),
             VMEM((16, LANES), BF16),

time: 139 us -> 126 us (0.906)
  Pallas kernels: 138 us -> 125 us
    pallas_call x1, Pallas kernels: 136 us -> 123 us  [local(): call(functools.partial(layer_kernel, blocks, parts, window, docs), result...]
where the time goes in v3:
time: 126 us
  Pallas kernels  125 us (99%)
    pallas_call x1, Pallas kernels, local(): call(functools.partial(layer_kernel, blocks, parts, window, docs), result...  123 us

profile of v3, /device:TPU:0, one launch (start us, length us, event | category | flops | bytes accessed | tf_op | source)
XLA Modules:
  0.0 125.5 jit_solution(7619056985669027301)
XLA Ops:
  0.6 122.6 %shard_map.228 = (bf16[2,128,512]{2,1,0:T(8,128)(2,1)}, bf16[2,128,512]{2,1,0:T(8,128)(2,1)}, f32[16,1536]{1,0:T(8,128)}, f32[16,512]{1,0:T(8,128)}, f32[16,2048...) custom-call(bf16[2,128,512]{2,1,0:T(8,128)(2,1)} %x_ref.1, s32[2,128]{1,0:T(2,128)} %seg_ref.1, ...), custom_call_target="tpu_custom_call" | custom-call | tf_op jit(solution)/shard_map/pallas_call | solution.py:1279
  123.2 2.1 %shard_map.229 = (bf16[2,128,512]{2,1,0:T(8,128)(2,1)}, bf16[2,128,512]{2,1,0:T(8,128)(2,1)}, f32[16,1536]{1,0:T(8,128)}, f32[16,512]{1,0:T(8,128)}, f32[16,2048...) custom-call(bf16[2,128,512]{2,1,0:T(8,128)(2,1)} %get-tuple-element., ...), custom_call_target="tpu_custom_call" | custom-call | tf_op jit(solution)/shard_map/pallas_call | solution.py:1347

commit v4 on v3

--- a/solution.py
+++ b/solution.py
@@ -18,7 +18,19 @@
 BF16 = jnp.bfloat16
 VMEM = pltpu.VMEM
 NEG = -1e30
-MOST = 2
+
+
+def column_of(kind, pair, width):
+    if kind == "q":
+        return 2 * width + pair * LANES
+    first = (pair % 2) * width + (pair // 2) * LANES
+    return first + (width // 2 if kind == "v" else 0)
+
+
+def columns_between(width):
+    for number, kind in enumerate("qkv"):
+        for pair in range(width // LANES):
+            yield number * width + pair * LANES, column_of(kind, pair, width)
 
 
 class Place:
@@ -42,6 +54,19 @@
     def deeper(self, offset):
         return lax.rem(self.z + offset + self.depth, self.depth)
 
+    def bits(self):
+        bit = self.depth // 2
+        while bit:
+            yield bit
+            bit //= 2
+
+    def flipped(self, bits):
+        z = self.z
+        for bit in self.bits():
+            if bits & bit:
+                z = z + bit - 2 * bit * lax.rem(lax.div(self.z, bit), 2)
+        return z
+
     def member(self, slot, part=None):
         part = self.part if part is None else part
         flat = part * GROUP + slot
@@ -103,7 +128,7 @@
 def halves_of(columns):
     if columns < 2 * LANES:
         return ((0, columns, "yx"),)
-    most = max(columns // 2, columns * MOST // 4)
+    most = columns // 2
     return ((0, most, "yx"), (most, columns - most, "xy"))
 
 
@@ -196,20 +221,25 @@
 def halves_of(columns):
     if columns < 2 * LANES:
         return ((0, columns, "yx"),)
-    most = max(columns // 2, columns * MOST // 4)
+    most = columns // 2
     return ((0, most, "yx"), (most, columns - most, "xy"))
 
 
 class TreeGather:
-    COUNT = 13
-
-    def __init__(self, place, src, dst, sems):
+    COUNT = 12
+
+    def __init__(self, place, src, dst, sems, cols=None):
         self.place, self.src, self.dst, self.sems = place, src, dst, sems
-        self.halves = halves_of(dst.shape[-1])
+        self.start, self.width = cols or (0, dst.shape[-1])
+        self.halves = halves_of(self.width)
+        self.cols = pl.ds(self.start, self.width)
+
+    def part(self, *index):
+        return self.dst.at[index + (slice(None), self.cols)]
 
     def cut(self, half, *index):
         start, width, _ = half
-        return self.dst.at[index + (slice(None), pl.ds(start, width))]
+        return self.dst.at[index + (slice(None), pl.ds(self.start + start, width))]
 
     def across(self, half, first):
         place = self.place
@@ -227,23 +257,42 @@
 
     def own(self):
         place = self.place
-        mine = self.dst.at[place.x, place.core, place.z, place.y]
-        return pltpu.make_async_copy(self.src, mine, self.sems.at[0])
+        mine = self.part(place.x, place.core, place.z, place.y)
+        return pltpu.make_async_copy(self.src.at[:, self.cols], mine, self.sems.at[0])
+
+    def send_piece(self, bits, bit):
+        place = self.place
+        piece = self.part(place.x, place.core, place.flipped(bits), place.y)
+        remote(
+            piece if bits else self.src.at[:, self.cols],
+            piece,
+            self.sems.at[1],
+            self.sems.at[11 + (bits | bit)],
+            place.at(z=place.flipped(bit)),
+        ).start()
+
+    def await_piece(self, bits):
+        place = self.place
+        piece = self.part(place.x, place.core, place.flipped(bits), place.y)
+        wait_received(place, piece, self.sems.at[11 + bits])
 
     def start_line(self):
-        place = self.place
-        for offset in range(1, place.depth):
-            remote(
-                self.src,
-                self.dst.at[place.x, place.core, place.z, place.y],
-                self.sems.at[1],
-                self.sems.at[2],
-                place.at(z=place.deeper(offset)),
-            ).start()
+        for bit in self.place.bits():
+            self.send_piece(0, bit)
         self.own().start()
 
+    def start_step(self):
+        known = [0]
+        for bit in self.place.bits():
+            for bits in known[1:]:
+                self.send_piece(bits, bit)
+            known += [bits | bit for bits in known]
+            if bit > 1:
+                for bits in known[len(known) // 2 :]:
+                    self.await_piece(bits)
+
     def lines(self):
-        return self.dst.at[0, 0, pl.ds(0, self.place.depth - 1), 0]
+        return self.part(0, 0, pl.ds(0, self.place.depth - 1), 0)
 
     def exchange(self, number, first):
         place, half = self.place, self.halves[number]
@@ -254,7 +303,7 @@
             mine,
             mine,
             self.sems.at[3 + base + number],
-            self.sems.at[9 + base + number],
+            self.sems.at[8 + base + number],
             place.at(x=x, y=y),
         )
 
@@ -262,22 +311,23 @@
         half = self.halves[number]
         x, y = self.across(half, first)
         region = self.region(half, first, self.place.core, x, y)
-        wait_received(self.place, region, self.sems.at[(9 if first else 11) + number])
+        wait_received(self.place, region, self.sems.at[(8 if first else 10) + number])
         return region
 
     def hand(self, region):
         place = self.place
         remote(
-            region, region, self.sems.at[7], self.sems.at[8], place.at(core=1 - place.core)
+            region, region, self.sems.at[7], self.sems.at[2], place.at(core=1 - place.core)
         ).start()
 
     def start_first(self):
         place = self.place
         self.own().wait()
-        wait_received(place, self.lines(), self.sems.at[2])
+        for bits in range(1, place.depth, 2):
+            self.await_piece(bits)
         for number in range(len(self.halves)):
             self.exchange(number, True).start()
-        self.hand(self.dst.at[place.x, place.core, slice(None), place.y])
+        self.hand(self.part(place.x, place.core, slice(None), place.y))
 
     def start_second(self):
         for number in range(len(self.halves)):
@@ -290,21 +340,26 @@
             self.hand(self.received(number, False))
 
     def finish(self):
-        wait_received(self.place, self.dst.at[:, 1 - self.place.core], self.sems.at[8])
+        every = slice(None)
+        region = self.part(every, 1 - self.place.core, every, every)
+        wait_received(self.place, region, self.sems.at[2])
 
     def drain(self):
         for number in range(len(self.halves)):
             self.exchange(number, True).wait_send()
             self.exchange(number, False).wait_send()
         wait_sent(self.place, self.lines(), self.sems.at[1])
-        wait_sent(self.place, self.dst.at[:, 0], self.sems.at[7])
+        every = slice(None)
+        wait_sent(self.place, self.part(every, 0, every, every), self.sems.at[7])
 
 
 class Reduce:
     COUNT = 8
 
-    def __init__(self, place, part, out, rc, total, rn, rz, sems):
-        self.place, self.part, self.out = place, part, out
+    def __init__(self, place, part, out, rc, total, rn, rz, sems, cols=None):
+        self.place, self.part = place, part
+        self.cols = pl.ds(*(cols or (0, part.shape[-1])))
+        self.out = out.at[:, self.cols]
         self.rc, self.total, self.rn, self.rz, self.sems = rc, total, rn, rz, sems
 
     @staticmethod
@@ -324,7 +379,7 @@
     def core(self):
         place = self.place
         return remote(
-            self.part.at[:, 1 - place.core],
+            self.part.at[:, 1 - place.core, :, :, :, self.cols],
             self.rc,
             self.sems.at[0],
             self.sems.at[1],
@@ -357,9 +412,7 @@
 
     def add_core(self, x, z, y):
         place = self.place
-        self.total[x, z, y] = (
-            self.part[x, place.core, z, y].astype(F32) + self.rc[x, z, y].astype(F32)
-        ).astype(self.total.dtype)
+        self.total[x, z, y] = self.part[x, place.core, z, y, :, self.cols] + self.rc[x, z, y]
 
     def start_columns(self):
         place = self.place
@@ -409,12 +462,14 @@
 class TreeReduce:
     COUNT = 12
 
-    def __init__(self, place, part, out, rc, total, ra, rb, fa, fb, rz, sems):
-        self.place, self.part, self.out = place, part, out
+    def __init__(self, place, part, out, rc, total, ra, rb, fa, fb, rz, sems, cols=None):
+        self.place, self.part = place, part
+        self.cols = pl.ds(*(cols or (0, part.shape[-1])))
+        self.out = out.at[:, self.cols]
         self.rc, self.total, self.rz = rc, total, rz
         self.second, self.first = (ra, rb), (fa, fb)
         self.sems = sems
-        self.halves = halves_of(part.shape[-1])
+        self.halves = halves_of(total.shape[-1])
 
     @staticmethod
     def scratch(depth, rows, cols, dtype):
@@ -427,11 +482,10 @@
             VMEM((depth, rows, wide), dtype),
             VMEM((depth, rows, narrow), dtype),
             VMEM((depth - 1, rows, cols), dtype),
-            pltpu.SemaphoreType.DMA((TreeReduce.COUNT,)),
+            pltpu.SemaphoreType.DMA((TreeReduce.COUNT + depth - 1,)),
         ]
 
-    core, line, start_core, add_core = Reduce.core, Reduce.line, Reduce.start_core, Reduce.add_core
-    finish = Reduce.finish
+    core, start_core, add_core = Reduce.core, Reduce.start_core, Reduce.add_core
 
     def cut(self, half, *index):
         start, width, _ = half
@@ -471,9 +525,7 @@
             self.exchange(number, True).start()
 
     def accumulate(self, index, value):
-        self.total[index] = (self.total[index].astype(F32) + value.astype(F32)).astype(
-            self.total.dtype
-        )
+        self.total[index] = self.total[index] + value
 
     def start_first(self):
         place = self.place
@@ -503,8 +555,39 @@
                 return carry
 
             lax.fori_loop(0, place.depth, add, 0)
-        for offset in range(1, place.depth):
-            self.line(offset).start()
+        self.send_over(1)
+
+    def offsets(self, bit):
+        return range(bit, self.place.depth, 2 * bit)
+
+    def send_over(self, bit):
+        place = self.place
+        for bits in self.offsets(bit):
+            remote(
+                self.total.at[place.x, place.flipped(bits), place.y],
+                self.rz.at[bits - 1],
+                self.sems.at[6],
+                self.sems.at[11 + bits],
+                place.at(z=place.flipped(bit)),
+            ).start()
+
+    def start_step(self):
+        place = self.place
+        bit = 1
+        while 2 * bit < place.depth:
+            for bits in self.offsets(bit):
+                wait_received(place, self.rz.at[bits - 1], self.sems.at[11 + bits])
+                here = (place.x, place.flipped(bits - bit), place.y)
+                self.total[here] = self.total[here] + self.rz[bits - 1]
+            bit *= 2
+            self.send_over(bit)
+
+    def finish(self):
+        place = self.place
+        last = place.depth // 2
+        wait_received(place, self.rz.at[last - 1], self.sems.at[11 + last])
+        total = self.total[place.x, place.z, place.y].astype(F32)
+        self.out[...] = total + self.rz[last - 1].astype(F32)
 
     def drain(self):
         self.core().wait_send()
@@ -603,9 +686,14 @@
     dos,
     doct_ref,
     act_s,
+    slope_s,
     gpre_s,
     gres_ref,
-    acc,
+    q_rows_s,
+    d_rows_s,
+    delta_ref,
+    dq_s,
+    grad_s,
     dqt_ref,
     dkv_sum,
     dq_in,
@@ -613,6 +701,8 @@
     halo_out,
     halo_in,
     gp,
+    win_s,
+    r_win_s,
     partials,
 ):
     place = Place(blocks)
@@ -684,6 +774,8 @@
     numbers = seg_ref[...].astype(F32)
     tile[...] = jnp.where(row == 0, numbers[0:1], numbers[1:2]).astype(BF16)
     segs[window + place.slot] = tile[...]
+    for source, target in columns_between(win_ref.shape[-1] // 3):
+        win_s[:, target : target + LANES] = win_ref[:, source : source + LANES]
     aux_ref[...] = jnp.zeros_like(aux_ref)
     for index, ref in enumerate(bias_refs):
         aux_ref[index : index + 1, 0 : ref.shape[-1]] = ref[...].astype(F32).reshape(1, ref.shape[-1])
@@ -695,29 +787,40 @@
 
     plan = (
         (aux_ref, gaux, None),
-        (win_ref, gwin, (width, 2 * width)),
-        (win_ref, gwin, (0, width)),
+        (win_s, gwin, (0, width)),
+        (win_s, gwin, (width, width)),
+        (win_s, gwin, (2 * width, width)),
     )
-    g_aux, g_kv, g_q = [
+    g_aux, g_even, g_odd, g_q = [
         Gather(place, src, dst, sems, cols)
-        for (src, dst, cols), sems in zip(plan, gather_sems[:3])
+        for (src, dst, cols), sems in zip(plan, gather_sems[:4])
     ]
+    plan = (
+        (wo_ref, gwo, None),
+        (wup_ref, gwup, (0, hidden // 2)),
+        (wup_ref, gwup, (hidden // 2, hidden // 2)),
+        (wdown_ref, gwdown, (0, width // 2)),
+        (wdown_ref, gwdown, (width // 2, width // 2)),
+    )
     rest = [
-        TreeGather(place, src, dst, sems)
-        for (src, dst), sems in zip(
-            ((wo_ref, gwo), (wup_ref, gwup), (wdown_ref, gwdown)), gather_sems[3:]
-        )
+        TreeGather(place, src, dst, sems, cols)
+        for (src, dst, cols), sems in zip(plan, gather_sems[4:])
     ]
-    g_kv.start_line()
+    g_wo, g_up0, g_up1, g_down0, g_down1 = rest
+    g_even.start_line()
     g_aux.start_line()
+    g_odd.start_line()
     g_q.start_line()
     loop(lambda offset: seg_copy(offset).start())
-    g_kv.start_columns()
+    g_wo.start_line()
+    g_up0.start_line()
+    g_up1.start_line()
+    g_even.start_columns()
     g_aux.start_columns()
+    g_odd.start_columns()
     g_q.start_columns()
-    for gather in rest:
-        gather.start_line()
-
+    g_down0.start_line()
+    g_down1.start_line()
     wait_received(place, segs.at[pl.ds(0, GROUP - 1)], seg_sems.at[1])
 
     def seg_halo(part):
@@ -735,11 +838,14 @@
         def _():
             seg_halo(place.part + 1).start()
 
-    g_kv.start_hands()
+    g_even.start_hands()
+    g_wo.start_step()
+    g_up0.start_step()
+    g_up1.start_step()
     g_aux.start_hands()
-    g_q.start_hands()
+    g_odd.start_hands()
     g_aux.finish()
-    g_kv.finish()
+    g_even.finish()
 
     aux = gaux[...].reshape(devices * 8, LANES)
     bias_q = spread_bias(aux, "query", per, width)
@@ -748,37 +854,59 @@
     low_lane = iota((LANES, LANES), 1) < HD
     wide = 2 * LANES
 
-    def column(kind, t):
-        weight = gwin[:, :, :, :, :, pl.ds(kind * width + t * wide, wide)]
-        return dot(tokens, weight.reshape(width, wide))
-
-    def corners(t):
+    def column(at):
+        return dot(tokens, gwin[:, :, :, :, :, pl.ds(at, wide)].reshape(width, wide))
+
+    def corners():
         for s in range(2):
             for u in range(2):
                 at = (slice(s * LANES, (s + 1) * LANES), slice(u * LANES, (u + 1) * LANES))
-                yield s * HEADS + t * 4 + u * 2, at
-
-    for t in range(width // wide):
-        k = column(1, t).astype(BF16).astype(F32)
-        v = (column(2, t) + bias_v[:, t * wide : (t + 1) * wide]).astype(BF16).astype(F32)
-        for head, at in corners(t):
-            k_at, v_at = k[at], v[at]
+                yield s, u, at
+
+    def project_pairs(odd):
+        k = column(column_of("k", odd, width)).astype(BF16).astype(F32)
+        v = column(column_of("v", odd, width))
+        for s, u, at in corners():
+            pair = odd + 2 * u
+            head = s * HEADS + 2 * pair
+            k_at = k[at]
+            v_at = (v[at] + bias_v[:, pair * LANES : (pair + 1) * LANES]).astype(BF16).astype(F32)
             ks[head] = jnp.where(low_lane, k_at, pltpu.roll(v_at, HD, 1)).astype(BF16)
             ks[head + 1] = jnp.where(low_lane, pltpu.roll(k_at, HD, 1), v_at).astype(BF16)
-    loop(lambda offset: k_copy(offset).start())
+
+        def start(offset):
+            head = lax.rem(place.other_slot(offset), HEADS)
+
+            @pl.when(lax.rem(lax.div(head, 2), 2) == odd)
+            def _():
+                k_copy(offset).start()
+
+        loop(start)
+
+    project_pairs(0)
+    g_q.start_hands()
+    g_wo.start_first()
+    g_up0.start_first()
+    g_up1.start_first()
+    g_down0.start_step()
+    g_down1.start_step()
+    g_odd.finish()
+    project_pairs(1)
     kv_ref[window + place.slot] = ks[place.slot]
     g_q.finish()
     for t in range(width // wide):
-        q = (column(0, t) + bias_q[:, t * wide : (t + 1) * wide]).astype(BF16).astype(F32) * 0.125
-        for head, at in corners(t):
+        q = column(column_of("q", 2 * t, width)) + bias_q[:, t * wide : (t + 1) * wide]
+        q = q.astype(BF16).astype(F32) * 0.125
+        for s, u, at in corners():
             turned = q[at].T.astype(BF16)
+            head = s * HEADS + 4 * t + 2 * u
             qs[head] = turned[:HD]
             qs[head + 1] = turned[HD:]
     loop(lambda offset: q_copy(offset).start())
     qt_ref[place.slot] = qs[place.slot]
-
-    for gather in rest:
-        gather.start_first()
+    g_wo.start_second()
+    g_up0.start_second()
+    g_up1.start_second()
 
     if parts > 1:
 
@@ -802,9 +930,8 @@
         count = jnp.sum(count, axis=1, keepdims=True)
         start = start + jnp.where(own >= number, count, 0.0)
     starts_ref[...] = start.astype(jnp.int32)
-
-    for gather in rest:
-        gather.start_second()
+    g_down0.start_first()
+    g_down1.start_first()
 
     def kv_halo(number, part):
         return remote(
@@ -829,8 +956,12 @@
         k_copy(offset, True).wait_recv()
         arrived(place.other_slot(-offset))
 
-    loop(kv_wait)
+    loop(kv_wait, 1, GROUP // 2)
+    loop(kv_wait, GROUP // 2, GROUP)
     all_here(qt_ref, q_sems)
+    g_wo.start_hands()
+    g_up0.start_hands()
+    g_up1.start_hands()
 
     many = window + 2
     older = window * LANES
@@ -851,11 +982,17 @@
     blank = jnp.zeros((HD, BLOCK), BF16)
 
     def attend(step, carry):
-        for number, gather in enumerate(rest):
-
-            @pl.when(step == 1 + 2 * number)
-            def _():
-                gather.start_hands()
+        @pl.when(step == 1)
+        def _():
+            g_down0.start_second()
+
+        @pl.when(step == 3)
+        def _():
+            g_down1.start_second()
+
+        @pl.when(step == 6)
+        def _():
+            g_down0.start_hands()
 
         if parts > 1:
 
@@ -917,8 +1054,8 @@
     wide_tokens = tokens.astype(F32)
     grads = grad_ref[...].reshape(rows, width).astype(F32)
     grad_ffn = (a1 * grads).astype(BF16)
-    for gather in rest:
-        gather.finish()
+    g_down1.start_hands()
+    g_wo.finish()
     full_out = gwo[...].reshape(width, width)
 
     all_here(mixed_t, o_sems)
@@ -932,21 +1069,25 @@
     ffn = jnp.zeros((rows, width), F32) + bias_down
     grad_res = grads
     tile_up = 512
+    g_up0.finish()
+    g_up1.finish()
     whole_up = gwup.reshape(width, hidden)
     whole_down = gwdown.reshape(hidden, width)
     for t in range(hidden // tile_up):
         cols = pl.ds(t * tile_up, tile_up)
-        w_up = whole_up[:, cols]
+        pre = dot(hidden_in, whole_up[:, cols]) + bias_up[:, t * tile_up : (t + 1) * tile_up]
+        phi = 0.5 * (1.0 + lax.erf(pre * (1.0 / math.sqrt(2.0))))
+        act_s[:, cols] = (pre * phi).astype(BF16)
+        slope = phi + pre * jnp.exp(-0.5 * pre * pre) * (1.0 / math.sqrt(2.0 * math.pi))
+        slope_s[:, cols] = slope
+    g_down0.finish()
+    g_down1.finish()
+    for t in range(hidden // tile_up):
+        cols = pl.ds(t * tile_up, tile_up)
         w_down = whole_down[cols, :]
-        pre = dot(hidden_in, w_up) + bias_up[:, t * tile_up : (t + 1) * tile_up]
-        phi = 0.5 * (1.0 + lax.erf(pre * (1.0 / math.sqrt(2.0))))
-        act = (pre * phi).astype(BF16)
-        act_s[:, cols] = act
-        ffn = ffn + dot(act, w_down)
-        slope = phi + pre * jnp.exp(-0.5 * pre * pre) * (1.0 / math.sqrt(2.0 * math.pi))
-        gpre = (dot_nt(grad_ffn, w_down) * slope).astype(BF16)
+        gpre = (dot_nt(grad_ffn, w_down) * slope_s[:, cols]).astype(BF16)
         gpre_s[:, cols] = gpre
-        grad_res = grad_res + dot_nt(gpre, w_up)
+        grad_res = grad_res + dot_nt(gpre, whole_up[:, cols])
     gres_ref[...] = grad_res
     grad_branch = (a0 * grad_res).astype(BF16)
     grad_mixed = dot_nt(grad_branch, full_out).astype(BF16).astype(F32)
@@ -956,38 +1097,50 @@
     loop(lambda offset: d_copy(offset).start())
     doct_ref[place.slot] = dos[place.slot]
 
-    kinds = (TreeReduce, TreeReduce, TreeReduce, Reduce, Reduce, Reduce)
-    t_out, t_up, t_down, t_kv, t_q, t_aux = [
-        kind(place, part, out, *scratch)
-        for kind, (part, out), scratch in zip(
-            kinds,
-            (
-                (p_out, r_out),
-                (p_up, r_up),
-                (p_down, r_down),
-                (p_win[1], r_win.at[:, pl.ds(width, 2 * width)]),
-                (p_win[0], r_win.at[:, pl.ds(0, width)]),
-                (p_aux, r_aux),
-            ),
-            trees,
-        )
+    sources = [
+        (TreeReduce, p_out, r_out, None),
+        (TreeReduce, p_up, r_up, (0, hidden // 2)),
+        (TreeReduce, p_up, r_up, (hidden // 2, hidden // 2)),
+        (TreeReduce, p_down, r_down, (0, width // 2)),
+        (TreeReduce, p_down, r_down, (width // 2, width // 2)),
+        (Reduce, p_win, r_win_s, (0, width)),
+        (Reduce, p_win, r_win_s, (width, width)),
+        (Reduce, p_win, r_win_s, (2 * width, width)),
+        (Reduce, p_aux, r_aux, None),
+    ]
+    t_out, t_up0, t_up1, t_down0, t_down1, t_even, t_odd, t_q, t_aux = [
+        kind(place, part, out, *scratch, cols)
+        for (kind, part, out, cols), scratch in zip(sources, trees)
     ]
     lead = (2, 2, depth, 2)
-    for t in range(hidden // tile_up):
-        cols = pl.ds(t * tile_up, tile_up)
-        block = dot_tn(act_s[:, cols], grad_ffn).astype(BF16)
-        p_down.reshape(hidden, width)[cols, :] = block
-    t_down.start_core()
-    for t in range(hidden // tile_up):
-        cols = pl.ds(t * tile_up, tile_up)
-        block = dot_tn(hidden_in, gpre_s[:, cols]).astype(BF16)
-        p_up.reshape(width, hidden)[:, cols] = block
-    t_up.start_core()
+    flat_down, flat_up = p_down.reshape(hidden, width), p_up.reshape(width, hidden)
+    for half, tree in enumerate((t_down0, t_down1)):
+        at = slice(half * width // 2, (half + 1) * width // 2)
+        for t in range(hidden // tile_up):
+            cols = pl.ds(t * tile_up, tile_up)
+            flat_down[cols, at] = dot_tn(act_s[:, cols], grad_ffn[:, at]).astype(BF16)
+        tree.start_core()
+    hidden_turned = hidden_in.T
+
+    def up_part(half, tree):
+        for t in range(hidden // tile_up // 2):
+            cols = pl.ds(half * hidden // 2 + t * tile_up, tile_up)
+            flat_up[:, cols] = dot(hidden_turned, gpre_s[:, cols]).astype(BF16)
+        tree.start_core()
+
+    up_part(0, t_up0)
+    t_down0.start_second()
+    up_part(1, t_up1)
+    t_down1.start_second()
     p_out.reshape(width, width)[...] = dot(
         jnp.concatenate([mixed_turned[0], mixed_turned[1]], axis=1), grad_branch
     ).astype(BF16)
     t_out.start_core()
-
+    t_up0.start_second()
+
+    for t in range(hidden // tile_up):
+        cols = pl.ds(t * tile_up, tile_up)
+        ffn = ffn + dot(act_s[:, cols], whole_down[cols, :])
     ffn_term = a1 * ffn
     stream = residual + ffn_term
     out_ref[...] = stream.astype(BF16).reshape(2, LANES, width)
@@ -1017,159 +1170,190 @@
     )
     p_aux[...] = folded.reshape(*lead, 8, LANES)
 
-    early = (t_down, t_up, t_out)
+    t_up1.start_second()
+    early = (t_down0, t_down1, t_up0, t_up1, t_out)
     low_block = iota((BLOCK, LANES), 1) < HD
 
-    def clear(number):
-        acc[number] = jnp.zeros((LANES, LANES), F32)
-
-    loop(clear, 0, span)
-
-    def back_halo(part):
+    def clear(m):
+        dq_s[m] = jnp.zeros((HD, BLOCK), F32)
+
+    loop(clear, 0, pairs_of_chunks)
+
+    def back_halo(u, part):
+        pair = pl.ds(2 * u, 2)
         return remote(
-            halo_out, halo_in, back_hs.at[0], back_hr.at[0], place.member(place.slot, part)
+            halo_out.at[pair],
+            halo_in.at[pair],
+            back_hs.at[u],
+            back_hr.at[u],
+            place.member(place.slot, part),
         )
 
-    def settle(number):
-        dkv_sum[number] = acc[window + number].astype(BF16)
-
-    def attend_back(m, carry):
-        for number, tree in enumerate(early):
-
-            @pl.when(m == 1 + number)
-            def _():
-                tree.start_second()
-
+    def ready(m):
         await_from(d_copy, 2 * m)
         await_from(d_copy, 2 * m + 1)
         qt, dt = two(qt_ref, 2 * m), two(doct_ref, 2 * m)
-        q_wide = jnp.concatenate([qt, blank], axis=0)
-        d_wide = jnp.concatenate([blank, dt], axis=0)
         both = jnp.concatenate([qt, dt], axis=0).astype(F32).T
-        q_and_d = jnp.concatenate(
-            [jnp.where(low_block, both, 0.0), jnp.where(low_block, 0.0, both)], axis=0
-        ).astype(BF16)
-        start = q_rows_of(starts_ref, m)
-        lse = q_rows_of(lse_ref, m)
+        here = pl.ds(2 * m, 2)
+        q_rows_s[here] = jnp.where(low_block, both, 0.0).astype(BF16).reshape(2, LANES, LANES)
+        d_rows_s[here] = jnp.where(low_block, 0.0, both).astype(BF16).reshape(2, LANES, LANES)
         delta = jnp.sum(dt.astype(F32) * two(of_ref, 2 * m), axis=0, keepdims=True)
-        base = m * BLOCK
-        q_place = base + older + iota((1, BLOCK), 1)
-        grad_scores = []
-        for block in range(reach + 1):
-            here = pl.ds(2 * (m + block), 2)
-            kv = kv_ref[here].reshape(BLOCK, LANES)
-            scores = masked(dot(kv, q_wide), start, q_place, block, base)
-            probs = jnp.exp(scores - lse)
-            grad_score = (probs * (dot(kv, d_wide) - delta)).astype(BF16)
-            grad_scores.append(grad_score)
-            both_scores = jnp.concatenate([grad_score, probs.astype(BF16)], axis=1)
-            acc[here] += dot(both_scores, q_and_d).reshape(2, LANES, LANES)
-        dq = dot(turned_window(m)[:HD], jnp.concatenate(grad_scores, axis=0)) * 0.125
+        delta_ref[pl.ds(2 * m, 1)] = delta[:, :LANES]
+        delta_ref[pl.ds(2 * m + 1, 1)] = delta[:, LANES:]
+
+    def key_block(u, low, count):
+        kv = kv_ref[pl.ds(2 * u, 2)].reshape(BLOCK, LANES)
+        keys_turned = two(kvt, 2 * u)[:HD]
+        k_place = u * BLOCK + iota((BLOCK, BLOCK), 0)
+        grad = jnp.zeros((BLOCK, LANES), F32)
+        for number in range(count):
+            m = low + number
+            here = pl.ds(2 * m, 2)
+            q_wide = jnp.concatenate([two(qt_ref, 2 * m), blank], axis=0)
+            d_wide = jnp.concatenate([blank, two(doct_ref, 2 * m)], axis=0)
+            visible = k_place >= q_rows_of(starts_ref, m)
+            if number == 0:
+                visible = visible & (k_place <= m * BLOCK + older + iota((1, BLOCK), 1))
+            scores = jnp.where(visible, dot(kv, q_wide), NEG)
+            probs = jnp.exp(scores - q_rows_of(lse_ref, m))
+            grad_scores = (probs * (dot(kv, d_wide) - q_rows_of(delta_ref, m))).astype(BF16)
+            grad = grad + dot(grad_scores, q_rows_s[here].reshape(BLOCK, LANES))
+            grad = grad + dot(probs.astype(BF16), d_rows_s[here].reshape(BLOCK, LANES))
+            dq_s[m] += dot(keys_turned, grad_scores)
+        grad_s[...] = grad
+
+    def settle(u):
+        pair = u - reach
+        if parts > 1:
+            late = pair - (pairs_of_chunks - reach)
+
+            @pl.when((late >= 0) & (place.part < parts - 1))
+            def _():
+                back_halo(late, place.part + 1).wait_recv()
+                grad_s[...] += halo_in[pl.ds(2 * late, 2)].reshape(BLOCK, LANES).astype(F32)
+
+        dkv_sum[pl.ds(2 * pair, 2)] = grad_s[...].astype(BF16).reshape(2, LANES, LANES)
+        dq = dq_s[pair] * 0.125
         for side in range(2):
-            dqt_ref[2 * m + side] = dq[:, side * LANES : (side + 1) * LANES].astype(BF16)
-            send_to(dq_copy, 2 * m + side)
+            send_to(dkv_copy, 2 * pair + side)
+            dqt_ref[2 * pair + side] = dq[:, side * LANES : (side + 1) * LANES].astype(BF16)
+            send_to(dq_copy, 2 * pair + side)
+
+    def attend_back(u, carry):
+        @pl.when(u == 0)
+        def _():
+            t_out.start_second()
+
+        @pl.when(u == 5)
+        def _():
+            t_down0.start_first()
+
+        @pl.when(u == 7)
+        def _():
+            t_down1.start_first()
+
+        @pl.when(u < pairs_of_chunks)
+        def _():
+            ready(u)
+
+        low = jnp.maximum(u - reach, 0)
+        count = jnp.minimum(u, pairs_of_chunks - 1) - low + 1
+        needed = (u >= reach) | (place.part > 0)
+        for number in range(1, reach + 2):
+
+            @pl.when(needed & (count == number))
+            def _():
+                key_block(u, low, number)
+
         if parts > 1:
 
-            @pl.when((m == reach - 1) & (place.part > 0))
+            @pl.when((u < reach) & (place.part > 0))
             def _():
-                def put(number):
-                    halo_out[number] = acc[number].astype(BF16)
-
-                loop(put, 0, window)
-                back_halo(place.part - 1).start()
-
-        if free:
-
-            @pl.when(m >= reach)
-            def _():
-                for side in range(2):
-                    chunk = 2 * (m - reach) + side
-                    settle(chunk)
-                    send_to(dkv_copy, chunk)
+                halo_out[pl.ds(2 * u, 2)] = grad_s[...].astype(BF16).reshape(2, LANES, LANES)
+                back_halo(u, place.part - 1).start()
+
+        @pl.when(u >= reach)
+        def _():
+            settle(u)
 
         return carry
 
-    lax.fori_loop(0, pairs_of_chunks, attend_back, 0)
+    lax.fori_loop(0, reach + pairs_of_chunks, attend_back, 0)
     dq_in[place.slot] = dqt_ref[place.slot]
-    loop(settle, GROUP - window, GROUP)
-    if parts > 1:
-
-        @pl.when(place.part < parts - 1)
-        def _():
-            back_halo(place.part + 1).wait_recv()
-
-            def add(number):
-                chunk = GROUP - window + number
-                total = acc[window + chunk] + halo_in[number].astype(F32)
-                dkv_sum[chunk] = total.astype(BF16)
-
-            loop(add, 0, window)
-
-    def late(offset):
-        @pl.when(place.other_slot(offset) >= GROUP - window)
-        def _():
-            dkv_copy(offset).start()
-
-    loop(late)
+    t_up0.start_first()
+    t_up1.start_first()
+    t_out.start_first()
     dkv_in[place.slot] = dkv_sum[place.slot]
-    for tree in early:
-        tree.start_first()
+    t_down0.start_line()
+    t_down1.start_line()
+
+    def weight_part(number):
+        part = dot(tokens_turned, gp[:, number * width : (number + 1) * width]).astype(BF16)
+        p_win[:, :, :, :, :, number * width : (number + 1) * width] = part.reshape(
+            *lead, width // devices, width
+        )
+
+    def token_part(number):
+        cols = slice(number * width, (number + 1) * width)
+        return dot_nt(gp[:, cols], full_in[:, cols])
 
     tokens_turned = tokens.T
+    full_in = gwin.reshape(width, 3 * width)
     all_here(dq_in, dq_sems)
     for s in range(2):
         turned = dq_in[pl.ds(s * HEADS, HEADS)].reshape(width, LANES).astype(F32)
-        gp[s * LANES : (s + 1) * LANES, 0:width] = turned.T.astype(BF16)
-    query_row = jnp.sum(gp[:, 0:width].astype(F32), axis=0, keepdims=True)
-    p_win[0][...] = (
-        dot(tokens_turned, gp[:, 0:width])
-        .astype(BF16)
-        .reshape(*lead, width // devices, width)
-    )
+        gp[s * LANES : (s + 1) * LANES, 2 * width :] = turned.T.astype(BF16)
+    weight_part(2)
     t_q.start_core()
-    full_in = gwin.reshape(width, 3 * width)
-    gx = gres_ref[...] + dot_nt(gp[:, 0:width], full_in[:, 0:width])
+    query_row = jnp.sum(gp[:, 2 * width :].astype(F32), axis=0, keepdims=True)
+    gx = gres_ref[...] + token_part(2)
+    t_up0.start_line()
+    t_up1.start_line()
+    t_out.start_line()
     t_q.start_columns()
 
     all_here(dkv_in, dkv_sems)
-    for s in range(2):
-        at_rows = slice(s * LANES, (s + 1) * LANES)
-        for pair in range(HEADS // 2):
-            even = dkv_in[s * HEADS + 2 * pair].astype(F32)
-            odd = dkv_in[s * HEADS + 2 * pair + 1].astype(F32)
-            keys = jnp.where(low_lane, even, pltpu.roll(odd, HD, 1))
-            values = jnp.where(low_lane, pltpu.roll(even, HD, 1), odd)
-            at = width + pair * LANES
-            gp[at_rows, at : at + LANES] = keys.astype(BF16)
-            gp[at_rows, width + at : width + at + LANES] = values.astype(BF16)
-    for t in range(2):
-        part = dot(tokens_turned, gp[:, (1 + t) * width : (2 + t) * width]).astype(BF16)
-        p_win[1][:, :, :, :, :, t * width : (t + 1) * width] = part.reshape(
-            *lead, width // devices, width
-        )
-    t_kv.start_core()
-    for tree in early:
-        tree.start_line()
-    value_row = jnp.sum(gp[:, 2 * width :].astype(F32), axis=0, keepdims=True)
+    for number in range(2):
+        for s in range(2):
+            at_rows = slice(s * LANES, (s + 1) * LANES)
+            for pair in range(number, HEADS // 2, 2):
+                even = dkv_in[s * HEADS + 2 * pair].astype(F32)
+                odd = dkv_in[s * HEADS + 2 * pair + 1].astype(F32)
+                keys = jnp.where(low_lane, even, pltpu.roll(odd, HD, 1))
+                values = jnp.where(low_lane, pltpu.roll(even, HD, 1), odd)
+                at = column_of("k", pair, width)
+                gp[at_rows, at : at + LANES] = keys.astype(BF16)
+                at = column_of("v", pair, width)
+                gp[at_rows, at : at + LANES] = values.astype(BF16)
+        weight_part(number)
+        (t_even, t_odd)[number].start_core()
+    value_rows = []
+    for pair in range(HEADS // 2):
+        at = column_of("v", pair, width)
+        value_rows.append(jnp.sum(gp[:, at : at + LANES].astype(F32), axis=0, keepdims=True))
     folded = fold_bias(query_row, devices * 8, "query", per) + fold_bias(
-        value_row, devices * 8, "value", per
+        jnp.concatenate(value_rows, axis=1), devices * 8, "value", per
     )
     p_aux[...] += folded.reshape(*lead, 8, LANES)
     t_aux.start_core()
+    t_even.start_columns()
     t_q.start_line()
-    t_kv.start_columns()
+    t_odd.start_columns()
     t_aux.start_columns()
-    for t in range(1, 3):
-        cols = slice(t * width, (t + 1) * width)
-        gx = gx + dot_nt(gp[:, cols], full_in[:, cols])
+    t_down0.start_step()
+    t_down1.start_step()
+    t_up0.start_step()
+    t_up1.start_step()
+    t_out.start_step()
+    gx = gx + token_part(0) + token_part(1)
     gx_ref[...] = gx.astype(BF16).reshape(2, LANES, width)
+    t_even.start_line()
     t_aux.start_line()
-    t_kv.start_line()
-    for tree in early:
+    t_odd.start_line()
+    for tree in early + (t_q, t_even, t_aux, t_odd):
         tree.finish()
-    t_q.finish()
-    t_aux.finish()
-    t_kv.finish()
+    for source, target in columns_between(width):
+        r_win[:, source : source + LANES] = r_win_s[:, target : target + LANES]
 
     all_sent(segs, seg_sems)
     all_sent(ks, k_sems)
@@ -1186,11 +1370,11 @@
 
         @pl.when(place.part > 0)
         def _():
-            back_halo(place.part - 1).wait_send()
-
-    for gather in (g_aux, g_kv, g_q, *rest):
+            loop(lambda u: back_halo(u, place.part - 1).wait_send(), 0, reach)
+
+    for gather in (g_aux, g_even, g_odd, g_q, *rest):
         gather.drain()
-    for tree in early + (t_q, t_kv, t_aux):
+    for tree in early + (t_q, t_even, t_odd, t_aux):
         tree.drain()
 
 
@@ -1259,14 +1443,7 @@
     dma = pltpu.SemaphoreType.DMA
     lead = (2, 2, depth, 2)
     in_rows, up_rows = input_weight.shape[0], down_weight.shape[0]
-    reduced = (
-        (in_rows, width, BF16),
-        (in_rows, hidden, BF16),
-        (up_rows, width, BF16),
-        (in_rows, 2 * width, BF16),
-        (in_rows, width, BF16),
-        (8, LANES, F32),
-    )
+    tree_parts = ((in_rows, width),) + ((in_rows, hidden // 2),) * 2 + ((up_rows, width // 2),) * 2
     tokens = seqs * rows
     results = (
         shape(seqs, rows, width),
@@ -1289,11 +1466,12 @@
                 VMEM((*lead, up_rows, width), BF16),
                 VMEM((*lead, 8, LANES), F32),
             ],
-            [dma((Gather.COUNT,))] * 3 + [dma((TreeGather.COUNT,))] * 3,
-            [TreeReduce.scratch(depth, *sizes) for sizes in reduced[:3]]
-            + [Reduce.scratch(depth, *sizes) for sizes in reduced[3:]],
+            [dma((Gather.COUNT,))] * 4 + [dma((TreeGather.COUNT + depth - 1,))] * 5,
+            [TreeReduce.scratch(depth, *sizes, BF16) for sizes in tree_parts]
+            + [Reduce.scratch(depth, in_rows, width, BF16)] * 3
+            + [Reduce.scratch(depth, 8, LANES, F32)],
             [dma((2,)), dma((GROUP,)), dma((2,)), dma((2,)), dma((GROUP,)), dma((2,)), dma((2,))],
-            [dma((1,)), dma((1,)), dma((window,)), dma((window,)), dma((1,)), dma((1,))],
+            [dma((1,)), dma((1,)), dma((window,)), dma((window,)), dma((window // 2,)), dma((window // 2,))],
             VMEM((span, 16, LANES), BF16),
             VMEM((16, LANES), BF16),
             VMEM((8, LANES), F32),
@@ -1310,9 +1488,14 @@
             VMEM((GROUP, HD, LANES), BF16),
             VMEM((GROUP, HD, LANES), BF16),
             VMEM((tokens, hidden), BF16),
+            VMEM((tokens, hidden), F32),
             VMEM((tokens, hidden), BF16),
             VMEM((tokens, width), F32),
-            VMEM((span, LANES, LANES), F32),
+            VMEM((GROUP, LANES, LANES), BF16),
+            VMEM((GROUP, LANES, LANES), BF16),
+            VMEM((GROUP, LANES), F32),
+            VMEM((GROUP // 2, HD, BLOCK), F32),
+            VMEM((BLOCK, LANES), F32),
             VMEM((GROUP, HD, LANES), BF16),
             VMEM((GROUP, LANES, LANES), BF16),
             VMEM((GROUP, HD, LANES), BF16),
@@ -1320,11 +1503,10 @@
             VMEM((window, LANES, LANES), BF16),
             VMEM((window, LANES, LANES), BF16),
             VMEM((tokens, 3 * width), BF16),
+            VMEM((in_rows, 3 * width), BF16),
+            VMEM((in_rows, 3 * width), F32),
             [
-                [
-                    VMEM((*lead, in_rows, width), BF16),
-                    VMEM((*lead, in_rows, 2 * width), BF16),
-                ],
+                VMEM((*lead, in_rows, 3 * width), BF16),
                 VMEM((*lead, in_rows, width), BF16),
                 VMEM((*lead, in_rows, hidden), BF16),
                 VMEM((*lead, up_rows, width), BF16),

time: 126 us -> 118 us (0.937)
  Pallas kernels: 125 us -> 117 us
    pallas_call x1, Pallas kernels: 123 us -> 115 us  [local(): call(functools.partial(layer_kernel, blocks, parts, window, docs), result...]
where the time goes in v4:
time: 118 us
  Pallas kernels  117 us (99%)
    pallas_call x1, Pallas kernels, local(): call(functools.partial(layer_kernel, blocks, parts, window, docs), result...  115 us

profile of v4, /device:TPU:0, one launch (start us, length us, event | category | flops | bytes accessed | tf_op | source)
XLA Modules:
  0.0 117.8 jit_solution(3863375035584819348)
XLA Ops:
  0.6 114.8 %shard_map.228 = (bf16[2,128,512]{2,1,0:T(8,128)(2,1)}, bf16[2,128,512]{2,1,0:T(8,128)(2,1)}, f32[16,1536]{1,0:T(8,128)}, f32[16,512]{1,0:T(8,128)}, f32[16,2048...) custom-call(bf16[2,128,512]{2,1,0:T(8,128)(2,1)} %x_ref.1, s32[2,128]{1,0:T(2,128)} %seg_ref.1, ...), custom_call_target="tpu_custom_call" | custom-call | tf_op jit(solution)/shard_map/pallas_call | solution.py:1456
  115.5 2.1 %shard_map.229 = (bf16[2,128,512]{2,1,0:T(8,128)(2,1)}, bf16[2,128,512]{2,1,0:T(8,128)(2,1)}, f32[16,1536]{1,0:T(8,128)}, f32[16,512]{1,0:T(8,128)}, f32[16,2048...) custom-call(bf16[2,128,512]{2,1,0:T(8,128)(2,1)} %get-tuple-element., ...), custom_call_target="tpu_custom_call" | custom-call | tf_op jit(solution)/shard_map/pallas_call | solution.py:1529

commit v5 on v4

--- a/solution.py
+++ b/solution.py
@@ -20,19 +20,6 @@
 NEG = -1e30
 
 
-def column_of(kind, pair, width):
-    if kind == "q":
-        return 2 * width + pair * LANES
-    first = (pair % 2) * width + (pair // 2) * LANES
-    return first + (width // 2 if kind == "v" else 0)
-
-
-def columns_between(width):
-    for number, kind in enumerate("qkv"):
-        for pair in range(width // LANES):
-            yield number * width + pair * LANES, column_of(kind, pair, width)
-
-
 class Place:
     def __init__(self, blocks):
         self.blocks = blocks
@@ -72,6 +59,13 @@
         flat = part * GROUP + slot
         return (lax.div(flat, self.blocks), lax.rem(flat, self.blocks))
 
+    def crossed(self, code):
+        slot = self.slot
+        for bit in (1, 2, 4, 8):
+            if code & bit:
+                slot = slot + bit - 2 * bit * lax.rem(lax.div(self.slot, bit), 2)
+        return slot
+
     def other_slot(self, offset):
         return lax.rem(self.slot + offset + GROUP, GROUP)
 
@@ -111,18 +105,15 @@
         hello(place.at(x=1 - place.x, y=1 - place.y))
         hello(place.at(core=1 - place.core))
         total += place.depth + 3
-    if parts > 1 and tree:
-
-        @pl.when(place.part > 0)
-        def _():
-            hello(place.member(place.slot, place.part - 1))
-
-        @pl.when(place.part < parts - 1)
-        def _():
-            hello(place.member(place.slot, place.part + 1))
-
-        total += jnp.where(place.part > 0, 1, 0) + jnp.where(place.part < parts - 1, 1, 0)
-    pl.semaphore_wait(barrier, total)
+
+    def range_of(offset, carry):
+        part = lax.rem(place.part + offset, parts)
+        hello(place.member(place.slot, part))
+        hello(place.member(place.crossed(1), part))
+        return carry
+
+    lax.fori_loop(1, parts, range_of, 0)
+    pl.semaphore_wait(barrier, total + 2 * (parts - 1))
 
 
 def halves_of(columns):
@@ -226,7 +217,7 @@
 
 
 class TreeGather:
-    COUNT = 12
+    COUNT = 7
 
     def __init__(self, place, src, dst, sems, cols=None):
         self.place, self.src, self.dst, self.sems = place, src, dst, sems
@@ -267,14 +258,14 @@
             piece if bits else self.src.at[:, self.cols],
             piece,
             self.sems.at[1],
-            self.sems.at[11 + (bits | bit)],
+            self.sems.at[6 + (bits | bit)],
             place.at(z=place.flipped(bit)),
         ).start()
 
     def await_piece(self, bits):
         place = self.place
         piece = self.part(place.x, place.core, place.flipped(bits), place.y)
-        wait_received(place, piece, self.sems.at[11 + bits])
+        wait_received(place, piece, self.sems.at[6 + bits])
 
     def start_line(self):
         for bit in self.place.bits():
@@ -298,26 +289,28 @@
         place, half = self.place, self.halves[number]
         x, y = self.across(half, first)
         mine = self.region(half, first, place.core, place.x, place.y)
-        base = 0 if first else 2
         return remote(
             mine,
             mine,
-            self.sems.at[3 + base + number],
-            self.sems.at[8 + base + number],
+            self.sems.at[3],
+            self.sems.at[4 if first else 5],
             place.at(x=x, y=y),
         )
+
+    def all_received(self, first):
+        every, place = slice(None), self.place
+        xs = 0 if first else every
+        wait_received(place, self.part(xs, 0, every, 0), self.sems.at[4 if first else 5])
 
     def received(self, number, first):
         half = self.halves[number]
         x, y = self.across(half, first)
-        region = self.region(half, first, self.place.core, x, y)
-        wait_received(self.place, region, self.sems.at[(8 if first else 10) + number])
-        return region
+        return self.region(half, first, self.place.core, x, y)
 
     def hand(self, region):
         place = self.place
         remote(
-            region, region, self.sems.at[7], self.sems.at[2], place.at(core=1 - place.core)
+            region, region, self.sems.at[6], self.sems.at[2], place.at(core=1 - place.core)
         ).start()
 
     def start_first(self):
@@ -330,12 +323,14 @@
         self.hand(self.part(place.x, place.core, slice(None), place.y))
 
     def start_second(self):
+        self.all_received(True)
         for number in range(len(self.halves)):
             region = self.received(number, True)
             self.exchange(number, False).start()
             self.hand(region)
 
     def start_hands(self):
+        self.all_received(False)
         for number in range(len(self.halves)):
             self.hand(self.received(number, False))
 
@@ -345,12 +340,12 @@
         wait_received(self.place, region, self.sems.at[2])
 
     def drain(self):
-        for number in range(len(self.halves)):
-            self.exchange(number, True).wait_send()
-            self.exchange(number, False).wait_send()
+        every, depth = slice(None), self.place.depth
+        wait_sent(
+            self.place, self.part(every, every, pl.ds(0, 3 * depth // 4), 0), self.sems.at[3]
+        )
         wait_sent(self.place, self.lines(), self.sems.at[1])
-        every = slice(None)
-        wait_sent(self.place, self.part(every, 0, every, every), self.sems.at[7])
+        wait_sent(self.place, self.part(every, 0, every, every), self.sems.at[6])
 
 
 class Reduce:
@@ -459,8 +454,79 @@
         wait_sent(place, self.rz, self.sems.at[6])
 
 
+class Total:
+    COUNT = 8
+
+    def __init__(self, place, mine, rc, rn, rz, sums, sems):
+        self.place, self.mine, self.rc, self.rn, self.rz = place, mine, rc, rn, rz
+        self.sums, self.sems = sums, sems
+
+    @staticmethod
+    def scratch(depth, rows):
+        return [
+            VMEM((rows, LANES), F32),
+            VMEM((rows, LANES), F32),
+            VMEM((3, rows, LANES), F32),
+            VMEM((depth - 1, rows, LANES), F32),
+            VMEM((2, rows, LANES), F32),
+            pltpu.SemaphoreType.DMA((Total.COUNT,)),
+        ]
+
+    others = Reduce.others
+
+    def core(self):
+        return remote(
+            self.mine,
+            self.rc,
+            self.sems.at[0],
+            self.sems.at[1],
+            self.place.at(core=1 - self.place.core),
+        )
+
+    def start_core(self):
+        self.core().start()
+
+    def start_columns(self):
+        self.core().wait_recv()
+        self.sums[0] = self.mine[...] + self.rc[...]
+        for number, (x, y) in enumerate(self.others()):
+            remote(
+                self.sums.at[0],
+                self.rn.at[number],
+                self.sems.at[2],
+                self.sems.at[3],
+                self.place.at(x=x, y=y),
+            ).start()
+
+    def start_line(self):
+        place = self.place
+        wait_received(place, self.rn, self.sems.at[3])
+        self.sums[1] = self.sums[0] + self.rn[0] + self.rn[1] + self.rn[2]
+        for offset in range(1, place.depth):
+            remote(
+                self.sums.at[1],
+                self.rz.at[offset - 1],
+                self.sems.at[4],
+                self.sems.at[5],
+                place.at(z=place.deeper(offset)),
+            ).start()
+
+    def result(self):
+        place = self.place
+        wait_received(place, self.rz, self.sems.at[5])
+        total = self.sums[1]
+        for offset in range(1, place.depth):
+            total = total + self.rz[offset - 1]
+        return total
+
+    def drain(self):
+        self.core().wait_send()
+        wait_sent(self.place, self.rn, self.sems.at[2])
+        wait_sent(self.place, self.rz, self.sems.at[4])
+
+
 class TreeReduce:
-    COUNT = 12
+    COUNT = 6
 
     def __init__(self, place, part, out, rc, total, ra, rb, fa, fb, rz, sems, cols=None):
         self.place, self.part = place, part
@@ -494,7 +560,6 @@
     def exchange(self, number, second):
         place, every = self.place, slice(None)
         half = self.halves[number]
-        slot = (2 if second else 8) + number
         over_x = (half[2] == "yx") == second
         device = place.at(x=1 - place.x) if over_x else place.at(y=1 - place.y)
         if second:
@@ -506,8 +571,8 @@
         return remote(
             self.total.at[self.cut(half, *index)],
             landing,
-            self.sems.at[slot],
-            self.sems.at[slot + 2],
+            self.sems.at[2],
+            self.sems.at[3 if second else 4],
             device,
         )
 
@@ -529,8 +594,8 @@
 
     def start_first(self):
         place = self.place
+        wait_received(place, self.rc.at[0], self.sems.at[3])
         for number, half in enumerate(self.halves):
-            self.exchange(number, True).wait_recv()
             landed = self.second[number]
 
             def add(z, carry):
@@ -546,8 +611,8 @@
 
     def start_line(self):
         place = self.place
+        wait_received(place, self.rc.at[0, :, 0], self.sems.at[4])
         for number, half in enumerate(self.halves):
-            self.exchange(number, False).wait_recv()
             landed = self.first[number]
 
             def add(z, carry):
@@ -566,8 +631,8 @@
             remote(
                 self.total.at[place.x, place.flipped(bits), place.y],
                 self.rz.at[bits - 1],
-                self.sems.at[6],
-                self.sems.at[11 + bits],
+                self.sems.at[5],
+                self.sems.at[5 + bits],
                 place.at(z=place.flipped(bit)),
             ).start()
 
@@ -576,7 +641,7 @@
         bit = 1
         while 2 * bit < place.depth:
             for bits in self.offsets(bit):
-                wait_received(place, self.rz.at[bits - 1], self.sems.at[11 + bits])
+                wait_received(place, self.rz.at[bits - 1], self.sems.at[5 + bits])
                 here = (place.x, place.flipped(bits - bit), place.y)
                 self.total[here] = self.total[here] + self.rz[bits - 1]
             bit *= 2
@@ -585,16 +650,14 @@
     def finish(self):
         place = self.place
         last = place.depth // 2
-        wait_received(place, self.rz.at[last - 1], self.sems.at[11 + last])
+        wait_received(place, self.rz.at[last - 1], self.sems.at[5 + last])
         total = self.total[place.x, place.z, place.y].astype(F32)
         self.out[...] = total + self.rz[last - 1].astype(F32)
 
     def drain(self):
         self.core().wait_send()
-        for number in range(len(self.halves)):
-            self.exchange(number, True).wait_send()
-            self.exchange(number, False).wait_send()
-        wait_sent(self.place, self.rz, self.sems.at[6])
+        wait_sent(self.place, self.rc.at[:, pl.ds(0, 3 * self.place.depth // 4)], self.sems.at[2])
+        wait_sent(self.place, self.rz, self.sems.at[5])
 
 
 def iota(shape, dim):
@@ -630,18 +693,22 @@
     return jnp.sum(jnp.where(iota((rows, total), 0) == owner, spread, 0.0), axis=0, keepdims=True)
 
 
-def fold_bias(row, rows, name, per):
-    total = row.shape[1]
-    owner = jnp.right_shift(iota((rows, total), 1), shift_of(per)) * 8 + BIASES.index(name)
-    chosen = jnp.where(iota((rows, total), 0) == owner, row, 0.0)
-    put = iota((total, LANES), 1) == (iota((total, LANES), 0) & (per - 1))
-    return lax.dot_general(
-        chosen,
-        put.astype(F32),
-        (((1,), (0,)), ((), ())),
-        precision=lax.Precision.HIGHEST,
-        preferred_element_type=F32,
-    )
+def head_bias(gathered, name, per, head, first):
+    rows = gathered.shape[0]
+    column = iota((LANES, LANES), 1) - first
+    pick = (iota((LANES, LANES), 0) == (column & (per - 1))) & (column >= 0) & (column < HD)
+    spread = dot(gathered.astype(BF16), pick.astype(BF16))
+    column = head * HD + iota((rows, LANES), 1) - first
+    owner = jnp.right_shift(column, shift_of(per)) * 8 + BIASES.index(name)
+    return jnp.sum(jnp.where(iota((rows, LANES), 0) == owner, spread, 0.0), axis=0, keepdims=True)
+
+
+def own_values(total, base, per, flat):
+    at = flat * per
+    row = iota(total.shape, 0) == base + lax.div(at, LANES)
+    chosen = jnp.sum(jnp.where(row, total, 0.0), axis=0, keepdims=True)
+    shift = lax.rem(LANES - lax.rem(at, LANES), LANES)
+    return pltpu.roll(jnp.broadcast_to(chosen, (8, LANES)), shift, 1)[0:1]
 
 
 def layer_kernel(
@@ -673,8 +740,13 @@
     segs,
     tile,
     aux_ref,
-    qs,
-    ks,
+    xg,
+    ws,
+    wh,
+    pw,
+    rw,
+    wsum,
+    w_in,
     qt_ref,
     kv_ref,
     kvt,
@@ -701,14 +773,13 @@
     halo_out,
     halo_in,
     gp,
-    win_s,
-    r_win_s,
     partials,
 ):
     place = Place(blocks)
     depth, devices = place.depth, 4 * blocks
     gwin, gwo, gwup, gwdown, gaux = gathered
-    p_win, p_out, p_up, p_down, p_aux = partials
+    in_rows = win_ref.shape[0]
+    p_out, p_up, p_down = partials
     width, hidden = gwin.shape[-1] // 3, gwup.shape[-1]
     per, per_up = width // devices, hidden // devices
     span, pairs_of_chunks, reach = window + GROUP, GROUP // 2, window // 2
@@ -738,10 +809,8 @@
     def entry(ref, base=0):
         return lambda index: ref.at[base + index]
 
-    seg_sems, k_sems, q_sems, o_sems, d_sems, dq_sems, dkv_sems = exchange_sems
+    seg_sems, x_s, x_r, w_sems, o_sems, d_sems, dq_sems, dkv_sems, g_sems = exchange_sems
     seg_copy = exchange(lambda target: tile, entry(segs, window), seg_sems)
-    k_copy = exchange(entry(ks), entry(kv_ref, window), k_sems, True)
-    q_copy = exchange(entry(qs), entry(qt_ref), q_sems)
     o_copy = exchange(entry(ot_ref), entry(mixed_t), o_sems)
     d_copy = exchange(entry(dos), entry(doct_ref), d_sems, True)
     dq_copy = exchange(entry(dqt_ref), entry(dq_in), dq_sems)
@@ -770,12 +839,12 @@
 
     greet(place, parts, True)
 
+    head, sequence = lax.div(place.slot, 2), lax.rem(place.slot, 2)
+    group_x = place.part * 2 + sequence
     row = iota((16, LANES), 0)
     numbers = seg_ref[...].astype(F32)
     tile[...] = jnp.where(row == 0, numbers[0:1], numbers[1:2]).astype(BF16)
     segs[window + place.slot] = tile[...]
-    for source, target in columns_between(win_ref.shape[-1] // 3):
-        win_s[:, target : target + LANES] = win_ref[:, source : source + LANES]
     aux_ref[...] = jnp.zeros_like(aux_ref)
     for index, ref in enumerate(bias_refs):
         aux_ref[index : index + 1, 0 : ref.shape[-1]] = ref[...].astype(F32).reshape(1, ref.shape[-1])
@@ -785,42 +854,92 @@
         def _():
             kv_ref[pl.ds(0, window)] = jnp.zeros((window, LANES, LANES), BF16)
 
-    plan = (
-        (aux_ref, gaux, None),
-        (win_s, gwin, (0, width)),
-        (win_s, gwin, (width, width)),
-        (win_s, gwin, (2 * width, width)),
-    )
-    g_aux, g_even, g_odd, g_q = [
-        Gather(place, src, dst, sems, cols)
-        for (src, dst, cols), sems in zip(plan, gather_sems[:4])
-    ]
+    g_aux = Gather(place, aux_ref, gaux, gather_sems[0])
     plan = (
         (wo_ref, gwo, None),
         (wup_ref, gwup, (0, hidden // 2)),
         (wup_ref, gwup, (hidden // 2, hidden // 2)),
         (wdown_ref, gwdown, (0, width // 2)),
         (wdown_ref, gwdown, (width // 2, width // 2)),
+        (win_ref, gwin, None),
     )
     rest = [
         TreeGather(place, src, dst, sems, cols)
-        for (src, dst, cols), sems in zip(plan, gather_sems[4:])
+        for (src, dst, cols), sems in zip(plan, gather_sems[1:])
     ]
-    g_wo, g_up0, g_up1, g_down0, g_down1 = rest
-    g_even.start_line()
-    g_aux.start_line()
-    g_odd.start_line()
-    g_q.start_line()
-    loop(lambda offset: seg_copy(offset).start())
+    g_wo, g_up0, g_up1, g_down0, g_down1, g_win = rest
+
+    def x_send(code, bit, src=None):
+        chunk = xg.at[place.crossed(code)]
+        remote(
+            chunk if src is None else src,
+            chunk,
+            x_s.at[0],
+            x_r.at[code ^ bit],
+            place.member(place.crossed(bit)),
+        ).start()
+
+    def x_here(*codes):
+        for code in codes:
+            wait_received(place, xg.at[place.crossed(code)], x_r.at[code])
+
+    x_send(0, 1, x_ref.at[1 - sequence])
     g_wo.start_line()
     g_up0.start_line()
     g_up1.start_line()
-    g_even.start_columns()
-    g_aux.start_columns()
-    g_odd.start_columns()
-    g_q.start_columns()
     g_down0.start_line()
     g_down1.start_line()
+    xg[pl.ds(place.slot, 1)] = x_ref[pl.ds(sequence, 1)]
+    g_aux.start_line()
+
+    low_rows = iota((in_rows, LANES), 1) < HD
+    for pair in range(HEADS // 2):
+        q_at, k_at, v_at = [
+            win_ref[:, kind * width + pair * LANES : kind * width + (pair + 1) * LANES].astype(F32)
+            for kind in range(3)
+        ]
+        ws[2 * pair, :, 0:LANES] = jnp.where(low_rows, k_at, swap_halves(v_at)).astype(BF16)
+        ws[2 * pair, :, LANES:] = jnp.where(low_rows, q_at, 0.0).astype(BF16)
+        ws[2 * pair + 1, :, 0:LANES] = jnp.where(low_rows, swap_halves(k_at), v_at).astype(BF16)
+        ws[2 * pair + 1, :, LANES:] = jnp.where(low_rows, swap_halves(q_at), 0.0).astype(BF16)
+
+    def to_heads(src, dst, send, recv):
+        def step(offset):
+            other = lax.rem(head + offset, HEADS)
+            remote(src.at[other], dst, send, recv, place.member(2 * other + sequence)).start()
+
+        loop(step, 1, HEADS)
+
+    def to_head_group(src, dst, send, recv):
+        for offset in range(1, 2 * parts):
+            other = lax.rem(group_x + offset, 2 * parts)
+            part, other_sequence = lax.div(other, 2), lax.rem(other, 2)
+            device = place.member(2 * head + other_sequence, part)
+            remote(src(part, other_sequence), dst(offset), send, recv, device).start()
+
+    every = slice(None)
+    to_heads(ws, wh.at[place.part, head, sequence], w_sems.at[0], w_sems.at[1])
+    wh[place.part, head, sequence] = ws[head]
+    loop(lambda offset: seg_copy(offset).start())
+    g_wo.start_step()
+    g_up0.start_step()
+    g_up1.start_step()
+    for bit in (4, 2, 8):
+        x_send(0, bit, x_ref.at[sequence])
+    g_down0.start_step()
+    g_down1.start_step()
+    x_here(1)
+    for bit in (4, 2, 8):
+        x_send(1, bit)
+    g_wo.start_first()
+    g_up0.start_first()
+    g_up1.start_first()
+    wait_received(place, ws.at[pl.ds(0, HEADS - 1)], w_sems.at[1])
+    own_rows = wh.at[place.part, every, sequence]
+    to_head_group(lambda *at: own_rows, lambda offset: own_rows, w_sems.at[2], w_sems.at[3])
+    g_aux.start_columns()
+    g_wo.start_second()
+
     wait_received(place, segs.at[pl.ds(0, GROUP - 1)], seg_sems.at[1])
 
     def seg_halo(part):
@@ -838,75 +957,72 @@
         def _():
             seg_halo(place.part + 1).start()
 
-    g_even.start_hands()
-    g_wo.start_step()
-    g_up0.start_step()
-    g_up1.start_step()
-    g_aux.start_hands()
-    g_odd.start_hands()
-    g_aux.finish()
-    g_even.finish()
-
-    aux = gaux[...].reshape(devices * 8, LANES)
-    bias_q = spread_bias(aux, "query", per, width)
-    bias_v = spread_bias(aux, "value", per, width)
-    tokens = x_ref[...].reshape(2 * LANES, width)
-    low_lane = iota((LANES, LANES), 1) < HD
-    wide = 2 * LANES
-
-    def column(at):
-        return dot(tokens, gwin[:, :, :, :, :, pl.ds(at, wide)].reshape(width, wide))
-
-    def corners():
-        for s in range(2):
-            for u in range(2):
-                at = (slice(s * LANES, (s + 1) * LANES), slice(u * LANES, (u + 1) * LANES))
-                yield s, u, at
-
-    def project_pairs(odd):
-        k = column(column_of("k", odd, width)).astype(BF16).astype(F32)
-        v = column(column_of("v", odd, width))
-        for s, u, at in corners():
-            pair = odd + 2 * u
-            head = s * HEADS + 2 * pair
-            k_at = k[at]
-            v_at = (v[at] + bias_v[:, pair * LANES : (pair + 1) * LANES]).astype(BF16).astype(F32)
-            ks[head] = jnp.where(low_lane, k_at, pltpu.roll(v_at, HD, 1)).astype(BF16)
-            ks[head + 1] = jnp.where(low_lane, pltpu.roll(k_at, HD, 1), v_at).astype(BF16)
-
-        def start(offset):
-            head = lax.rem(place.other_slot(offset), HEADS)
-
-            @pl.when(lax.rem(lax.div(head, 2), 2) == odd)
-            def _():
-                k_copy(offset).start()
-
-        loop(start)
-
-    project_pairs(0)
-    g_q.start_hands()
-    g_wo.start_first()
-    g_up0.start_first()
-    g_up1.start_first()
-    g_down0.start_step()
-    g_down1.start_step()
-    g_odd.finish()
-    project_pairs(1)
-    kv_ref[window + place.slot] = ks[place.slot]
-    g_q.finish()
-    for t in range(width // wide):
-        q = column(column_of("q", 2 * t, width)) + bias_q[:, t * wide : (t + 1) * wide]
-        q = q.astype(BF16).astype(F32) * 0.125
-        for s, u, at in corners():
-            turned = q[at].T.astype(BF16)
-            head = s * HEADS + 4 * t + 2 * u
-            qs[head] = turned[:HD]
-            qs[head + 1] = turned[HD:]
-    loop(lambda offset: q_copy(offset).start())
-    qt_ref[place.slot] = qs[place.slot]
-    g_wo.start_second()
+    x_here(4)
+    x_send(4, 2)
+    x_send(4, 8)
+    g_down0.start_first()
+    g_down1.start_first()
     g_up0.start_second()
     g_up1.start_second()
+    g_aux.start_hands()
+    x_here(5)
+    x_send(5, 2)
+    x_send(5, 8)
+    x_here(2, 3)
+    x_send(2, 8)
+    x_send(3, 8)
+    g_aux.finish()
+    wait_received(place, rw, w_sems.at[3])
+
+    aux = gaux[...].reshape(devices * 8, LANES)
+    bias_q = head_bias(aux, "query", per, head, 0)
+    bias_v = head_bias(aux, "value", per, head, HD)
+
+    def kv_halo(number, part):
+        return remote(
+            kv_ref.at[GROUP + number],
+            kv_ref.at[number],
+            kv_hs.at[0],
+            kv_hr.at[number],
+            place.member(place.slot, part),
+        )
+
+    def project(code):
+        first = 2 * lax.div(place.crossed(code), 2)
+        rows = xg[pl.ds(first, 2)].reshape(2 * LANES, width)
+        made = dot(rows, wh[...].reshape(width, 2 * LANES))
+        kv = (made[:, :LANES] + bias_v).astype(BF16)
+        q = (made[:, LANES:] + bias_q).astype(BF16).astype(F32) * 0.125
+        for side in range(2):
+            chunk = first + side
+            at = slice(side * LANES, (side + 1) * LANES)
+            kv_ref[window + chunk] = kv[at]
+            kvt[window + chunk] = kv[at].T
+            qt_ref[chunk] = q[at].T[:HD].astype(BF16)
+            if parts > 1:
+
+                @pl.when((place.part < parts - 1) & (chunk >= GROUP - window))
+                def _():
+                    kv_halo(chunk - (GROUP - window), place.part + 1).start()
+
+    project(0)
+    project(2)
+    g_down0.start_second()
+    g_down1.start_second()
+    g_wo.start_hands()
+    project(4)
+    x_here(6, 7)
+    x_send(6, 8)
+    x_send(7, 8)
+    project(6)
+    g_up0.start_hands()
+    g_up1.start_hands()
+    x_here(8, 9)
+    project(8)
+    x_here(12, 13)
+    project(12)
+    g_down0.start_hands()
+    g_down1.start_hands()
 
     if parts > 1:
 
@@ -918,7 +1034,6 @@
         def _():
             seg_halo(place.part - 1).wait_recv()
 
-    sequence = lax.div(place.slot, HEADS)
     chosen = jnp.where(iota((span, 16, LANES), 1) == sequence, segs[...].astype(F32), 0.0)
     seen = jnp.sum(chosen, axis=1)
     outside = (iota((span, LANES), 0) < window) & (place.part == 0)
@@ -930,38 +1045,11 @@
         count = jnp.sum(count, axis=1, keepdims=True)
         start = start + jnp.where(own >= number, count, 0.0)
     starts_ref[...] = start.astype(jnp.int32)
-    g_down0.start_first()
-    g_down1.start_first()
-
-    def kv_halo(number, part):
-        return remote(
-            kv_ref.at[GROUP + number],
-            kv_ref.at[number],
-            kv_hs.at[number],
-            kv_hr.at[number],
-            place.member(place.slot, part),
-        )
-
-    def arrived(source):
-        kvt[window + source] = kv_ref[window + source].T
-        if parts > 1:
-
-            @pl.when((place.part < parts - 1) & (source >= GROUP - window))
-            def _():
-                kv_halo(source - (GROUP - window), place.part + 1).start()
-
-    arrived(place.slot)
-
-    def kv_wait(offset):
-        k_copy(offset, True).wait_recv()
-        arrived(place.other_slot(-offset))
-
-    loop(kv_wait, 1, GROUP // 2)
-    loop(kv_wait, GROUP // 2, GROUP)
-    all_here(qt_ref, q_sems)
-    g_wo.start_hands()
-    g_up0.start_hands()
-    g_up1.start_hands()
+
+    x_here(10, 11)
+    project(10)
+    x_here(14, 15)
+    project(14)
 
     many = window + 2
     older = window * LANES
@@ -982,17 +1070,17 @@
     blank = jnp.zeros((HD, BLOCK), BF16)
 
     def attend(step, carry):
-        @pl.when(step == 1)
-        def _():
-            g_down0.start_second()
-
-        @pl.when(step == 3)
-        def _():
-            g_down1.start_second()
-
-        @pl.when(step == 6)
-        def _():
-            g_down0.start_hands()
+        @pl.when(step == 0)
+        def _():
+            g_win.start_line()
+
+        @pl.when(step == 4)
+        def _():
+            g_win.start_step()
+
+        @pl.when(step == 7)
+        def _():
+            g_win.start_first()
 
         if parts > 1:
 
@@ -1051,15 +1139,16 @@
     bias_down = spread_bias(aux, "down", per, width)
     bias_up = spread_bias(aux, "up", per_up, hidden)
     rows = 2 * LANES
-    wide_tokens = tokens.astype(F32)
+    wide_tokens = x_ref[...].reshape(rows, width).astype(F32)
     grads = grad_ref[...].reshape(rows, width).astype(F32)
     grad_ffn = (a1 * grads).astype(BF16)
-    g_down1.start_hands()
+    g_win.start_second()
     g_wo.finish()
     full_out = gwo[...].reshape(width, width)
 
     all_here(mixed_t, o_sems)
-    mixed_turned = mixed_t[...].reshape(2, width, LANES)
+    mixed_all = mixed_t[...].reshape(HEADS, 2, HD, LANES)
+    mixed_turned = [mixed_all[:, s].reshape(width, LANES) for s in range(2)]
     mixed = jnp.concatenate([mixed_turned[0].T, mixed_turned[1].T], axis=0)
     branch = dot(mixed, full_out) + bias_out
     attn_term = a0 * branch
@@ -1080,6 +1169,25 @@
         act_s[:, cols] = (pre * phi).astype(BF16)
         slope = phi + pre * jnp.exp(-0.5 * pre * pre) * (1.0 / math.sqrt(2.0 * math.pi))
         slope_s[:, cols] = slope
+    sources = [
+        (TreeReduce, p_out, r_out, None),
+        (TreeReduce, p_up, r_up, (0, hidden // 2)),
+        (TreeReduce, p_up, r_up, (hidden // 2, hidden // 2)),
+        (TreeReduce, p_down, r_down, (0, width // 2)),
+        (TreeReduce, p_down, r_down, (width // 2, width // 2)),
+    ]
+    t_out, t_up0, t_up1, t_down0, t_down1 = [
+        kind(place, part, out, *scratch, cols)
+        for (kind, part, out, cols), scratch in zip(sources, trees)
+    ]
+    t_aux = Total(place, *trees[-1])
+    flat_down, flat_up = p_down.reshape(hidden, width), p_up.reshape(width, hidden)
+    for half, tree in enumerate((t_down0, t_down1)):
+        at = slice(half * width // 2, (half + 1) * width // 2)
+        for t in range(hidden // tile_up):
+            cols = pl.ds(t * tile_up, tile_up)
+            flat_down[cols, at] = dot_tn(act_s[:, cols], grad_ffn[:, at]).astype(BF16)
+        tree.start_core()
     g_down0.finish()
     g_down1.finish()
     for t in range(hidden // tile_up):
@@ -1088,55 +1196,35 @@
         gpre = (dot_nt(grad_ffn, w_down) * slope_s[:, cols]).astype(BF16)
         gpre_s[:, cols] = gpre
         grad_res = grad_res + dot_nt(gpre, whole_up[:, cols])
+    hidden_turned = hidden_in.T
+
+    def up_part(half, tree):
+        for t in range(hidden // tile_up // 2):
+            cols = pl.ds(half * hidden // 2 + t * tile_up, tile_up)
+            flat_up[:, cols] = dot(hidden_turned, gpre_s[:, cols]).astype(BF16)
+        tree.start_core()
+
+    up_part(0, t_up0)
+    t_down0.start_second()
+    g_win.start_hands()
+    up_part(1, t_up1)
+    t_down1.start_second()
     gres_ref[...] = grad_res
     grad_branch = (a0 * grad_res).astype(BF16)
     grad_mixed = dot_nt(grad_branch, full_out).astype(BF16).astype(F32)
     for s in range(2):
         turned = grad_mixed[s * LANES : (s + 1) * LANES].T.astype(BF16)
-        dos[pl.ds(s * HEADS, HEADS)] = turned.reshape(HEADS, HD, LANES)
+        for number in range(HEADS):
+            dos[2 * number + s] = turned[number * HD : (number + 1) * HD]
     loop(lambda offset: d_copy(offset).start())
     doct_ref[place.slot] = dos[place.slot]
-
-    sources = [
-        (TreeReduce, p_out, r_out, None),
-        (TreeReduce, p_up, r_up, (0, hidden // 2)),
-        (TreeReduce, p_up, r_up, (hidden // 2, hidden // 2)),
-        (TreeReduce, p_down, r_down, (0, width // 2)),
-        (TreeReduce, p_down, r_down, (width // 2, width // 2)),
-        (Reduce, p_win, r_win_s, (0, width)),
-        (Reduce, p_win, r_win_s, (width, width)),
-        (Reduce, p_win, r_win_s, (2 * width, width)),
-        (Reduce, p_aux, r_aux, None),
-    ]
-    t_out, t_up0, t_up1, t_down0, t_down1, t_even, t_odd, t_q, t_aux = [
-        kind(place, part, out, *scratch, cols)
-        for (kind, part, out, cols), scratch in zip(sources, trees)
-    ]
-    lead = (2, 2, depth, 2)
-    flat_down, flat_up = p_down.reshape(hidden, width), p_up.reshape(width, hidden)
-    for half, tree in enumerate((t_down0, t_down1)):
-        at = slice(half * width // 2, (half + 1) * width // 2)
-        for t in range(hidden // tile_up):
-            cols = pl.ds(t * tile_up, tile_up)
-            flat_down[cols, at] = dot_tn(act_s[:, cols], grad_ffn[:, at]).astype(BF16)
-        tree.start_core()
-    hidden_turned = hidden_in.T
-
-    def up_part(half, tree):
-        for t in range(hidden // tile_up // 2):
-            cols = pl.ds(half * hidden // 2 + t * tile_up, tile_up)
-            flat_up[:, cols] = dot(hidden_turned, gpre_s[:, cols]).astype(BF16)
-        tree.start_core()
-
-    up_part(0, t_up0)
-    t_down0.start_second()
-    up_part(1, t_up1)
-    t_down1.start_second()
+    t_up0.start_second()
+
     p_out.reshape(width, width)[...] = dot(
         jnp.concatenate([mixed_turned[0], mixed_turned[1]], axis=1), grad_branch
     ).astype(BF16)
     t_out.start_core()
-    t_up0.start_second()
+    t_up1.start_second()
 
     for t in range(hidden // tile_up):
         cols = pl.ds(t * tile_up, tile_up)
@@ -1155,22 +1243,29 @@
         whole(grad_res * branch),
         whole(grads * ffn),
     )
-    lane = iota((devices * 8, LANES), 1)
-    scalars = jnp.zeros((devices * 8, LANES), F32)
+    lane = iota((1, LANES), 1)
+    scalars = jnp.zeros((1, LANES), F32)
     for number, value in enumerate(sums):
         scalars = scalars + jnp.where(lane == number, value, 0.0)
     up_row = jnp.sum(gpre_s[...].astype(F32), axis=0, keepdims=True)
     down_row = jnp.sum(grad_ffn.astype(F32), axis=0, keepdims=True)
     out_row = jnp.sum(grad_branch.astype(F32), axis=0, keepdims=True)
-    folded = (
-        fold_bias(out_row, devices * 8, "output", per)
-        + fold_bias(down_row, devices * 8, "down", per)
-        + fold_bias(up_row, devices * 8, "up", per_up)
-        + jnp.where((iota((devices * 8, LANES), 0) & 7) == SCALARS, scalars, 0.0)
-    )
-    p_aux[...] = folded.reshape(*lead, 8, LANES)
-
-    t_up1.start_second()
+    wide_rows = width // LANES
+    bases = {name: number * wide_rows for number, name in enumerate(BIASES)}
+    last_row = (len(BIASES) - 1) * wide_rows + hidden // LANES
+
+    def keep(base, row):
+        for number in range(row.shape[1] // LANES):
+            here = slice(number * LANES, (number + 1) * LANES)
+            t_aux.mine[base + number : base + number + 1] = row[:, here]
+
+    t_aux.mine[...] = jnp.zeros_like(t_aux.mine)
+    keep(bases["output"], out_row)
+    keep(bases["down"], down_row)
+    keep(bases["up"], up_row)
+    keep(last_row, scalars)
+
+    t_out.start_second()
     early = (t_down0, t_down1, t_up0, t_up1, t_out)
     low_block = iota((BLOCK, LANES), 1) < HD
 
@@ -1184,7 +1279,7 @@
         return remote(
             halo_out.at[pair],
             halo_in.at[pair],
-            back_hs.at[u],
+            back_hs.at[0],
             back_hr.at[u],
             place.member(place.slot, part),
         )
@@ -1240,17 +1335,25 @@
             send_to(dq_copy, 2 * pair + side)
 
     def attend_back(u, carry):
-        @pl.when(u == 0)
-        def _():
-            t_out.start_second()
+        @pl.when(u == 1)
+        def _():
+            t_down0.start_first()
+
+        @pl.when(u == 3)
+        def _():
+            t_down1.start_first()
 
         @pl.when(u == 5)
         def _():
-            t_down0.start_first()
+            t_up0.start_first()
 
         @pl.when(u == 7)
         def _():
-            t_down1.start_first()
+            t_up1.start_first()
+
+        @pl.when(u == 9)
+        def _():
+            t_out.start_first()
 
         @pl.when(u < pairs_of_chunks)
         def _():
@@ -1280,84 +1383,98 @@
 
     lax.fori_loop(0, reach + pairs_of_chunks, attend_back, 0)
     dq_in[place.slot] = dqt_ref[place.slot]
-    t_up0.start_first()
-    t_up1.start_first()
-    t_out.start_first()
-    dkv_in[place.slot] = dkv_sum[place.slot]
     t_down0.start_line()
     t_down1.start_line()
-
-    def weight_part(number):
-        part = dot(tokens_turned, gp[:, number * width : (number + 1) * width]).astype(BF16)
-        p_win[:, :, :, :, :, number * width : (number + 1) * width] = part.reshape(
-            *lead, width // devices, width
-        )
-
-    def token_part(number):
-        cols = slice(number * width, (number + 1) * width)
-        return dot_nt(gp[:, cols], full_in[:, cols])
-
-    tokens_turned = tokens.T
-    full_in = gwin.reshape(width, 3 * width)
+    t_up0.start_line()
+    t_up1.start_line()
+    dkv_in[place.slot] = dkv_sum[place.slot]
+
+    dq_all = jnp.concatenate([dqt_ref[i] for i in range(GROUP)], axis=1)
+    dkv_all = dkv_sum[...].reshape(GROUP * LANES, LANES)
+    twice = jnp.concatenate([dq_all, dq_all], axis=0)
+    query_row = dot_nt(jnp.ones((8, GROUP * LANES), BF16), twice)[0:1]
+    value_row = jnp.sum(dkv_all.astype(F32), axis=0, keepdims=True)
+    value_row = jnp.where(lane < HD, swap_halves(value_row), value_row)
+    mine = (iota((wide_rows, LANES), 0) == lax.div(head, 2)) & (
+        lax.div(iota((wide_rows, LANES), 1), HD) == lax.rem(head, 2)
+    )
+    for name, sums_row in (("query", query_row), ("value", value_row)):
+        t_aux.mine[bases[name] : bases[name] + wide_rows] = jnp.where(mine, sums_row, 0.0)
+    t_aux.start_core()
+    x_rows = xg[...].reshape(GROUP * LANES, width)
+    turned = jnp.concatenate(
+        [dot_tn(dkv_all, x_rows), dot(dq_all, x_rows), jnp.zeros((HD, width), F32)], axis=0
+    )
+    pw[...] = turned.T.astype(BF16).reshape(pw.shape)
+    to_head_group(
+        lambda *at: pw.at[at[0], every, at[1]],
+        lambda offset: rw.at[offset - 1],
+        g_sems.at[0],
+        g_sems.at[1],
+    )
+    t_aux.start_columns()
+    t_out.start_line()
+    t_down0.start_step()
+    wait_received(place, rw, g_sems.at[1])
+    total = pw[place.part, every, sequence].astype(F32)
+    for number in range(2 * parts - 1):
+        total = total + rw[number].astype(F32)
+    wsum[...] = total
+    to_heads(wsum, w_in.at[head], g_sems.at[2], g_sems.at[3])
+    w_in[head] = wsum[head]
+    t_aux.start_line()
+    t_down1.start_step()
+    t_up0.start_step()
+
     all_here(dq_in, dq_sems)
     for s in range(2):
-        turned = dq_in[pl.ds(s * HEADS, HEADS)].reshape(width, LANES).astype(F32)
-        gp[s * LANES : (s + 1) * LANES, 2 * width :] = turned.T.astype(BF16)
-    weight_part(2)
-    t_q.start_core()
-    query_row = jnp.sum(gp[:, 2 * width :].astype(F32), axis=0, keepdims=True)
-    gx = gres_ref[...] + token_part(2)
-    t_up0.start_line()
-    t_up1.start_line()
-    t_out.start_line()
-    t_q.start_columns()
-
-    all_here(dkv_in, dkv_sems)
-    for number in range(2):
-        for s in range(2):
-            at_rows = slice(s * LANES, (s + 1) * LANES)
-            for pair in range(number, HEADS // 2, 2):
-                even = dkv_in[s * HEADS + 2 * pair].astype(F32)
-                odd = dkv_in[s * HEADS + 2 * pair + 1].astype(F32)
-                keys = jnp.where(low_lane, even, pltpu.roll(odd, HD, 1))
-                values = jnp.where(low_lane, pltpu.roll(even, HD, 1), odd)
-                at = column_of("k", pair, width)
-                gp[at_rows, at : at + LANES] = keys.astype(BF16)
-                at = column_of("v", pair, width)
-                gp[at_rows, at : at + LANES] = values.astype(BF16)
-        weight_part(number)
-        (t_even, t_odd)[number].start_core()
-    value_rows = []
-    for pair in range(HEADS // 2):
-        at = column_of("v", pair, width)
-        value_rows.append(jnp.sum(gp[:, at : at + LANES].astype(F32), axis=0, keepdims=True))
-    folded = fold_bias(query_row, devices * 8, "query", per) + fold_bias(
-        jnp.concatenate(value_rows, axis=1), devices * 8, "value", per
-    )
-    p_aux[...] += folded.reshape(*lead, 8, LANES)
-    t_aux.start_core()
-    t_even.start_columns()
-    t_q.start_line()
-    t_odd.start_columns()
-    t_aux.start_columns()
-    t_down0.start_step()
-    t_down1.start_step()
-    t_up0.start_step()
+        turned = jnp.concatenate([dq_in[2 * number + s] for number in range(HEADS)], axis=0)
+        gp[s * LANES : (s + 1) * LANES, 0:width] = turned.astype(F32).T.astype(BF16)
+    g_win.finish()
+    full_in = gwin.reshape(width, 3 * width)
+    gx = gres_ref[...] + dot_nt(gp[:, 0:width], full_in[:, 0:width])
     t_up1.start_step()
     t_out.start_step()
-    gx = gx + token_part(0) + token_part(1)
+    all_here(dkv_in, dkv_sems)
+    low_lane = iota((LANES, LANES), 1) < HD
+    for s in range(2):
+        at_rows = slice(s * LANES, (s + 1) * LANES)
+        for pair in range(HEADS // 2):
+            even = dkv_in[4 * pair + s].astype(F32)
+            odd = dkv_in[4 * pair + 2 + s].astype(F32)
+            keys = jnp.where(low_lane, even, swap_halves(odd))
+            values = jnp.where(low_lane, swap_halves(even), odd)
+            at = width + pair * LANES
+            gp[at_rows, at : at + LANES] = keys.astype(BF16)
+            gp[at_rows, width + at : width + at + LANES] = values.astype(BF16)
+    gx = gx + dot_nt(gp[:, width:], full_in[:, width:])
     gx_ref[...] = gx.astype(BF16).reshape(2, LANES, width)
-    t_even.start_line()
-    t_aux.start_line()
-    t_odd.start_line()
-    for tree in early + (t_q, t_even, t_aux, t_odd):
+    wait_received(place, w_in.at[pl.ds(0, HEADS - 1)], g_sems.at[3])
+    for pair in range(HEADS // 2):
+        even, odd = w_in[2 * pair], w_in[2 * pair + 1]
+        even_kv, odd_kv = even[:, :LANES], odd[:, :LANES]
+        parts_of = (
+            jnp.where(low_rows, even[:, LANES:], swap_halves(odd[:, LANES:])),
+            jnp.where(low_rows, even_kv, swap_halves(odd_kv)),
+            jnp.where(low_rows, swap_halves(even_kv), odd_kv),
+        )
+        for kind, value in enumerate(parts_of):
+            at = kind * width + pair * LANES
+            r_win[:, at : at + LANES] = value
+    for tree in early:
         tree.finish()
-    for source, target in columns_between(width):
-        r_win[:, source : source + LANES] = r_win_s[:, target : target + LANES]
-
+    totals = t_aux.result()
+    flat = place.part * GROUP + place.slot
+    for number, name in enumerate(BIASES):
+        own = own_values(totals, bases[name], per_up if name == "up" else per, flat)
+        r_aux[number : number + 1] = own
+    r_aux[SCALARS : SCALARS + 1] = totals[last_row : last_row + 1]
     all_sent(segs, seg_sems)
-    all_sent(ks, k_sems)
-    all_sent(qs, q_sems)
+    wait_sent(place, xg.at[pl.ds(0, GROUP - 1)], x_s.at[0])
+    wait_sent(place, ws.at[pl.ds(0, HEADS - 1)], w_sems.at[0])
+    wait_sent(place, rw, w_sems.at[2])
+    wait_sent(place, rw, g_sems.at[0])
+    wait_sent(place, w_in.at[pl.ds(0, HEADS - 1)], g_sems.at[2])
     all_sent(ot_ref, o_sems)
     all_sent(dos, d_sems)
     all_sent(dqt_ref, dq_sems)
@@ -1366,16 +1483,20 @@
 
         @pl.when(place.part < parts - 1)
         def _():
-            loop(lambda number: kv_halo(number, place.part + 1).wait_send(), 0, window)
+            wait_sent(place, kv_ref.at[pl.ds(0, window)], kv_hs.at[0])
 
         @pl.when(place.part > 0)
         def _():
-            loop(lambda u: back_halo(u, place.part - 1).wait_send(), 0, reach)
-
-    for gather in (g_aux, g_even, g_odd, g_q, *rest):
+            wait_sent(place, halo_out, back_hs.at[0])
+
+    for gather in (g_aux, *rest):
         gather.drain()
-    for tree in early + (t_q, t_even, t_odd, t_aux):
+    for tree in early + (t_aux,):
         tree.drain()
+
+
+def swap_halves(values):
+    return jnp.concatenate([values[:, HD:], values[:, :HD]], axis=1)
 
 
 def two(ref, index):
@@ -1445,6 +1566,7 @@
     in_rows, up_rows = input_weight.shape[0], down_weight.shape[0]
     tree_parts = ((in_rows, width),) + ((in_rows, hidden // 2),) * 2 + ((up_rows, width // 2),) * 2
     tokens = seqs * rows
+    total_rows = -(-((len(BIASES) - 1) * width + hidden + LANES) // (8 * LANES)) * 8
     results = (
         shape(seqs, rows, width),
         shape(seqs, rows, width),
@@ -1466,17 +1588,21 @@
                 VMEM((*lead, up_rows, width), BF16),
                 VMEM((*lead, 8, LANES), F32),
             ],
-            [dma((Gather.COUNT,))] * 4 + [dma((TreeGather.COUNT + depth - 1,))] * 5,
+            [dma((Gather.COUNT,))] + [dma((TreeGather.COUNT + depth - 1,))] * 6,
             [TreeReduce.scratch(depth, *sizes, BF16) for sizes in tree_parts]
-            + [Reduce.scratch(depth, in_rows, width, BF16)] * 3
-            + [Reduce.scratch(depth, 8, LANES, F32)],
-            [dma((2,)), dma((GROUP,)), dma((2,)), dma((2,)), dma((GROUP,)), dma((2,)), dma((2,))],
-            [dma((1,)), dma((1,)), dma((window,)), dma((window,)), dma((window // 2,)), dma((window // 2,))],
+            + [Total.scratch(depth, total_rows)],
+            [dma((n,)) for n in (2, 1, GROUP, 4, 2, GROUP, 2, 2, 4)],
+            [dma((1,)), dma((1,)), dma((1,)), dma((window,)), dma((1,)), dma((window // 2,))],
             VMEM((span, 16, LANES), BF16),
             VMEM((16, LANES), BF16),
             VMEM((8, LANES), F32),
-            VMEM((GROUP, HD, LANES), BF16),
-            VMEM((GROUP, LANES, LANES), BF16),
+            VMEM((GROUP, LANES, width), BF16),
+            VMEM((HEADS, in_rows, 2 * LANES), BF16),
+            VMEM((parts, HEADS, 2, in_rows, 2 * LANES), BF16),
+            VMEM((parts, HEADS, 2, in_rows, 2 * LANES), BF16),
+            VMEM((2 * parts - 1, HEADS, in_rows, 2 * LANES), BF16),
+            VMEM((HEADS, in_rows, 2 * LANES), F32),
+            VMEM((HEADS, in_rows, 2 * LANES), F32),
             VMEM((GROUP, HD, LANES), BF16),
             VMEM((span, LANES, LANES), BF16),
             VMEM((span, LANES, LANES), BF16),
@@ -1503,14 +1629,10 @@
             VMEM((window, LANES, LANES), BF16),
             VMEM((window, LANES, LANES), BF16),
             VMEM((tokens, 3 * width), BF16),
-            VMEM((in_rows, 3 * width), BF16),
-            VMEM((in_rows, 3 * width), F32),
             [
-                VMEM((*lead, in_rows, 3 * width), BF16),
                 VMEM((*lead, in_rows, width), BF16),
                 VMEM((*lead, in_rows, hidden), BF16),
                 VMEM((*lead, up_rows, width), BF16),
-                VMEM((*lead, 8, LANES), F32),
             ],
         ],
         collective=0,

time: 118 us -> 114 us (0.966)
  Pallas kernels: 117 us -> 112 us
    pallas_call x1, Pallas kernels: 115 us -> 110 us  [local(): call(functools.partial(layer_kernel, blocks, parts, window, docs), result...]
where the time goes in v5:
time: 114 us; the launch traced here: 113 us
  Pallas kernels  112 us (98%)
    pallas_call x1, Pallas kernels, local(): call(functools.partial(layer_kernel, blocks, parts, window, docs), result...  110 us

profile of v5, /device:TPU:0, one launch (start us, length us, event | category | flops | bytes accessed | tf_op | source)
XLA Modules:
  0.0 113.2 jit_solution(8153660370343147547)
XLA Ops:
  0.6 110.3 %shard_map.228 = (bf16[2,128,512]{2,1,0:T(8,128)(2,1)}, bf16[2,128,512]{2,1,0:T(8,128)(2,1)}, f32[16,1536]{1,0:T(8,128)}, f32[16,512]{1,0:T(8,128)}, f32[16,2048...) custom-call(bf16[2,128,512]{2,1,0:T(8,128)(2,1)} %x_ref.1, s32[2,128]{1,0:T(2,128)} %seg_ref.1, ...), custom_call_target="tpu_custom_call" | custom-call | tf_op jit(solution)/shard_map/pallas_call | solution.py:1578
  110.9 2.1 %shard_map.229 = (bf16[2,128,512]{2,1,0:T(8,128)(2,1)}, bf16[2,128,512]{2,1,0:T(8,128)(2,1)}, f32[16,1536]{1,0:T(8,128)}, f32[16,512]{1,0:T(8,128)}, f32[16,2048...) custom-call(bf16[2,128,512]{2,1,0:T(8,128)(2,1)} %get-tuple-element., ...), custom_call_target="tpu_custom_call" | custom-call | tf_op jit(solution)/shard_map/pallas_call | solution.py:1651

commit v6 on v5

--- a/solution.py
+++ b/solution.py
@@ -13,7 +13,6 @@
 LANES = 128
 GROUP = 16
 BLOCK = 256
-VMEM_BYTES = 60 * 1024 * 1024
 F32 = jnp.float32
 BF16 = jnp.bfloat16
 VMEM = pltpu.VMEM
@@ -113,7 +112,7 @@
         return carry
 
     lax.fori_loop(1, parts, range_of, 0)
-    pl.semaphore_wait(barrier, total + 2 * (parts - 1))
+    return barrier, total + 2 * (parts - 1)
 
 
 def halves_of(columns):
@@ -716,15 +715,15 @@
     parts,
     window,
     docs,
-    x_ref,
-    seg_ref,
-    win_ref,
-    wo_ref,
-    wup_ref,
-    wdown_ref,
-    bias_refs,
+    x_hbm,
+    seg_hbm,
+    win_hbm,
+    wo_hbm,
+    wup_hbm,
+    wdown_hbm,
+    bias_hbm,
     alphas_ref,
-    grad_ref,
+    grad_hbm,
     out_ref,
     gx_ref,
     r_win,
@@ -774,9 +773,12 @@
     halo_in,
     gp,
     partials,
+    loaded,
+    load_sems,
 ):
     place = Place(blocks)
     depth, devices = place.depth, 4 * blocks
+    x_ref, seg_ref, win_ref, wo_ref, wup_ref, wdown_ref, grad_ref, *bias_refs = loaded
     gwin, gwo, gwup, gwdown, gaux = gathered
     in_rows = win_ref.shape[0]
     p_out, p_up, p_down = partials
@@ -837,7 +839,16 @@
         def _():
             copy(offset, True).wait_recv()
 
-    greet(place, parts, True)
+    sources = (x_hbm, seg_hbm, win_hbm, wo_hbm, wup_hbm, wdown_hbm, grad_hbm, *bias_hbm)
+    loads = [
+        pltpu.make_async_copy(src, dst, load_sems.at[number])
+        for number, (src, dst) in enumerate(zip(sources, loaded))
+    ]
+    for load in loads:
+        load.start()
+    barrier, expected = greet(place, parts, True)
+    for load in loads:
+        load.wait()
 
     head, sequence = lax.div(place.slot, 2), lax.rem(place.slot, 2)
     group_x = place.part * 2 + sequence
@@ -883,15 +894,6 @@
         for code in codes:
             wait_received(place, xg.at[place.crossed(code)], x_r.at[code])
 
-    x_send(0, 1, x_ref.at[1 - sequence])
-    g_wo.start_line()
-    g_up0.start_line()
-    g_up1.start_line()
-    g_down0.start_line()
-    g_down1.start_line()
-    xg[pl.ds(place.slot, 1)] = x_ref[pl.ds(sequence, 1)]
-    g_aux.start_line()
-
     low_rows = iota((in_rows, LANES), 1) < HD
     for pair in range(HEADS // 2):
         q_at, k_at, v_at = [
@@ -902,6 +904,17 @@
         ws[2 * pair, :, LANES:] = jnp.where(low_rows, q_at, 0.0).astype(BF16)
         ws[2 * pair + 1, :, 0:LANES] = jnp.where(low_rows, swap_halves(k_at), v_at).astype(BF16)
         ws[2 * pair + 1, :, LANES:] = jnp.where(low_rows, swap_halves(q_at), 0.0).astype(BF16)
+
+    xg[pl.ds(place.slot, 1)] = x_ref[pl.ds(sequence, 1)]
+    pl.semaphore_wait(barrier, expected)
+
+    x_send(0, 1, x_ref.at[1 - sequence])
+    g_wo.start_line()
+    g_up0.start_line()
+    g_up1.start_line()
+    g_down0.start_line()
+    g_down1.start_line()
+    g_aux.start_line()
 
     def to_heads(src, dst, send, recv):
         def step(offset):
@@ -1515,7 +1528,7 @@
     results[12][...] = jnp.sqrt(sums_ref[SCALARS, 0:3] * (1.0 / tokens_all))
 
 
-def call(kernel, out_shape, in_specs, out_specs, scratch, collective=None):
+def call(kernel, out_shape, in_specs, out_specs, scratch, megabytes, collective=None):
     return pl.pallas_call(
         kernel,
         out_shape=out_shape,
@@ -1525,7 +1538,7 @@
         compiler_params=pltpu.CompilerParams(
             collective_id=collective,
             has_side_effects=collective is not None,
-            vmem_limit_bytes=VMEM_BYTES,
+            vmem_limit_bytes=megabytes * 1024 * 1024,
         ),
     )
 
@@ -1561,6 +1574,7 @@
         return jax.ShapeDtypeStruct(dims, dtype)
 
     vmem, smem = pl.BlockSpec(memory_space=VMEM), pl.BlockSpec(memory_space=pltpu.SMEM)
+    hbm = pl.BlockSpec(memory_space=pltpu.HBM)
     dma = pltpu.SemaphoreType.DMA
     lead = (2, 2, depth, 2)
     in_rows, up_rows = input_weight.shape[0], down_weight.shape[0]
@@ -1578,7 +1592,7 @@
     carried = call(
         functools.partial(layer_kernel, blocks, parts, window, docs),
         results + (shape(8, LANES, dtype=F32),),
-        [vmem] * 6 + [(vmem,) * 5] + [smem, vmem],
+        [hbm] * 6 + [(hbm,) * 5] + [smem, hbm],
         (vmem,) * 7,
         [
             [
@@ -1634,7 +1648,26 @@
                 VMEM((*lead, in_rows, hidden), BF16),
                 VMEM((*lead, up_rows, width), BF16),
             ],
+            [
+                VMEM(array.shape, array.dtype)
+                for array in (
+                    layer_input,
+                    segments,
+                    input_weight,
+                    output_weight,
+                    up_weight,
+                    down_weight,
+                    out_grad,
+                    query_bias,
+                    value_bias,
+                    output_bias,
+                    down_bias,
+                    up_bias,
+                )
+            ],
+            dma((12,)),
         ],
+        megabytes=60 if in_rows >= 16 else 60,
         collective=0,
     )(
         layer_input,
@@ -1657,6 +1690,7 @@
         [vmem] * 7,
         (vmem,) * 13,
         [],
+        megabytes=60,
     )(*carried)
 
 

time: 114 us -> 114 us (level)
  no operation moved by 1% of the time
where the time goes in v6:
time: 114 us; the launch traced here: 113 us
  Pallas kernels  112 us (98%)
    pallas_call x1, Pallas kernels, local(): call(functools.partial(layer_kernel, blocks, parts, window, docs), result...  110 us

profile of v6, /device:TPU:0, one launch (start us, length us, event | category | flops | bytes accessed | tf_op | source)
XLA Modules:
  0.0 112.7 jit_solution(18225213949902560948)
XLA Ops:
  0.6 109.8 %shard_map.228 = (bf16[2,128,512]{2,1,0:T(8,128)(2,1)}, bf16[2,128,512]{2,1,0:T(8,128)(2,1)}, f32[16,1536]{1,0:T(8,128)}, f32[16,512]{1,0:T(8,128)}, f32[16,2048...) custom-call(bf16[2,128,512]{2,1,0:T(8,128)(2,1)} %x_hbm.1, s32[2,128]{1,0:T(2,128)} %seg_hbm.1, ...), custom_call_target="tpu_custom_call" | custom-call | tf_op jit(solution)/shard_map/pallas_call | solution.py:1592
  110.4 2.1 %shard_map.229 = (bf16[2,128,512]{2,1,0:T(8,128)(2,1)}, bf16[2,128,512]{2,1,0:T(8,128)(2,1)}, f32[16,1536]{1,0:T(8,128)}, f32[16,512]{1,0:T(8,128)}, f32[16,2048...) custom-call(bf16[2,128,512]{2,1,0:T(8,128)(2,1)} %get-tuple-element., ...), custom_call_target="tpu_custom_call" | custom-call | tf_op jit(solution)/shard_map/pallas_call | solution.py:1684
